TPU v7x, 32 devices: a whole 2x2x4 slice. The times are simulated.
32 devices in a mesh: space: 16 (over z, x, core), scen: 2 (over y).
Axes of the slice: x: 2, y: 2, z: 4, core: 2. Of those that a mesh axis runs over, the one named last changes fastest.
Arguments:
- dwell_map: bfloat16 [4096, 256], P('space', 'scen'), may hold values from 0 to 1
- target_map: bfloat16 [4096, 256], P('space'), may hold values from -6 to 6
- bound_mask: int32 [4096, 256], P('space', 'scen'), may hold values 0 or 1
- offsets: int32 [4, 2], replicated, may hold values from -32 to 32, as said below
- rate_index: int32 [4, 1], replicated, may hold values from 0 to 3
- rate_table: float32 [4], replicated, may hold values from 0.5 to 2
- row_kernels: bfloat16 [4, 63], replicated, may hold values from -0.75 to 0.75
- col_kernels: bfloat16 [4, 63], replicated, may hold values from -0.75 to 0.75
Outputs:
- dwell_next: bfloat16 [4096, 256], P('space', 'scen')
Inputs may be any that keep to these rules, and one draw needn't show every extreme that they name: `offsets`: each entry lies between -32 and 32; in each column some scenario has 32 and another -32. `rate_index`: every level is used by some scenario.
All inputs are finite; a program needn't handle non-finite values. No bound on the sum of `bound_mask` on one device may be relied on, other than what follows from the above.
Results may differ from a plain program's by a relative error of at most 0.014.
Values may be sent and summed in bfloat16 or wider, within the bound.
No kernel may reach another device: no remote copies, remote signals or barrier semaphores. Data moves between devices by JAX's collectives and lax.ppermute only.
A program may use at most 64 MiB of HBM per device.

v0:
```python
import jax
import jax.numpy as jnp
from jax import lax
from jax.sharding import PartitionSpec as P

S_DEV = 2
KTAPS = 63
REACH = 32


step_size = 1.0


def extended(x, sides, width):
    for axis, dim in sides:
        count, length = (lax.axis_size(axis), x.shape[dim])
        up = [(i, (i + 1) % count) for i in range(count - 1)]
        down = [(j, i) for i, j in up]
        last = lax.slice_in_dim(x, length - width, length, axis=dim)
        first = lax.slice_in_dim(x, 0, width, axis=dim)
        before = lax.ppermute(last, axis, up)
        after = lax.ppermute(first, axis, down)
        x = jnp.concatenate([before, x, after], axis=dim)
    return x


def band_line(kernel, start_at, row_count, col_count):
    kernel_line = jnp.zeros((col_count + 1,), kernel.dtype)
    kernel_line = lax.dynamic_update_slice(kernel_line, kernel, (start_at,))
    return jnp.tile(kernel_line, row_count)[: row_count * col_count].reshape(row_count, col_count)


def column_pass(values, kernels, shifts):
    scen_count, height, col_total = values.shape
    col_block = 128
    padded = jnp.pad(values, ((0, 0), (0, 0), (col_block, col_block)))

    def column_one_band(kernel, shift):
        return band_line(kernel, shift + col_block, col_block, 3 * col_block)

    matrices = jax.vmap(column_one_band)(kernels, shifts)
    product = jnp.zeros((scen_count, height, col_total // col_block, col_block), jnp.float32)
    for piece in range(3):
        view = padded[:, :, piece * col_block : piece * col_block + col_total].reshape(
            scen_count, height, col_total // col_block, col_block
        )
        part_mat = matrices[:, :, piece * col_block : (piece + 1) * col_block]
        product = product + jnp.einsum(
            "srny,scy->srnc", view, part_mat, preferred_element_type=jnp.float32
        )
    return product.reshape(scen_count, height, col_total)


def row_pass(values, kernels, shifts, out_rows):
    in_rows = values.shape[-2]
    rim_depth = (in_rows - out_rows) // 2
    row_block = 128
    block_count = -(-out_rows // row_block)
    window = row_block + 2 * rim_depth
    if values.ndim == 2:
        padded = values
    else:
        padded = values

    def row_one_band(kernel, shift):
        return band_line(kernel, shift + rim_depth, row_block, window)

    matrices = jax.vmap(row_one_band)(kernels, shifts)
    results = []
    for block_id in range(block_count):
        begin = block_id * row_block
        if values.ndim == 2:
            view = padded[begin : begin + window]
            results.append(
                jnp.einsum("sie,ew->siw", matrices, view, preferred_element_type=jnp.float32)
            )
        else:
            view = padded[:, begin : begin + window]
            results.append(
                jnp.einsum("sie,sew->siw", matrices, view, preferred_element_type=jnp.float32)
            )
    return jnp.concatenate(results, axis=1)


def shards(
    dwell_map, target_map, bound_mask, offsets, rate_index, rate_table, row_kernels, col_kernels
):
    tile_rows = dwell_map.shape[0]
    radius = (KTAPS - 1) // 2
    halo_rows = REACH + radius
    scen_count = S_DEV * lax.axis_size("scen")
    first_scen = lax.axis_index("scen") * S_DEV
    my_offsets = lax.dynamic_slice_in_dim(offsets, first_scen, S_DEV, 0)
    shift_rows = my_offsets[:, 0]
    shift_cols = my_offsets[:, 1]
    level_ids = lax.dynamic_slice_in_dim(rate_index, first_scen, S_DEV, 0)[:, 0]
    onehot = (
        level_ids[:, None] == jnp.arange(rate_table.shape[0], dtype=jnp.int32)[None, :]
    ).astype(jnp.float32)
    my_rates = jnp.sum(onehot * rate_table[None, :], axis=1)
    my_row_taps = jnp.sum(
        onehot[:, :, None] * row_kernels.astype(jnp.float32)[None], axis=1
    ).astype(jnp.bfloat16)
    my_col_taps = jnp.sum(
        onehot[:, :, None] * col_kernels.astype(jnp.float32)[None], axis=1
    ).astype(jnp.bfloat16)
    full_map = lax.all_gather(dwell_map, "scen", axis=1, tiled=True)
    rim_rows = extended(full_map, (("space", 0),), halo_rows)
    forward = row_pass(rim_rows, my_row_taps, -radius - shift_rows, tile_rows).astype(jnp.bfloat16)
    removal = my_rates[:, None, None] * column_pass(forward, my_col_taps, -radius - shift_cols)
    misfit = (removal - target_map.astype(jnp.float32)[None]).astype(jnp.bfloat16)
    misfit_rows = extended(misfit, (("space", 1),), halo_rows)
    back_cols = column_pass(misfit_rows, my_col_taps[:, ::-1], -radius + shift_cols).astype(
        jnp.bfloat16
    )
    adjoint = row_pass(back_cols, my_row_taps[:, ::-1], -radius + shift_rows, tile_rows)
    group_sum = jnp.sum((my_rates / scen_count)[:, None, None] * adjoint, axis=0)
    gradient = lax.psum_scatter(
        group_sum.astype(jnp.bfloat16), "scen", scatter_dimension=1, tiled=True
    ).astype(jnp.float32)
    stepped = dwell_map.astype(jnp.float32) - step_size * gradient
    return jnp.where(bound_mask == 1, jnp.maximum(stepped, 0.0), stepped).astype(jnp.bfloat16)


def solution(mesh):
    return jax.shard_map(
        shards,
        mesh=mesh,
        in_specs=(
            P("space", "scen"),
            P("space", None),
            P("space", "scen"),
            P(),
            P(),
            P(),
            P(),
            P(),
        ),
        out_specs=P("space", "scen"),
        check_vma=False,
    )
```

profile of v0, /device:TPU:0, one launch (start us, length us, event | category | flops | bytes accessed | tf_op | source)
XLA Modules:
  0.0 108.4 jit_solution(8607052065254966917)
XLA Ops:
  6.5 6.3 %all_gather.3 = bf16[256,256]{1,0:T(8,128)(2,1)S(1)} all-gather(bf16[256,128]{1,0:T(8,128)(2,1)} %param.8), channel_id=1, replica_groups=mesh['space'=16,'scen'=2] {'scen'}, dimensions={1}, use_global_device_ids=true | all-gather | bytes 196608 | tf_op jit(solution)/shard_map/all_gather | solution.py:107
  14.1 3.0 %collective-permute-start = (bf16[63,256]{1,0:T(8,128)(2,1)S(1)}, bf16[63,256]{1,0:T(8,128)(2,1)S(1)}, u32[]{:S(2)}, u32[]{:S(2)}) collective-permute-start(bf16[63,256]{1,0:T(8,128)(2,1)S(1)} %get-tuple-element.85), channel_id=1, source_target_pairs={{0,2},{2,4},{4,6},{6,8},{8,10},{10,12},{12,14},{14,16},{16,18},{18... | collective-permute-start | bytes 96776 | tf_op jit(solution)/shard_map/ppermute | solution.py:21
  20.4 12.7 %while.5 = (s32[]{:T(128)}, bf16[2,255]{1,0:T(2,128)(2,1)S(1)}, s32[2,2]{1,0:T(2,128)S(1)}, bf16[2,63]{1,0:T(2,128)(2,1)S(1)}, s32[]{:T(128)}, /*index=5*/s32[2]{0:T(128)S(1)}) while((s32[]{:T(128)}, bf16[2,255]{1,0:T(2,128)(2,1)S(1)}, s32[2,2]{1,0:T(2,128)S(1)}, bf16[2,63]{1,0:T(2,128)(2,1)S(1)}, s32[]{:T(128)}, /*index=5*/s32[2]{0:T(128)S(1)}) %tuple.88), condition=%wide.while_cond.1, body=%wide.while_body.1.sunk | while | flops 74 | bytes 769 | solution.py:29
  21.0 2.1 %and_reduce_fusion.9 = pred[]{:T(512)} fusion(s32[2]{0:T(128)S(1)} %get-tuple-element.250, s32[1]{0:T(128)} %bitcast.121, s32[1]{0:T(128)} %bitcast.122), kind=kLoop, calls=%fused_computation.3.clone.1 | loop fusion | flops 9 | bytes 17 | tf_op jit(solution)/shard_map/vmap(vmap())/scatter
  23.1 2.0 %broadcast_select_fusion.9 = bf16[1,63]{1,0:T(2,128)(2,1)S(1)} fusion(pred[]{:T(512)} %and_reduce_fusion.9, bf16[2,63]{1,0:T(2,128)(2,1)S(1)} %get-tuple-element.248, s32[]{:T(128)} %get-tuple-element.239, bf16[2,255]{1,0:T(2,128)(2,1)S(1)} %get-tuple-element.240, s32[]{:T(128)} %bitcast.123, s32[]{:T(128)} %bitcast.124), kind=kLoop, calls=%fused_computation.4.clone.1 | loop fusion | flops 63 | bytes 391 | tf_op jit(solution)/shard_map/vmap(vmap())/scatter
  27.4 2.1 %and_reduce_fusion.9 = pred[]{:T(512)} fusion(s32[2]{0:T(128)S(1)} %get-tuple-element.250, s32[1]{0:T(128)} %bitcast.121, s32[1]{0:T(128)} %bitcast.122), kind=kLoop, calls=%fused_computation.3.clone.1 | loop fusion | flops 9 | bytes 17 | tf_op jit(solution)/shard_map/vmap(vmap())/scatter
  29.5 2.0 %broadcast_select_fusion.9 = bf16[1,63]{1,0:T(2,128)(2,1)S(1)} fusion(pred[]{:T(512)} %and_reduce_fusion.9, bf16[2,63]{1,0:T(2,128)(2,1)S(1)} %get-tuple-element.248, s32[]{:T(128)} %get-tuple-element.239, bf16[2,255]{1,0:T(2,128)(2,1)S(1)} %get-tuple-element.240, s32[]{:T(128)} %bitcast.123, s32[]{:T(128)} %bitcast.124), kind=kLoop, calls=%fused_computation.4.clone.1 | loop fusion | flops 63 | bytes 391 | tf_op jit(solution)/shard_map/vmap(vmap())/scatter
  33.9 12.6 %while.6 = (s32[]{:T(128)}, bf16[2,385]{1,0:T(2,128)(2,1)S(1)}, s32[2,2]{1,0:T(2,128)S(1)}, bf16[2,63]{1,0:T(2,128)(2,1)S(1)}, s32[]{:T(128)}, /*index=5*/s32[2]{0:T(128)S(1)}) while((s32[]{:T(128)}, bf16[2,385]{1,0:T(2,128)(2,1)S(1)}, s32[2,2]{1,0:T(2,128)S(1)}, bf16[2,63]{1,0:T(2,128)(2,1)S(1)}, s32[]{:T(128)}, /*index=5*/s32[2]{0:T(128)S(1)}) %tuple.90), condition=%wide.while_cond.2, body=%wide.while_body.2.sunk | while | flops 74 | bytes 769 | solution.py:29
  34.5 2.0 %and_reduce_fusion.10 = pred[]{:T(512)} fusion(s32[2]{0:T(128)S(1)} %get-tuple-element.268, s32[1]{0:T(128)} %bitcast.125, s32[1]{0:T(128)} %bitcast.126), kind=kLoop, calls=%fused_computation.6.clone.1 | loop fusion | flops 9 | bytes 17 | tf_op jit(solution)/shard_map/vmap(vmap())/scatter
  36.5 2.0 %broadcast_select_fusion.10 = bf16[1,63]{1,0:T(2,128)(2,1)S(1)} fusion(pred[]{:T(512)} %and_reduce_fusion.10, bf16[2,63]{1,0:T(2,128)(2,1)S(1)} %get-tuple-element.266, s32[]{:T(128)} %get-tuple-element.257, bf16[2,385]{1,0:T(2,128)(2,1)S(1)} %get-tuple-element.258, s32[]{:T(128)} %bitcast.127, s32[]{:T(128)} %bitcast.128), kind=kLoop, calls=%fused_computation.7.clone.1 | loop fusion | flops 63 | bytes 391 | tf_op jit(solution)/shard_map/vmap(vmap())/scatter
  40.8 2.0 %and_reduce_fusion.10 = pred[]{:T(512)} fusion(s32[2]{0:T(128)S(1)} %get-tuple-element.268, s32[1]{0:T(128)} %bitcast.125, s32[1]{0:T(128)} %bitcast.126), kind=kLoop, calls=%fused_computation.6.clone.1 | loop fusion | flops 9 | bytes 17 | tf_op jit(solution)/shard_map/vmap(vmap())/scatter
  42.9 2.0 %broadcast_select_fusion.10 = bf16[1,63]{1,0:T(2,128)(2,1)S(1)} fusion(pred[]{:T(512)} %and_reduce_fusion.10, bf16[2,63]{1,0:T(2,128)(2,1)S(1)} %get-tuple-element.266, s32[]{:T(128)} %get-tuple-element.257, bf16[2,385]{1,0:T(2,128)(2,1)S(1)} %get-tuple-element.258, s32[]{:T(128)} %bitcast.127, s32[]{:T(128)} %bitcast.128), kind=kLoop, calls=%fused_computation.7.clone.1 | loop fusion | flops 63 | bytes 391 | tf_op jit(solution)/shard_map/vmap(vmap())/scatter
  46.5 12.3 %while.7 = (s32[]{:T(128)}, bf16[2,385]{1,0:T(2,128)(2,1)S(1)}, s32[2,2]{1,0:T(2,128)S(1)}, bf16[2,63]{1,0:T(2,128)(2,1)S(1)}, s32[]{:T(128)}, /*index=5*/s32[2]{0:T(128)S(1)}) while((s32[]{:T(128)}, bf16[2,385]{1,0:T(2,128)(2,1)S(1)}, s32[2,2]{1,0:T(2,128)S(1)}, bf16[2,63]{1,0:T(2,128)(2,1)S(1)}, s32[]{:T(128)}, /*index=5*/s32[2]{0:T(128)S(1)}) %tuple.91), condition=%wide.while_cond.3, body=%wide.while_body.3.sunk | while | flops 74 | bytes 769 | solution.py:29
  47.2 2.0 %and_reduce_fusion.11 = pred[]{:T(512)} fusion(s32[2]{0:T(128)S(1)} %get-tuple-element.286, s32[1]{0:T(128)} %bitcast.129, s32[1]{0:T(128)} %bitcast.130), kind=kLoop, calls=%fused_computation.9.clone.1 | loop fusion | flops 9 | bytes 17 | tf_op jit(solution)/shard_map/vmap(vmap())/scatter
  49.2 1.9 %broadcast_select_fusion.11 = bf16[1,63]{1,0:T(2,128)(2,1)S(1)} fusion(pred[]{:T(512)} %and_reduce_fusion.11, bf16[2,63]{1,0:T(2,128)(2,1)S(1)} %get-tuple-element.284, s32[]{:T(128)} %get-tuple-element.275, bf16[2,385]{1,0:T(2,128)(2,1)S(1)} %get-tuple-element.276, s32[]{:T(128)} %bitcast.131, s32[]{:T(128)} %bitcast.132), kind=kLoop, calls=%fused_computation.10.clone.1 | loop fusion | flops 63 | bytes 391 | tf_op jit(solution)/shard_map/vmap(vmap())/scatter
  53.4 2.0 %and_reduce_fusion.11 = pred[]{:T(512)} fusion(s32[2]{0:T(128)S(1)} %get-tuple-element.286, s32[1]{0:T(128)} %bitcast.129, s32[1]{0:T(128)} %bitcast.130), kind=kLoop, calls=%fused_computation.9.clone.1 | loop fusion | flops 9 | bytes 17 | tf_op jit(solution)/shard_map/vmap(vmap())/scatter
  55.4 1.9 %broadcast_select_fusion.11 = bf16[1,63]{1,0:T(2,128)(2,1)S(1)} fusion(pred[]{:T(512)} %and_reduce_fusion.11, bf16[2,63]{1,0:T(2,128)(2,1)S(1)} %get-tuple-element.284, s32[]{:T(128)} %get-tuple-element.275, bf16[2,385]{1,0:T(2,128)(2,1)S(1)} %get-tuple-element.276, s32[]{:T(128)} %bitcast.131, s32[]{:T(128)} %bitcast.132), kind=kLoop, calls=%fused_computation.10.clone.1 | loop fusion | flops 63 | bytes 391 | tf_op jit(solution)/shard_map/vmap(vmap())/scatter
  58.9 12.3 %while.4 = (s32[]{:T(128)}, bf16[2,255]{1,0:T(2,128)(2,1)S(1)}, s32[2,2]{1,0:T(2,128)S(1)}, bf16[2,63]{1,0:T(2,128)(2,1)S(1)}, s32[]{:T(128)}, /*index=5*/s32[2]{0:T(128)S(1)}) while((s32[]{:T(128)}, bf16[2,255]{1,0:T(2,128)(2,1)S(1)}, s32[2,2]{1,0:T(2,128)S(1)}, bf16[2,63]{1,0:T(2,128)(2,1)S(1)}, s32[]{:T(128)}, /*index=5*/s32[2]{0:T(128)S(1)}) %tuple.89), condition=%wide.while_cond, body=%wide.while_body.sunk | while | flops 74 | bytes 769 | solution.py:29
  59.5 2.0 %and_reduce_fusion.8 = pred[]{:T(512)} fusion(s32[2]{0:T(128)S(1)} %get-tuple-element.232, s32[1]{0:T(128)} %bitcast.117, s32[1]{0:T(128)} %bitcast.118), kind=kLoop, calls=%fused_computation.clone.1 | loop fusion | flops 9 | bytes 17 | tf_op jit(solution)/shard_map/vmap(vmap())/scatter
  61.5 2.0 %broadcast_select_fusion.8 = bf16[1,63]{1,0:T(2,128)(2,1)S(1)} fusion(pred[]{:T(512)} %and_reduce_fusion.8, bf16[2,63]{1,0:T(2,128)(2,1)S(1)} %get-tuple-element.230, s32[]{:T(128)} %get-tuple-element.221, bf16[2,255]{1,0:T(2,128)(2,1)S(1)} %get-tuple-element.222, s32[]{:T(128)} %bitcast.119, s32[]{:T(128)} %bitcast.120), kind=kLoop, calls=%fused_computation.1.clone.1 | loop fusion | flops 63 | bytes 391 | tf_op jit(solution)/shard_map/vmap(vmap())/scatter
  65.7 2.0 %and_reduce_fusion.8 = pred[]{:T(512)} fusion(s32[2]{0:T(128)S(1)} %get-tuple-element.232, s32[1]{0:T(128)} %bitcast.117, s32[1]{0:T(128)} %bitcast.118), kind=kLoop, calls=%fused_computation.clone.1 | loop fusion | flops 9 | bytes 17 | tf_op jit(solution)/shard_map/vmap(vmap())/scatter
  67.8 2.0 %broadcast_select_fusion.8 = bf16[1,63]{1,0:T(2,128)(2,1)S(1)} fusion(pred[]{:T(512)} %and_reduce_fusion.8, bf16[2,63]{1,0:T(2,128)(2,1)S(1)} %get-tuple-element.230, s32[]{:T(128)} %get-tuple-element.221, bf16[2,255]{1,0:T(2,128)(2,1)S(1)} %get-tuple-element.222, s32[]{:T(128)} %bitcast.119, s32[]{:T(128)} %bitcast.120), kind=kLoop, calls=%fused_computation.1.clone.1 | loop fusion | flops 63 | bytes 391 | tf_op jit(solution)/shard_map/vmap(vmap())/scatter
  75.9 3.5 %collective-permute-start.2 = (bf16[2,63,256]{1,2,0:T(8,128)(2,1)S(1)}, bf16[2,63,256]{1,2,0:T(8,128)(2,1)S(1)}, u32[]{:S(2)}, u32[]{:S(2)}) collective-permute-start(bf16[2,63,256]{1,2,0:T(8,128)(2,1)S(1)} %get-tuple-element.83), channel_id=1, source_target_pairs={{0,2},{2,4},{4,6},{6,8},{8,10},{10,12},{12,14},{14,16},{16,18},{18... | collective-permute-start | bytes 193544 | tf_op jit(solution)/shard_map/ppermute | solution.py:21
  85.1 14.7 %reduce-scatter.4.cloned.1.call-done = bf16[128,256]{1,0:T(8,128)(2,1)} async-done(((bf16[256,256]{1,0:T(8,128)(2,1)}), bf16[128,256]{1,0:T(8,128)(2,1)}) %reduce-scatter.4.cloned.1.call-update) | async-done | bytes 65552
  (112 shorter events, 34.6 us)
Async XLA Ops:
  6.5 10.6 %copy-start = (s32[4,2]{0,1:T(2,128)S(1)}, s32[4,2]{0,1:T(2,128)}, u32[]{:S(2)}) copy-start(s32[4,2]{0,1:T(2,128)} %param.11) | copy-start | bytes 100
  6.5 93.3 %reduce-scatter.4.cloned.1.call-start = ((), (), s32[]{:S(2)}) async-start(), calls=%async_computation.1 | async-start | bytes 196608
  12.8 61.5 %collective-permute-start.1 = (bf16[63,256]{1,0:T(8,128)(2,1)S(1)}, bf16[63,256]{1,0:T(8,128)(2,1)S(1)}, u32[]{:S(2)}, u32[]{:S(2)}) collective-permute-start(bf16[63,256]{1,0:T(8,128)(2,1)S(1)} %get-tuple-element.86), channel_id=1, source_target_pairs={{2,0},{4,2},{6,4},{8,6},{10,8},{12,10},{14,12},{16,14},{18,16},{20... | collective-permute-start | bytes 96776 | tf_op jit(solution)/shard_map/ppermute | solution.py:22
  14.1 60.5 %collective-permute-start = (bf16[63,256]{1,0:T(8,128)(2,1)S(1)}, bf16[63,256]{1,0:T(8,128)(2,1)S(1)}, u32[]{:S(2)}, u32[]{:S(2)}) collective-permute-start(bf16[63,256]{1,0:T(8,128)(2,1)S(1)} %get-tuple-element.85), channel_id=1, source_target_pairs={{0,2},{2,4},{4,6},{6,8},{8,10},{10,12},{12,14},{14,16},{16,18},{18... | collective-permute-start | bytes 96776 | tf_op jit(solution)/shard_map/ppermute | solution.py:21
  17.4 0.7 copy-start.8
  18.1 0.7 copy-start.6
  18.8 0.7 copy-start.7
  19.7 0.7 copy-start.4
  33.2 0.7 copy-start.5
  58.9 12.3 %copy-start.9 = (f32[4]{0:T(128)S(1)}, f32[4]{0:T(128)}, u32[]{:S(2)}) copy-start(f32[4]{0:T(128)} %param.13) | copy-start | bytes 52
  73.3 0.9 copy-start.2
  75.9 6.8 %collective-permute-start.2 = (bf16[2,63,256]{1,2,0:T(8,128)(2,1)S(1)}, bf16[2,63,256]{1,2,0:T(8,128)(2,1)S(1)}, u32[]{:S(2)}, u32[]{:S(2)}) collective-permute-start(bf16[2,63,256]{1,2,0:T(8,128)(2,1)S(1)} %get-tuple-element.83), channel_id=1, source_target_pairs={{0,2},{2,4},{4,6},{6,8},{8,10},{10,12},{12,14},{14,16},{16,18},{18... | collective-permute-start | bytes 193544 | tf_op jit(solution)/shard_map/ppermute | solution.py:21
  79.3 3.3 %collective-permute-start.3 = (bf16[2,63,256]{1,2,0:T(8,128)(2,1)S(1)}, bf16[2,63,256]{1,2,0:T(8,128)(2,1)S(1)}, u32[]{:S(2)}, u32[]{:S(2)}) collective-permute-start(bf16[2,63,256]{1,2,0:T(8,128)(2,1)S(1)} %get-tuple-element.84), channel_id=1, source_target_pairs={{2,0},{4,2},{6,4},{8,6},{10,8},{12,10},{14,12},{16,14},{18,16},{20... | collective-permute-start | bytes 193544 | tf_op jit(solution)/shard_map/ppermute | solution.py:22
  85.1 15.7 %copy-start.3 = (s32[256,128]{1,0:T(8,128)S(1)}, s32[256,128]{1,0:T(8,128)}, u32[]{:S(2)}) copy-start(s32[256,128]{1,0:T(8,128)} %param.10) | copy-start | bytes 393220
  99.9 1.0 copy-start.1
Sparse Core Ops, SparseCore 0:
  85.3 14.5 reduce-scatter.3
where the time goes:
time: 109 us; the launch traced here: 108 us
  other arithmetic  33.8 us (31%)
  local copies, waits for them, and re-layouts  28.1 us (26%)
  waiting for transfers between devices  14.7 us (13%)
  between operations  13.8 us (13%)
  starting transfers between devices  9.1 us (8%)
  blocking collectives  6.28 us (6%)
  matrix products  2.27 us (2%)
    scatter x16, other arithmetic  32.2 us
    scatter x24, local copies, waits for them, and re-layouts  17.6 us
    unnamed x2, waiting for transfers between devices  14.7 us
    ppermute x2, starting transfers between devices, extended(): before = lax.ppermute(last, axis, up)  6.51 us
    all_gather x1, blocking collectives, shards(): full_map = lax.all_gather(dwell_map, 'scen', axis=1, tiled=True)  6.28 us
    unnamed x28, local copies, waits for them, and re-layouts  6.04 us
    ppermute x2, starting transfers between devices, extended(): after = lax.ppermute(first, axis, down)  2.58 us
    another operation x8, local copies, waits for them, and re-layouts, band_line(): jnp.tile(kernel_line, row_count)[:row_count * col_count]  2.46 us
  transfers between devices with their start and end apart: 5, of which 1 were waited for; matrix products, arithmetic and copies ran while one was open for 51% of the time, Pallas kernels for 0%

commit v1 on v0

v1 whole, which is shorter than its diff:
```python
import functools

import jax
import jax.numpy as jnp
from jax import lax
from jax.experimental import pallas as pl
from jax.experimental.pallas import tpu as pltpu
from jax.sharding import PartitionSpec as P

KTAPS = 63
RADIUS = 31
BLOCK = 128
HALF = 64
STEP_SIZE = 1.0
BF16 = jnp.bfloat16
F32 = jnp.float32


def band(taps, start, width):
    line = jnp.concatenate([taps, jnp.zeros((1, width - KTAPS), F32)], axis=1)
    line = pltpu.roll(jnp.broadcast_to(line, (8, width)), start, 1)
    lines = jnp.broadcast_to(line[0:1], (BLOCK, width))
    return pltpu.roll(lines, 0, 1, stride=1, stride_axis=0).astype(BF16)


def bands_kernel(offsets, levels, row_taps, col_taps, fwd_ref, adj_ref, col_ref):
    scen_total, width = col_ref.shape[0], col_ref.shape[1]
    blocks = width // BLOCK
    turn = (
        lax.broadcasted_iota(jnp.int32, (KTAPS, KTAPS), 0)
        + lax.broadcasted_iota(jnp.int32, (KTAPS, KTAPS), 1)
        == KTAPS - 1
    )
    rows = row_taps[...].astype(F32)
    turned = jnp.dot(
        row_taps[...], turn.astype(F32).astype(BF16), preferred_element_type=F32
    )
    cols = col_taps[...].astype(F32)

    def pick(table, level):
        out = table[0:1]
        for r in range(1, table.shape[0]):
            out = jnp.where(level == r, table[r : r + 1], out)
        return out

    for s in range(scen_total):
        level = levels[s, 0]
        shift_row, shift_col = offsets[s, 0], offsets[s, 1]
        fwd_ref[s * BLOCK : (s + 1) * BLOCK, :] = band(
            pick(rows, level), HALF - RADIUS - shift_row, 2 * BLOCK
        )
        adj_ref[s] = band(pick(turned, level), HALF - RADIUS + shift_row, 2 * BLOCK)
        near = band(pick(cols, level), BLOCK - RADIUS - shift_col, 3 * BLOCK)
        for j in range(blocks):
            for y in range(blocks):
                piece = jnp.zeros((BLOCK, BLOCK), BF16)
                if abs(y - j) <= 1:
                    piece = near[:, (y - j + 1) * BLOCK : (y - j + 2) * BLOCK]
                col_ref[s, j * BLOCK : (j + 1) * BLOCK, y * BLOCK : (y + 1) * BLOCK] = piece


def step_kernel(blocks, place, levels, rates, fwd, adj, col, *refs):
    mids, aboves, belows = refs[:blocks], refs[blocks : 2 * blocks], refs[2 * blocks : 3 * blocks]
    target, bound, out, dwell_all, target_all, fwd_all, back_all = refs[3 * blocks :]
    scen_total = adj.shape[0]
    tile = out.shape[0]
    deep = tile + 2 * HALF
    own, first_row, last_row, first_col, last_col = [place[i] for i in range(5)]
    own_lanes = pl.ds(pl.multiple_of(own, BLOCK), BLOCK)
    if blocks == 2:
        spots = [own_lanes, pl.ds(pl.multiple_of(BLOCK - own, BLOCK), BLOCK)]
    else:
        spots = [own_lanes, pl.ds(0, BLOCK), pl.ds(2 * BLOCK, BLOCK)][:blocks]

    target_all[HALF : HALF + tile, :] = target[...]
    for b, lanes in enumerate(spots):
        dwell_all[0:BLOCK, lanes] = aboves[b][0:BLOCK, :]
        dwell_all[BLOCK : BLOCK + tile, lanes] = mids[b][...]
        dwell_all[BLOCK + tile :, lanes] = belows[b][0:BLOCK, :]
        target_all[0:HALF, lanes] = aboves[b][BLOCK:, :]
        target_all[HALF + tile :, lanes] = belows[b][BLOCK:, :]

    for r in range(deep // BLOCK):
        view = dwell_all[r * BLOCK : (r + 2) * BLOCK, :]
        lines = jnp.dot(fwd[...], view, preferred_element_type=F32).astype(BF16)
        for s in range(scen_total):
            fwd_all[s, r * BLOCK : (r + 1) * BLOCK, :] = lines[s * BLOCK : (s + 1) * BLOCK]

    goal = target_all[...].astype(F32)
    for s in range(scen_total):
        rate = rates[levels[s, 0]]
        removal = lax.dot_general(
            fwd_all[s], col[s], (((1,), (1,)), ((), ())), preferred_element_type=F32
        )
        above_rate = jnp.where(first_row == 1, 0.0, rate)
        below_rate = jnp.where(last_row == 1, 0.0, rate)
        removal = jnp.concatenate(
            [
                above_rate * removal[:HALF],
                rate * removal[HALF : deep - HALF],
                below_rate * removal[deep - HALF :],
            ],
            axis=0,
        )
        misfit = (removal - goal).astype(BF16)
        if blocks > 2:
            lane = lax.broadcasted_iota(jnp.int32, misfit.shape, 1)
            inside = (lane >= first_col * BLOCK) & (lane < (blocks - last_col) * BLOCK)
            misfit = jnp.where(inside, misfit, jnp.zeros_like(misfit))
        back = jnp.dot(misfit, col[s, :, own_lanes], preferred_element_type=F32)
        back_all[s] = ((rate / scen_total) * back).astype(BF16)

    for r in range(tile // BLOCK):
        here = slice(r * BLOCK, (r + 1) * BLOCK)
        gradient = jnp.zeros((BLOCK, BLOCK), F32)
        for s in range(scen_total):
            view = back_all[s, r * BLOCK : (r + 2) * BLOCK, :]
            gradient += jnp.dot(adj[s], view, preferred_element_type=F32)
        stepped = mids[0][here, :].astype(F32) - STEP_SIZE * gradient
        out[here, :] = jnp.where(
            bound[here, :] == 1, jnp.maximum(stepped, 0.0), stepped
        ).astype(BF16)


def shards(
    dwell_map, target_map, bound_mask, offsets, rate_index, rate_table, row_kernels, col_kernels
):
    tile = dwell_map.shape[0]
    n_space, n_scen = lax.axis_size("space"), lax.axis_size("scen")
    space, scen = lax.axis_index("space"), lax.axis_index("scen")
    scen_total = offsets.shape[0]
    blocks = min(n_scen, 3)
    width = blocks * BLOCK
    deep = tile + 2 * HALF

    smem = pl.BlockSpec(memory_space=pltpu.SMEM)
    vmem = pl.BlockSpec(memory_space=pltpu.VMEM)

    sides = {1: [], 2: [1]}.get(n_scen, [-1, 1])

    def moved(x, rows, cols):
        pairs = []
        for i in range(n_space):
            for j in range(n_scen):
                a, b = i + rows, j + cols
                if n_scen == 2:
                    b = b % 2
                if 0 <= a < n_space and 0 <= b < n_scen:
                    pairs.append((a * n_scen + b, i * n_scen + j))
        return lax.ppermute(x, ("space", "scen"), pairs)

    own_target = lax.dynamic_slice_in_dim(target_map, scen * BLOCK, BLOCK, 1)
    to_below = jnp.concatenate([dwell_map[tile - BLOCK :], own_target[tile - HALF :]], axis=0)
    to_above = jnp.concatenate([dwell_map[:BLOCK], own_target[:HALF]], axis=0)
    aboves = [moved(to_below, -1, c) for c in [0] + sides]
    belows = [moved(to_above, 1, c) for c in [0] + sides]
    mids = [dwell_map] + [moved(dwell_map, 0, c) for c in sides]

    fwd, adj, col = pl.pallas_call(
        bands_kernel,
        out_shape=(
            jax.ShapeDtypeStruct((scen_total * BLOCK, 2 * BLOCK), BF16),
            jax.ShapeDtypeStruct((scen_total, BLOCK, 2 * BLOCK), BF16),
            jax.ShapeDtypeStruct((scen_total, width, width), BF16),
        ),
        in_specs=[smem, smem, vmem, vmem],
        out_specs=(vmem, vmem, vmem),
        cost_estimate=pl.CostEstimate(flops=10**8, bytes_accessed=10**6, transcendentals=0),
        name="bands",
    )(offsets, rate_index, row_kernels, col_kernels)

    if n_scen <= 2:
        own = scen * BLOCK
        target = target_map
    else:
        own = jnp.int32(BLOCK)
        target = lax.dynamic_slice_in_dim(
            jnp.pad(target_map, ((0, 0), (BLOCK, BLOCK))), scen * BLOCK, width, 1
        )
    place = jnp.stack(
        [
            own,
            (space == 0).astype(jnp.int32),
            (space == n_space - 1).astype(jnp.int32),
            (scen == 0).astype(jnp.int32),
            (scen == n_scen - 1).astype(jnp.int32),
        ]
    ).astype(jnp.int32)

    return pl.pallas_call(
        functools.partial(step_kernel, blocks),
        out_shape=jax.ShapeDtypeStruct(dwell_map.shape, BF16),
        in_specs=[smem] * 3 + [vmem] * (5 + 3 * blocks),
        out_specs=vmem,
        scratch_shapes=[
            pltpu.VMEM((tile + 2 * BLOCK, width), BF16),
            pltpu.VMEM((deep, width), BF16),
            pltpu.VMEM((scen_total, deep, width), BF16),
            pltpu.VMEM((scen_total, deep, BLOCK), BF16),
        ],
        compiler_params=pltpu.CompilerParams(vmem_limit_bytes=48 * 1024 * 1024),
        cost_estimate=pl.CostEstimate(flops=10**9, bytes_accessed=10**6, transcendentals=0),
        name="step",
    )(place, rate_index, rate_table, fwd, adj, col, *mids, *aboves, *belows, target, bound_mask)


def solution(mesh):
    return jax.shard_map(
        shards,
        mesh=mesh,
        in_specs=(
            P("space", "scen"),
            P("space", None),
            P("space", "scen"),
            P(),
            P(),
            P(),
            P(),
            P(),
        ),
        out_specs=P("space", "scen"),
        check_vma=False,
    )
```

time: 109 us -> 25.7 us (0.24)
  the two profiles are of different devices: /device:TPU:0 before, /device:TPU:24 now
where the time goes in v1:
time: 25.7 us; the launch traced here: 25.3 us
  starting transfers between devices  13.6 us (53%)
  local copies, waits for them, and re-layouts  6.63 us (26%)
  Pallas kernels  4.94 us (19%)
    ppermute x5, starting transfers between devices, moved(): return lax.ppermute(x, ('space', 'scen'), pairs)  13.6 us
    unnamed x22, local copies, waits for them, and re-layouts  5.72 us
    pallas_call x1, Pallas kernels, shards(): pl.pallas_call(bands_kernel, out_shape=(jax.ShapeDtypeStruct((scen_total...  2.53 us
    pallas_call x1, Pallas kernels, shards(): pl.pallas_call(functools.partial(step_kernel, blocks), out_shape=jax.Shap...  2.41 us
    slice x2, local copies, waits for them, and re-layouts, shards(): to_above = jnp.concatenate([dwell_map[:BLOCK], own_target[:HALF]], axis=0)  0.82 us
  transfers between devices with their start and end apart: 5, of which 0 were waited for; matrix products, arithmetic and copies ran while one was open for 6% of the time, Pallas kernels for 10%

profile of v1, /device:TPU:24, one launch (start us, length us, event | category | flops | bytes accessed | tf_op | source)
XLA Modules:
  0.0 25.3 jit_solution(17823598635877710045)
XLA Ops:
  0.0 0.8 %fusion = (bf16[128,128]{1,0:T(8,128)(2,1)S(1)}, bf16[128,128]{1,0:T(8,128)(2,1)S(1)}) fusion(bf16[256,128]{1,0:T(8,128)(2,1)} %refs_0_.1), kind=kLoop, calls=%fused_computation.3 | loop fusion | bytes 131072 | tf_op jit(solution)/shard_map/slice | solution.py:154
  0.8 0.1 copy-done.1
  1.0 3.0 %collective-permute-start.2 = (bf16[192,128]{1,0:T(8,128)(2,1)S(1)}, bf16[192,128]{1,0:T(8,128)(2,1)S(1)}, u32[]{:S(2)}, u32[]{:S(2)}) collective-permute-start(bf16[192,128]{1,0:T(8,128)(2,1)S(1)} %pad_maximum_fusion), channel_id=1, source_target_pairs={{1,2},{0,3},{3,4},{2,5},{5,6},{4,7},{7,8},{6,9},{9,10},{8,11},{11,... | collective-permute-start | bytes 147464 | tf_op jit(solution)/shard_map/ppermute | solution.py:150
  4.0 3.5 %collective-permute-start.1 = (bf16[192,128]{1,0:T(8,128)(2,1)S(1)}, bf16[192,128]{1,0:T(8,128)(2,1)S(1)}, u32[]{:S(2)}, u32[]{:S(2)}) collective-permute-start(bf16[192,128]{1,0:T(8,128)(2,1)S(1)} %pad_maximum_fusion), channel_id=1, source_target_pairs={{0,2},{1,3},{2,4},{3,5},{4,6},{5,7},{6,8},{7,9},{8,10},{9,11},{10,... | collective-permute-start | bytes 147464 | tf_op jit(solution)/shard_map/ppermute | solution.py:150
  7.5 0.6 %collective-permute-start = (bf16[256,128]{1,0:T(8,128)(2,1)S(1)}, bf16[256,128]{1,0:T(8,128)(2,1)S(1)}, u32[]{:S(2)}, u32[]{:S(2)}) collective-permute-start(bf16[256,128]{1,0:T(8,128)(2,1)S(1)} %copy-done), channel_id=1, source_target_pairs={{1,0},{0,1},{3,2},{2,3},{5,4},{4,5},{7,6},{6,7},{9,8},{8,9},{11,10... | collective-permute-start | bytes 196616 | tf_op jit(solution)/shard_map/ppermute | solution.py:150
  8.1 3.6 %collective-permute-start.4 = (bf16[192,128]{1,0:T(8,128)(2,1)S(1)}, bf16[192,128]{1,0:T(8,128)(2,1)S(1)}, u32[]{:S(2)}, u32[]{:S(2)}) collective-permute-start(bf16[192,128]{1,0:T(8,128)(2,1)S(1)} %pad_maximum_fusion.1), channel_id=1, source_target_pairs={{3,0},{2,1},{5,2},{4,3},{7,4},{6,5},{9,6},{8,7},{11,8},{10,9},{13,... | collective-permute-start | bytes 147464 | tf_op jit(solution)/shard_map/ppermute | solution.py:150
  11.7 2.9 %collective-permute-start.3 = (bf16[192,128]{1,0:T(8,128)(2,1)S(1)}, bf16[192,128]{1,0:T(8,128)(2,1)S(1)}, u32[]{:S(2)}, u32[]{:S(2)}) collective-permute-start(bf16[192,128]{1,0:T(8,128)(2,1)S(1)} %pad_maximum_fusion.1), channel_id=1, source_target_pairs={{2,0},{3,1},{4,2},{5,3},{6,4},{7,5},{8,6},{9,7},{10,8},{11,9},{12,... | collective-permute-start | bytes 147464 | tf_op jit(solution)/shard_map/ppermute | solution.py:150
  14.6 0.0 copy-start.9
  14.6 0.6 %copy-done.9 = s32[4,1]{0,1:T(1,128)S(1)} copy-done((s32[4,1]{0,1:T(1,128)S(1)}, s32[4,1]{0,1:T(1,128)}, u32[]{:S(2)}) %copy-start.9) | copy-done | bytes 40
  15.2 0.7 %copy.11.levels = s32[4,1]{1,0:T(4,128)} copy(s32[4,1]{0,1:T(1,128)S(1)} %copy-done.9) | data formatting | bytes 32 | tf_op args[4]
  15.9 0.0 copy-done.8
  15.9 0.7 %copy.9.offsets = s32[4,2]{1,0:T(4,128)} copy(s32[4,2]{0,1:T(2,128)S(1)} %copy-done.8) | data formatting | bytes 64 | tf_op args[3]
  16.6 0.1 stack.39.place
  16.7 2.5 %bands.1 = (bf16[512,256]{1,0:T(8,128)(2,1)}, bf16[4,128,256]{2,1,0:T(8,128)(2,1)}, bf16[4,256,256]{2,1,0:T(8,128)(2,1)}) custom-call(s32[4,2]{1,0:T(4,128)} %copy.9.offsets, s32[4,1]{1,0:T(4,128)} %copy.11.levels, bf16[4,63]{1,0:T(4,128)(2,1)} %row_taps.1, bf16[4,63]{1,0:T(4,128)(2,1)} %col_taps.1), custom_call_target="tpu_custom_call" | custom-call | flops 100000000 | bytes 1000000 | tf_op jit(solution)/shard_map/bands/pallas_call | solution.py:159
  19.2 0.0 collective-permute-done.2.refs_3_
  19.2 0.0 collective-permute-done.1.refs_2_
  19.2 0.0 collective-permute-done.4.refs_5_
  19.2 0.0 copy-start.2
  19.2 0.0 copy-start.4
  19.3 0.7 %copy-done.2 = s32[4,1]{1,0:T(4,128)S(1)} copy-done((s32[4,1]{1,0:T(4,128)S(1)}, s32[4,1]{1,0:T(4,128)}, u32[]{:S(2)}) %copy-start.2) | copy-done | bytes 40
  19.9 1.0 %copy-done.5 = bf16[4,256,256]{2,1,0:T(8,128)(2,1)S(1)} copy-done((bf16[4,256,256]{2,1,0:T(8,128)(2,1)S(1)}, bf16[4,256,256]{2,1,0:T(8,128)(2,1)}, u32[]{:S(2)}) %copy-start.5) | copy-done | bytes 524312
  21.0 0.9 %copy-done.6 = bf16[512,256]{1,0:T(8,128)(2,1)S(1)} copy-done((bf16[512,256]{1,0:T(8,128)(2,1)S(1)}, bf16[512,256]{1,0:T(8,128)(2,1)}, u32[]{:S(2)}) %copy-start.6) | copy-done | bytes 262168
  21.9 0.9 %copy-done.7 = bf16[4,128,256]{2,1,0:T(8,128)(2,1)S(1)} copy-done((bf16[4,128,256]{2,1,0:T(8,128)(2,1)S(1)}, bf16[4,128,256]{2,1,0:T(8,128)(2,1)}, u32[]{:S(2)}) %copy-start.7) | copy-done | bytes 262168
  22.9 2.4 %step.1 = bf16[256,128]{1,0:T(8,128)(2,1)} custom-call(s32[5]{0:T(128)S(1)} %stack.39.place, s32[4,1]{1,0:T(4,128)S(1)} %copy-done.2, f32[4]{0:T(128)S(1)} %copy-done.4, bf16[512,256]{1,0:T(8,128)(2,1)S(1)} %copy-done.6, bf16[4,128,256]{2,1,0:T(8,128)(2,1)S(1)} %copy-done.7, bf16[4,256,256]{2,1,0:T(8,128)(2,1)S(1)} %copy-done.5, ...), custom_call_target="tpu_custom_call" | custom-call | flops 1000000000 | bytes 1000000 | tf_op jit(solution)/shard_map/step/pallas_call | solution.py:190
  (15 shorter events, 0.0 us)
Async XLA Ops:
  0.0 0.9 %copy-start.1 = (bf16[256,256]{1,0:T(8,128)(2,1)S(1)}, bf16[256,256]{1,0:T(8,128)(2,1)}, u32[]{:S(2)}) copy-start(bf16[256,256]{1,0:T(8,128)(2,1)} %refs_6_.1) | copy-start | bytes 393220
  0.9 6.5 %copy-start = (bf16[256,128]{1,0:T(8,128)(2,1)S(1)}, bf16[256,128]{1,0:T(8,128)(2,1)}, u32[]{:S(2)}) copy-start(bf16[256,128]{1,0:T(8,128)(2,1)} %refs_0_.1) | copy-start | bytes 196612
  1.0 18.2 %collective-permute-start.2 = (bf16[192,128]{1,0:T(8,128)(2,1)S(1)}, bf16[192,128]{1,0:T(8,128)(2,1)S(1)}, u32[]{:S(2)}, u32[]{:S(2)}) collective-permute-start(bf16[192,128]{1,0:T(8,128)(2,1)S(1)} %pad_maximum_fusion), channel_id=1, source_target_pairs={{1,2},{0,3},{3,4},{2,5},{5,6},{4,7},{7,8},{6,9},{9,10},{8,11},{11,... | collective-permute-start | bytes 147464 | tf_op jit(solution)/shard_map/ppermute | solution.py:150
  4.0 15.2 %collective-permute-start.1 = (bf16[192,128]{1,0:T(8,128)(2,1)S(1)}, bf16[192,128]{1,0:T(8,128)(2,1)S(1)}, u32[]{:S(2)}, u32[]{:S(2)}) collective-permute-start(bf16[192,128]{1,0:T(8,128)(2,1)S(1)} %pad_maximum_fusion), channel_id=1, source_target_pairs={{0,2},{1,3},{2,4},{3,5},{4,6},{5,7},{6,8},{7,9},{8,10},{9,11},{10,... | collective-permute-start | bytes 147464 | tf_op jit(solution)/shard_map/ppermute | solution.py:150
  7.5 11.7 %collective-permute-start = (bf16[256,128]{1,0:T(8,128)(2,1)S(1)}, bf16[256,128]{1,0:T(8,128)(2,1)S(1)}, u32[]{:S(2)}, u32[]{:S(2)}) collective-permute-start(bf16[256,128]{1,0:T(8,128)(2,1)S(1)} %copy-done), channel_id=1, source_target_pairs={{1,0},{0,1},{3,2},{2,3},{5,4},{4,5},{7,6},{6,7},{9,8},{8,9},{11,10... | collective-permute-start | bytes 196616 | tf_op jit(solution)/shard_map/ppermute | solution.py:150
  8.1 11.1 %collective-permute-start.4 = (bf16[192,128]{1,0:T(8,128)(2,1)S(1)}, bf16[192,128]{1,0:T(8,128)(2,1)S(1)}, u32[]{:S(2)}, u32[]{:S(2)}) collective-permute-start(bf16[192,128]{1,0:T(8,128)(2,1)S(1)} %pad_maximum_fusion.1), channel_id=1, source_target_pairs={{3,0},{2,1},{5,2},{4,3},{7,4},{6,5},{9,6},{8,7},{11,8},{10,9},{13,... | collective-permute-start | bytes 147464 | tf_op jit(solution)/shard_map/ppermute | solution.py:150
  11.7 7.5 %collective-permute-start.3 = (bf16[192,128]{1,0:T(8,128)(2,1)S(1)}, bf16[192,128]{1,0:T(8,128)(2,1)S(1)}, u32[]{:S(2)}, u32[]{:S(2)}) collective-permute-start(bf16[192,128]{1,0:T(8,128)(2,1)S(1)} %pad_maximum_fusion.1), channel_id=1, source_target_pairs={{2,0},{3,1},{4,2},{5,3},{6,4},{7,5},{8,6},{9,7},{10,8},{11,9},{12,... | collective-permute-start | bytes 147464 | tf_op jit(solution)/shard_map/ppermute | solution.py:150
  14.6 0.7 %copy-start.9 = (s32[4,1]{0,1:T(1,128)S(1)}, s32[4,1]{0,1:T(1,128)}, u32[]{:S(2)}) copy-start(s32[4,1]{0,1:T(1,128)} %param.12) | copy-start | bytes 52
  15.2 0.7 %copy-start.8 = (s32[4,2]{0,1:T(2,128)S(1)}, s32[4,2]{0,1:T(2,128)}, u32[]{:S(2)}) copy-start(s32[4,2]{0,1:T(2,128)} %param.11) | copy-start | bytes 100
  16.7 2.6 %copy-start.3 = (s32[256,128]{1,0:T(8,128)S(1)}, s32[256,128]{1,0:T(8,128)}, u32[]{:S(2)}) copy-start(s32[256,128]{1,0:T(8,128)} %refs_7_.1) | copy-start | bytes 393220
  19.2 0.7 %copy-start.2 = (s32[4,1]{1,0:T(4,128)S(1)}, s32[4,1]{1,0:T(4,128)}, u32[]{:S(2)}) copy-start(s32[4,1]{1,0:T(4,128)} %copy.11.levels) | copy-start | bytes 52
  19.2 0.7 %copy-start.4 = (f32[4]{0:T(128)S(1)}, f32[4]{0:T(128)}, u32[]{:S(2)}) copy-start(f32[4]{0:T(128)} %rates.1) | copy-start | bytes 52
  19.9 1.0 %copy-start.5 = (bf16[4,256,256]{2,1,0:T(8,128)(2,1)S(1)}, bf16[4,256,256]{2,1,0:T(8,128)(2,1)}, u32[]{:S(2)}) copy-start(bf16[4,256,256]{2,1,0:T(8,128)(2,1)} %get-tuple-element.10.col) | copy-start | bytes 1572868
  21.0 0.9 %copy-start.6 = (bf16[512,256]{1,0:T(8,128)(2,1)S(1)}, bf16[512,256]{1,0:T(8,128)(2,1)}, u32[]{:S(2)}) copy-start(bf16[512,256]{1,0:T(8,128)(2,1)} %get-tuple-element.8.fwd) | copy-start | bytes 786436
  21.9 0.9 %copy-start.7 = (bf16[4,128,256]{2,1,0:T(8,128)(2,1)S(1)}, bf16[4,128,256]{2,1,0:T(8,128)(2,1)}, u32[]{:S(2)}) copy-start(bf16[4,128,256]{2,1,0:T(8,128)(2,1)} %get-tuple-element.9.adj) | copy-start | bytes 786436

commit v2 on v1

--- a/solution.py
+++ b/solution.py
@@ -23,7 +23,7 @@
     return pltpu.roll(lines, 0, 1, stride=1, stride_axis=0).astype(BF16)
 
 
-def bands_kernel(offsets, levels, row_taps, col_taps, fwd_ref, adj_ref, col_ref):
+def bands_kernel(offsets, levels, rates, row_taps, col_taps, fwd_ref, adj_ref, col_ref, rate_ref):
     scen_total, width = col_ref.shape[0], col_ref.shape[1]
     blocks = width // BLOCK
     turn = (
@@ -44,8 +44,9 @@
         return out
 
     for s in range(scen_total):
-        level = levels[s, 0]
-        shift_row, shift_col = offsets[s, 0], offsets[s, 1]
+        level = levels[s]
+        rate_ref[s] = jnp.full(rate_ref.shape[1:], rates[level], F32)
+        shift_row, shift_col = offsets[0, s], offsets[1, s]
         fwd_ref[s * BLOCK : (s + 1) * BLOCK, :] = band(
             pick(rows, level), HALF - RADIUS - shift_row, 2 * BLOCK
         )
@@ -59,26 +60,50 @@
                 col_ref[s, j * BLOCK : (j + 1) * BLOCK, y * BLOCK : (y + 1) * BLOCK] = piece
 
 
-def step_kernel(blocks, place, levels, rates, fwd, adj, col, *refs):
-    mids, aboves, belows = refs[:blocks], refs[blocks : 2 * blocks], refs[2 * blocks : 3 * blocks]
-    target, bound, out, dwell_all, target_all, fwd_all, back_all = refs[3 * blocks :]
+def step_kernel(blocks, rates, fwd, adj, col, *refs):
+    mids, outers = refs[:blocks], refs[blocks : 2 * blocks]
+    inners, target, bound, out, dwell_all, target_all, fwd_all, back_all = refs[2 * blocks :]
     scen_total = adj.shape[0]
     tile = out.shape[0]
     deep = tile + 2 * HALF
-    own, first_row, last_row, first_col, last_col = [place[i] for i in range(5)]
+    space, scen = lax.axis_index("space"), lax.axis_index("scen")
+    first_row, last_row = space == 0, space == lax.axis_size("space") - 1
+    even = lax.rem(space, 2) == 0
+    own = scen * BLOCK if blocks == 2 else (blocks - 1) // 2 * BLOCK
     own_lanes = pl.ds(pl.multiple_of(own, BLOCK), BLOCK)
     if blocks == 2:
         spots = [own_lanes, pl.ds(pl.multiple_of(BLOCK - own, BLOCK), BLOCK)]
     else:
         spots = [own_lanes, pl.ds(0, BLOCK), pl.ds(2 * BLOCK, BLOCK)][:blocks]
 
+    def rows(at, count):
+        return pl.ds(pl.multiple_of(at, HALF), count)
+
+    inner_dwell = rows(jnp.where(even, BLOCK + tile, 0), BLOCK)
+    outer_dwell = rows(jnp.where(even, 0, BLOCK + tile), BLOCK)
+    inner_target = rows(jnp.where(even, HALF + tile, 0), HALF)
+    outer_target = rows(jnp.where(even, 0, HALF + tile), HALF)
     target_all[HALF : HALF + tile, :] = target[...]
     for b, lanes in enumerate(spots):
-        dwell_all[0:BLOCK, lanes] = aboves[b][0:BLOCK, :]
         dwell_all[BLOCK : BLOCK + tile, lanes] = mids[b][...]
-        dwell_all[BLOCK + tile :, lanes] = belows[b][0:BLOCK, :]
-        target_all[0:HALF, lanes] = aboves[b][BLOCK:, :]
-        target_all[HALF + tile :, lanes] = belows[b][BLOCK:, :]
+        low = blocks * BLOCK + b * HALF
+        dwell_all[inner_dwell, lanes] = inners[b * BLOCK : (b + 1) * BLOCK, :]
+        target_all[inner_target, lanes] = inners[low : low + HALF, :]
+        dwell_all[outer_dwell, lanes] = outers[b][:BLOCK, :]
+        target_all[outer_target, lanes] = outers[b][BLOCK:, :]
+
+    @pl.when(first_row | last_row)
+    def _():
+        dwell_all[outer_dwell, :] = jnp.zeros((BLOCK, blocks * BLOCK), BF16)
+        target_all[outer_target, :] = jnp.zeros((HALF, blocks * BLOCK), BF16)
+
+    if blocks > 2:
+        for edge, lanes in zip((scen == 0, scen == lax.axis_size("scen") - 1), spots[1:]):
+
+            @pl.when(edge)
+            def _():
+                dwell_all[:, lanes] = jnp.zeros((tile + 2 * BLOCK, BLOCK), BF16)
+                target_all[:, lanes] = jnp.zeros((deep, BLOCK), BF16)
 
     for r in range(deep // BLOCK):
         view = dwell_all[r * BLOCK : (r + 2) * BLOCK, :]
@@ -88,25 +113,24 @@
 
     goal = target_all[...].astype(F32)
     for s in range(scen_total):
-        rate = rates[levels[s, 0]]
+        rate = rates[s, 0:1, 0:1]
         removal = lax.dot_general(
             fwd_all[s], col[s], (((1,), (1,)), ((), ())), preferred_element_type=F32
         )
-        above_rate = jnp.where(first_row == 1, 0.0, rate)
-        below_rate = jnp.where(last_row == 1, 0.0, rate)
         removal = jnp.concatenate(
             [
-                above_rate * removal[:HALF],
+                jnp.where(first_row, 0.0, rate) * removal[:HALF],
                 rate * removal[HALF : deep - HALF],
-                below_rate * removal[deep - HALF :],
+                jnp.where(last_row, 0.0, rate) * removal[deep - HALF :],
             ],
             axis=0,
         )
         misfit = (removal - goal).astype(BF16)
         if blocks > 2:
             lane = lax.broadcasted_iota(jnp.int32, misfit.shape, 1)
-            inside = (lane >= first_col * BLOCK) & (lane < (blocks - last_col) * BLOCK)
-            misfit = jnp.where(inside, misfit, jnp.zeros_like(misfit))
+            low = jnp.where(scen == 0, BLOCK, 0)
+            high = jnp.where(scen == lax.axis_size("scen") - 1, 2 * BLOCK, 3 * BLOCK)
+            misfit = jnp.where((lane >= low) & (lane < high), misfit, jnp.zeros_like(misfit))
         back = jnp.dot(misfit, col[s, :, own_lanes], preferred_element_type=F32)
         back_all[s] = ((rate / scen_total) * back).astype(BF16)
 
@@ -138,59 +162,80 @@
 
     sides = {1: [], 2: [1]}.get(n_scen, [-1, 1])
 
-    def moved(x, rows, cols):
+    def moved(x, partner):
         pairs = []
         for i in range(n_space):
             for j in range(n_scen):
-                a, b = i + rows, j + cols
-                if n_scen == 2:
-                    b = b % 2
-                if 0 <= a < n_space and 0 <= b < n_scen:
-                    pairs.append((a * n_scen + b, i * n_scen + j))
+                a, b = partner(i, j)
+                pairs.append((a * n_scen + b % n_scen, i * n_scen + j))
         return lax.ppermute(x, ("space", "scen"), pairs)
 
-    own_target = lax.dynamic_slice_in_dim(target_map, scen * BLOCK, BLOCK, 1)
-    to_below = jnp.concatenate([dwell_map[tile - BLOCK :], own_target[tile - HALF :]], axis=0)
-    to_above = jnp.concatenate([dwell_map[:BLOCK], own_target[:HALF]], axis=0)
-    aboves = [moved(to_below, -1, c) for c in [0] + sides]
-    belows = [moved(to_above, 1, c) for c in [0] + sides]
-    mids = [dwell_map] + [moved(dwell_map, 0, c) for c in sides]
-
-    fwd, adj, col = pl.pallas_call(
+    def side(cols):
+        return lambda i, j: (i, j + cols)
+
+    def inner(i, j):
+        return i ^ 1, j
+
+    def outer(cols):
+        def partner(i, j):
+            if i in (0, n_space - 1):
+                return i, (j ^ 1 if n_scen % 2 == 0 else j)
+            return ((i - 1) ^ 1) + 1, j + cols
+
+        return partner
+
+    odd = lax.rem(space, 2)
+
+    def edge(x, low, count):
+        return lax.dynamic_slice_in_dim(x, low * (tile - count), count, 0)
+
+    window = [0] + sides
+    columns = [lax.rem(scen + n_scen + c, n_scen) * BLOCK for c in window]
+    mids = [dwell_map] + [moved(dwell_map, side(c)) for c in sides]
+    to_outer = jnp.concatenate(
+        [
+            edge(dwell_map, odd, BLOCK),
+            lax.dynamic_slice(target_map, (odd * (tile - HALF), columns[0]), (HALF, BLOCK)),
+        ],
+        axis=0,
+    )
+    outers = [moved(to_outer, outer(c)) for c in window]
+    to_inner = jnp.concatenate(
+        [edge(m, 1 - odd, BLOCK) for m in mids]
+        + [
+            lax.dynamic_slice(target_map, ((1 - odd) * (tile - HALF), c), (HALF, BLOCK))
+            for c in columns
+        ],
+        axis=0,
+    )
+    inners = moved(to_inner, inner)
+
+    levels = rate_index.reshape(scen_total)
+    fwd, adj, col, rates = pl.pallas_call(
         bands_kernel,
         out_shape=(
-            jax.ShapeDtypeStruct((scen_total * BLOCK, 2 * BLOCK), BF16),
-            jax.ShapeDtypeStruct((scen_total, BLOCK, 2 * BLOCK), BF16),
-            jax.ShapeDtypeStruct((scen_total, width, width), BF16),
+            pltpu.VMEM((scen_total * BLOCK, 2 * BLOCK), BF16),
+            pltpu.VMEM((scen_total, BLOCK, 2 * BLOCK), BF16),
+            pltpu.VMEM((scen_total, width, width), BF16),
+            pltpu.VMEM((scen_total, 8, BLOCK), F32),
         ),
-        in_specs=[smem, smem, vmem, vmem],
-        out_specs=(vmem, vmem, vmem),
+        in_specs=[smem] * 3 + [vmem] * 2,
+        out_specs=(vmem,) * 4,
         cost_estimate=pl.CostEstimate(flops=10**8, bytes_accessed=10**6, transcendentals=0),
         name="bands",
-    )(offsets, rate_index, row_kernels, col_kernels)
+    )(offsets.T, levels, rate_table, row_kernels, col_kernels)
 
     if n_scen <= 2:
-        own = scen * BLOCK
         target = target_map
     else:
-        own = jnp.int32(BLOCK)
         target = lax.dynamic_slice_in_dim(
             jnp.pad(target_map, ((0, 0), (BLOCK, BLOCK))), scen * BLOCK, width, 1
         )
-    place = jnp.stack(
-        [
-            own,
-            (space == 0).astype(jnp.int32),
-            (space == n_space - 1).astype(jnp.int32),
-            (scen == 0).astype(jnp.int32),
-            (scen == n_scen - 1).astype(jnp.int32),
-        ]
-    ).astype(jnp.int32)
 
     return pl.pallas_call(
         functools.partial(step_kernel, blocks),
         out_shape=jax.ShapeDtypeStruct(dwell_map.shape, BF16),
-        in_specs=[smem] * 3 + [vmem] * (5 + 3 * blocks),
+        in_specs=[vmem] * (7 + 2 * blocks),
         out_specs=vmem,
         scratch_shapes=[
             pltpu.VMEM((tile + 2 * BLOCK, width), BF16),
@@ -201,7 +246,7 @@
         compiler_params=pltpu.CompilerParams(vmem_limit_bytes=48 * 1024 * 1024),
         cost_estimate=pl.CostEstimate(flops=10**9, bytes_accessed=10**6, transcendentals=0),
         name="step",
-    )(place, rate_index, rate_table, fwd, adj, col, *mids, *aboves, *belows, target, bound_mask)
+    )(rates, fwd, adj, col, *mids, *outers, inners, target, bound_mask)
 
 
 def solution(mesh):

time: 25.7 us -> 13.9 us (0.54)
  the two profiles are of different devices: /device:TPU:24 before, /device:TPU:0 now
where the time goes in v2:
time: 13.9 us; the launch traced here: 13.6 us
  starting transfers between devices  5.13 us (37%)
  waiting for transfers between devices  4.87 us (35%)
  Pallas kernels  3.47 us (25%)
    ppermute x4, starting transfers between devices, moved(): return lax.ppermute(x, ('space', 'scen'), pairs)  5.13 us
    ppermute x4, waiting for transfers between devices, moved(): return lax.ppermute(x, ('space', 'scen'), pairs)  4.87 us
    pallas_call x1, Pallas kernels, shards(): pl.pallas_call(functools.partial(step_kernel, blocks), out_shape=jax.Shap...  1.87 us
    pallas_call x1, Pallas kernels, shards(): pl.pallas_call(bands_kernel, out_shape=(pltpu.VMEM((scen_total * BLOCK, 2...  1.6 us
  transfers between devices with their start and end apart: 4, of which 3 were waited for; matrix products, arithmetic and copies ran while one was open for 0% of the time, Pallas kernels for 12%

profile of v2, /device:TPU:0, one launch (start us, length us, event | category | flops | bytes accessed | tf_op | source)
XLA Modules:
  0.0 13.6 jit_solution(11722837524063942318)
XLA Ops:
  0.0 0.0 copy-start
  0.0 0.0 copy-start.1
  0.0 3.0 %collective-permute-start = (bf16[256,128]{1,0:T(8,128)(2,1)}, bf16[256,128]{1,0:T(8,128)(2,1)S(1)}, u32[]{:S(2)}, u32[]{:S(2)}) collective-permute-start(bf16[256,128]{1,0:T(8,128)(2,1)} %refs_0_.1), channel_id=1, source_target_pairs={{1,0},{0,1},{3,2},{2,3},{5,4},{4,5},{7,6},{6,7},{9,8},{8,9},{11,10... | collective-permute-start | bytes 196616 | tf_op jit(solution)/shard_map/ppermute | solution.py:171
  3.0 0.0 copy-done
  3.0 0.0 copy-done.1
  3.0 2.5 %collective-permute-done.refs_1_ = bf16[256,128]{1,0:T(8,128)(2,1)S(1)} collective-permute-done((bf16[256,128]{1,0:T(8,128)(2,1)}, bf16[256,128]{1,0:T(8,128)(2,1)S(1)}, u32[]{:S(2)}, u32[]{:S(2)}) %collective-permute-start) | collective-permute-done | bytes 65568 | tf_op jit(solution)/shard_map/ppermute | solution.py:171
  5.5 0.1 collective-permute-start.3
  5.6 2.0 %collective-permute-start.2 = (bf16[192,128]{1,0:T(8,128)(2,1)S(1)}, bf16[192,128]{1,0:T(8,128)(2,1)S(1)}, u32[]{:S(2)}, u32[]{:S(2)}) collective-permute-start(bf16[192,128]{1,0:T(8,128)(2,1)S(1)} %pad_maximum_fusion.1), channel_id=1, source_target_pairs={{1,0},{0,1},{5,2},{4,3},{3,4},{2,5},{9,6},{8,7},{7,8},{6,9},{13,10... | collective-permute-start | bytes 147464 | tf_op jit(solution)/shard_map/ppermute | solution.py:171
  7.6 0.1 collective-permute-start.1
  7.7 0.0 copy-start.2
  7.7 1.6 %bands.1 = (bf16[512,256]{1,0:T(8,128)(2,1)S(1)}, bf16[4,128,256]{2,1,0:T(8,128)(2,1)S(1)}, bf16[4,256,256]{2,1,0:T(8,128)(2,1)S(1)}, f32[4,8,128]{2,1,0:T(8,128)S(1)}) custom-call(s32[2,4]{1,0:T(2,128)} %bitcast.2, s32[4]{0:T(128)} %bitcast.3, f32[4]{0:T(128)} %rates.1, bf16[4,63]{1,0:T(4,128)(2,1)} %row_taps.1, bf16[4,63]{1,0:T(4,128)(2,1)} %col_taps.1), custom_call_target="tpu_custom_call" | custom-call | flops 100000000 | bytes 1000000 | tf_op jit(solution)/shard_map/bands/pallas_call | solution.py:214
  9.3 0.4 %collective-permute-done.2.refs_3_ = bf16[192,128]{1,0:T(8,128)(2,1)S(1)} collective-permute-done((bf16[192,128]{1,0:T(8,128)(2,1)S(1)}, bf16[192,128]{1,0:T(8,128)(2,1)S(1)}, u32[]{:S(2)}, u32[]{:S(2)}) %collective-permute-start.2) | collective-permute-done | bytes 49184 | tf_op jit(solution)/shard_map/ppermute | solution.py:171
  9.8 2.0 %collective-permute-done.1.refs_2_ = bf16[192,128]{1,0:T(8,128)(2,1)S(1)} collective-permute-done((bf16[192,128]{1,0:T(8,128)(2,1)S(1)}, bf16[192,128]{1,0:T(8,128)(2,1)S(1)}, u32[]{:S(2)}, u32[]{:S(2)}) %collective-permute-start.1) | collective-permute-done | bytes 49184 | tf_op jit(solution)/shard_map/ppermute | solution.py:171
  11.7 0.0 collective-permute-done.3.refs_4_
  11.7 0.0 copy-done.2
  11.7 1.9 %step.1 = bf16[256,128]{1,0:T(8,128)(2,1)} custom-call(f32[4,8,128]{2,1,0:T(8,128)S(1)} %get-tuple-element.9.rates, bf16[512,256]{1,0:T(8,128)(2,1)S(1)} %get-tuple-element.10.fwd, bf16[4,128,256]{2,1,0:T(8,128)(2,1)S(1)} %get-tuple-element.11.adj, bf16[4,256,256]{2,1,0:T(8,128)(2,1)S(1)} %get-tuple-element.12.col, bf16[256,128]{1,0:T(8,128)(2,1)S(1)} %copy-done, ...), custom_call_target="tpu_custom_call" | custom-call | flops 1000000000 | bytes 1000000 | tf_op jit(solution)/shard_map/step/pallas_call | solution.py:235
  (5 shorter events, 0.0 us)
Async XLA Ops:
  0.0 3.0 %copy-start = (bf16[256,128]{1,0:T(8,128)(2,1)S(1)}, bf16[256,128]{1,0:T(8,128)(2,1)}, u32[]{:S(2)}) copy-start(bf16[256,128]{1,0:T(8,128)(2,1)} %refs_0_.1) | copy-start | bytes 196612
  0.0 3.0 %copy-start.1 = (bf16[256,256]{1,0:T(8,128)(2,1)S(1)}, bf16[256,256]{1,0:T(8,128)(2,1)}, u32[]{:S(2)}) copy-start(bf16[256,256]{1,0:T(8,128)(2,1)} %refs_5_.1) | copy-start | bytes 393220
  0.0 5.5 %collective-permute-start = (bf16[256,128]{1,0:T(8,128)(2,1)}, bf16[256,128]{1,0:T(8,128)(2,1)S(1)}, u32[]{:S(2)}, u32[]{:S(2)}) collective-permute-start(bf16[256,128]{1,0:T(8,128)(2,1)} %refs_0_.1), channel_id=1, source_target_pairs={{1,0},{0,1},{3,2},{2,3},{5,4},{4,5},{7,6},{6,7},{9,8},{8,9},{11,10... | collective-permute-start | bytes 196616 | tf_op jit(solution)/shard_map/ppermute | solution.py:171
  5.5 6.2 %collective-permute-start.3 = (bf16[384,128]{1,0:T(8,128)(2,1)S(1)}, bf16[384,128]{1,0:T(8,128)(2,1)S(1)}, u32[]{:S(2)}, u32[]{:S(2)}) collective-permute-start(bf16[384,128]{1,0:T(8,128)(2,1)S(1)} %pad_maximum_fusion), channel_id=1, source_target_pairs={{2,0},{3,1},{0,2},{1,3},{6,4},{7,5},{4,6},{5,7},{10,8},{11,9},{8,1... | collective-permute-start | bytes 294920 | tf_op jit(solution)/shard_map/ppermute | solution.py:171
  5.6 4.2 %collective-permute-start.2 = (bf16[192,128]{1,0:T(8,128)(2,1)S(1)}, bf16[192,128]{1,0:T(8,128)(2,1)S(1)}, u32[]{:S(2)}, u32[]{:S(2)}) collective-permute-start(bf16[192,128]{1,0:T(8,128)(2,1)S(1)} %pad_maximum_fusion.1), channel_id=1, source_target_pairs={{1,0},{0,1},{5,2},{4,3},{3,4},{2,5},{9,6},{8,7},{7,8},{6,9},{13,10... | collective-permute-start | bytes 147464 | tf_op jit(solution)/shard_map/ppermute | solution.py:171
  7.6 4.1 %collective-permute-start.1 = (bf16[192,128]{1,0:T(8,128)(2,1)S(1)}, bf16[192,128]{1,0:T(8,128)(2,1)S(1)}, u32[]{:S(2)}, u32[]{:S(2)}) collective-permute-start(bf16[192,128]{1,0:T(8,128)(2,1)S(1)} %pad_maximum_fusion.1), channel_id=1, source_target_pairs={{1,0},{0,1},{4,2},{5,3},{2,4},{3,5},{8,6},{9,7},{6,8},{7,9},{12,10... | collective-permute-start | bytes 147464 | tf_op jit(solution)/shard_map/ppermute | solution.py:171
  7.7 4.0 %copy-start.2 = (s32[256,128]{1,0:T(8,128)S(1)}, s32[256,128]{1,0:T(8,128)}, u32[]{:S(2)}) copy-start(s32[256,128]{1,0:T(8,128)} %refs_6_.1) | copy-start | bytes 393220

commit v3 on v2

--- a/solution.py
+++ b/solution.py
@@ -62,7 +62,8 @@
 
 def step_kernel(blocks, rates, fwd, adj, col, *refs):
     mids, outers = refs[:blocks], refs[blocks : 2 * blocks]
-    inners, target, bound, out, dwell_all, target_all, fwd_all, back_all = refs[2 * blocks :]
+    inners = refs[2 * blocks : 3 * blocks]
+    target, bound, out, dwell_all, target_all, fwd_all, back_all = refs[3 * blocks :]
     scen_total = adj.shape[0]
     tile = out.shape[0]
     deep = tile + 2 * HALF
@@ -86,9 +87,8 @@
     target_all[HALF : HALF + tile, :] = target[...]
     for b, lanes in enumerate(spots):
         dwell_all[BLOCK : BLOCK + tile, lanes] = mids[b][...]
-        low = blocks * BLOCK + b * HALF
-        dwell_all[inner_dwell, lanes] = inners[b * BLOCK : (b + 1) * BLOCK, :]
-        target_all[inner_target, lanes] = inners[low : low + HALF, :]
+        dwell_all[inner_dwell, lanes] = inners[b][:BLOCK, :]
+        target_all[inner_target, lanes] = inners[b][BLOCK:, :]
         dwell_all[outer_dwell, lanes] = outers[b][:BLOCK, :]
         target_all[outer_target, lanes] = outers[b][BLOCK:, :]
 
@@ -173,8 +173,8 @@
     def side(cols):
         return lambda i, j: (i, j + cols)
 
-    def inner(i, j):
-        return i ^ 1, j
+    def inner(cols):
+        return lambda i, j: (i ^ 1, j + cols)
 
     def outer(cols):
         def partner(i, j):
@@ -201,14 +201,13 @@
     )
     outers = [moved(to_outer, outer(c)) for c in window]
     to_inner = jnp.concatenate(
-        [edge(m, 1 - odd, BLOCK) for m in mids]
-        + [
-            lax.dynamic_slice(target_map, ((1 - odd) * (tile - HALF), c), (HALF, BLOCK))
-            for c in columns
+        [
+            edge(dwell_map, 1 - odd, BLOCK),
+            lax.dynamic_slice(target_map, ((1 - odd) * (tile - HALF), columns[0]), (HALF, BLOCK)),
         ],
         axis=0,
     )
-    inners = moved(to_inner, inner)
+    inners = [moved(to_inner, inner(c)) for c in window]
 
     levels = rate_index.reshape(scen_total)
     fwd, adj, col, rates = pl.pallas_call(
@@ -235,7 +234,7 @@
     return pl.pallas_call(
         functools.partial(step_kernel, blocks),
         out_shape=jax.ShapeDtypeStruct(dwell_map.shape, BF16),
-        in_specs=[vmem] * (7 + 2 * blocks),
+        in_specs=[vmem] * (6 + 3 * blocks),
         out_specs=vmem,
         scratch_shapes=[
             pltpu.VMEM((tile + 2 * BLOCK, width), BF16),
@@ -246,7 +245,7 @@
         compiler_params=pltpu.CompilerParams(vmem_limit_bytes=48 * 1024 * 1024),
         cost_estimate=pl.CostEstimate(flops=10**9, bytes_accessed=10**6, transcendentals=0),
         name="step",
-    )(rates, fwd, adj, col, *mids, *outers, inners, target, bound_mask)
+    )(rates, fwd, adj, col, *mids, *outers, *inners, target, bound_mask)
 
 
 def solution(mesh):

time: 13.9 us -> 12.1 us (0.87); the launches traced: 13.6 us -> 12 us
  waiting for transfers between devices: 4.87 us -> 2.07 us
  local copies, waits for them, and re-layouts: 0.04 us -> 0.95 us
  starting transfers between devices: 5.13 us -> 5.43 us
    ppermute x4 -> x5, waiting for transfers between devices: 4.87 us -> 2.07 us  [moved(): return lax.ppermute(x, ('space', 'scen'), pairs)]
    unnamed x6, local copies, waits for them, and re-layouts: 0.01 us -> 0.94 us
    ppermute x4 -> x5, starting transfers between devices: 5.13 us -> 5.43 us  [moved(): return lax.ppermute(x, ('space', 'scen'), pairs)]
  transfers between devices with their start and end apart: 4 -> 5, of which waited for: 3 -> 2; matrix products, arithmetic and copies ran while one was open for 0% -> 0% of each run, Pallas kernels for 12% -> 13%
where the time goes in v3:
time: 12.1 us; the launch traced here: 12 us
  starting transfers between devices  5.43 us (45%)
  Pallas kernels  3.48 us (29%)
  waiting for transfers between devices  2.07 us (17%)
  local copies, waits for them, and re-layouts  0.95 us (8%)
    ppermute x5, starting transfers between devices, moved(): return lax.ppermute(x, ('space', 'scen'), pairs)  5.43 us
    ppermute x5, waiting for transfers between devices, moved(): return lax.ppermute(x, ('space', 'scen'), pairs)  2.07 us
    pallas_call x1, Pallas kernels, shards(): pl.pallas_call(functools.partial(step_kernel, blocks), out_shape=jax.Shap...  1.87 us
    pallas_call x1, Pallas kernels, shards(): pl.pallas_call(bands_kernel, out_shape=(pltpu.VMEM((scen_total * BLOCK, 2...  1.61 us
    unnamed x6, local copies, waits for them, and re-layouts  0.94 us
  transfers between devices with their start and end apart: 5, of which 2 were waited for; matrix products, arithmetic and copies ran while one was open for 0% of the time, Pallas kernels for 13%

profile of v3, /device:TPU:0, one launch (start us, length us, event | category | flops | bytes accessed | tf_op | source)
XLA Modules:
  0.0 12.0 jit_solution(11247929983597864235)
XLA Ops:
  0.0 0.0 copy-start
  0.0 0.0 copy-start.1
  0.0 0.8 %copy-done = bf16[256,128]{1,0:T(8,128)(2,1)S(1)} copy-done((bf16[256,128]{1,0:T(8,128)(2,1)S(1)}, bf16[256,128]{1,0:T(8,128)(2,1)}, u32[]{:S(2)}) %copy-start) | copy-done | bytes 65560
  0.8 0.1 copy-done.1
  1.0 3.0 %collective-permute-start.2 = (bf16[192,128]{1,0:T(8,128)(2,1)S(1)}, bf16[192,128]{1,0:T(8,128)(2,1)S(1)}, u32[]{:S(2)}, u32[]{:S(2)}) collective-permute-start(bf16[192,128]{1,0:T(8,128)(2,1)S(1)} %pad_maximum_fusion), channel_id=1, source_target_pairs={{1,0},{0,1},{5,2},{4,3},{3,4},{2,5},{9,6},{8,7},{7,8},{6,9},{13,10... | collective-permute-start | bytes 147464 | tf_op jit(solution)/shard_map/ppermute | solution.py:171
  4.0 0.1 collective-permute-start.1
  4.1 1.9 %collective-permute-start = (bf16[256,128]{1,0:T(8,128)(2,1)S(1)}, bf16[256,128]{1,0:T(8,128)(2,1)S(1)}, u32[]{:S(2)}, u32[]{:S(2)}) collective-permute-start(bf16[256,128]{1,0:T(8,128)(2,1)S(1)} %copy-done), channel_id=1, source_target_pairs={{1,0},{0,1},{3,2},{2,3},{5,4},{4,5},{7,6},{6,7},{9,8},{8,9},{11,10... | collective-permute-start | bytes 196616 | tf_op jit(solution)/shard_map/ppermute | solution.py:171
  6.0 0.4 %collective-permute-start.4 = (bf16[192,128]{1,0:T(8,128)(2,1)S(1)}, bf16[192,128]{1,0:T(8,128)(2,1)S(1)}, u32[]{:S(2)}, u32[]{:S(2)}) collective-permute-start(bf16[192,128]{1,0:T(8,128)(2,1)S(1)} %pad_maximum_fusion.1), channel_id=1, source_target_pairs={{3,0},{2,1},{1,2},{0,3},{7,4},{6,5},{5,6},{4,7},{11,8},{10,9},{9,1... | collective-permute-start | bytes 147464 | tf_op jit(solution)/shard_map/ppermute | solution.py:171
  6.4 0.0 collective-permute-start.3
  6.4 0.0 copy-start.2
  6.4 1.6 %bands.1 = (bf16[512,256]{1,0:T(8,128)(2,1)S(1)}, bf16[4,128,256]{2,1,0:T(8,128)(2,1)S(1)}, bf16[4,256,256]{2,1,0:T(8,128)(2,1)S(1)}, f32[4,8,128]{2,1,0:T(8,128)S(1)}) custom-call(s32[2,4]{1,0:T(2,128)} %bitcast.2, s32[4]{0:T(128)} %bitcast.3, f32[4]{0:T(128)} %rates.1, bf16[4,63]{1,0:T(4,128)(2,1)} %row_taps.1, bf16[4,63]{1,0:T(4,128)(2,1)} %col_taps.1), custom_call_target="tpu_custom_call" | custom-call | flops 100000000 | bytes 1000000 | tf_op jit(solution)/shard_map/bands/pallas_call | solution.py:213
  8.0 0.0 collective-permute-done.2.refs_3_
  8.0 0.5 %collective-permute-done.1.refs_2_ = bf16[192,128]{1,0:T(8,128)(2,1)S(1)} collective-permute-done((bf16[192,128]{1,0:T(8,128)(2,1)S(1)}, bf16[192,128]{1,0:T(8,128)(2,1)S(1)}, u32[]{:S(2)}, u32[]{:S(2)}) %collective-permute-start.1) | collective-permute-done | bytes 49184 | tf_op jit(solution)/shard_map/ppermute | solution.py:171
  8.5 1.6 %collective-permute-done.4.refs_5_ = bf16[192,128]{1,0:T(8,128)(2,1)S(1)} collective-permute-done((bf16[192,128]{1,0:T(8,128)(2,1)S(1)}, bf16[192,128]{1,0:T(8,128)(2,1)S(1)}, u32[]{:S(2)}, u32[]{:S(2)}) %collective-permute-start.4) | collective-permute-done | bytes 49184 | tf_op jit(solution)/shard_map/ppermute | solution.py:171
  10.1 0.0 collective-permute-done.3.refs_4_
  10.1 0.0 collective-permute-done.refs_1_
  10.1 0.0 copy-done.2
  10.1 1.9 %step.1 = bf16[256,128]{1,0:T(8,128)(2,1)} custom-call(f32[4,8,128]{2,1,0:T(8,128)S(1)} %get-tuple-element.9.rates, bf16[512,256]{1,0:T(8,128)(2,1)S(1)} %get-tuple-element.10.fwd, bf16[4,128,256]{2,1,0:T(8,128)(2,1)S(1)} %get-tuple-element.11.adj, bf16[4,256,256]{2,1,0:T(8,128)(2,1)S(1)} %get-tuple-element.12.col, bf16[256,128]{1,0:T(8,128)(2,1)S(1)} %copy-done, ...), custom_call_target="tpu_custom_call" | custom-call | flops 1000000000 | bytes 1000000 | tf_op jit(solution)/shard_map/step/pallas_call | solution.py:234
  (4 shorter events, 0.0 us)
Async XLA Ops:
  0.0 0.8 %copy-start = (bf16[256,128]{1,0:T(8,128)(2,1)S(1)}, bf16[256,128]{1,0:T(8,128)(2,1)}, u32[]{:S(2)}) copy-start(bf16[256,128]{1,0:T(8,128)(2,1)} %refs_0_.1) | copy-start | bytes 196612
  0.0 0.9 %copy-start.1 = (bf16[256,256]{1,0:T(8,128)(2,1)S(1)}, bf16[256,256]{1,0:T(8,128)(2,1)}, u32[]{:S(2)}) copy-start(bf16[256,256]{1,0:T(8,128)(2,1)} %refs_6_.1) | copy-start | bytes 393220
  1.0 7.1 %collective-permute-start.2 = (bf16[192,128]{1,0:T(8,128)(2,1)S(1)}, bf16[192,128]{1,0:T(8,128)(2,1)S(1)}, u32[]{:S(2)}, u32[]{:S(2)}) collective-permute-start(bf16[192,128]{1,0:T(8,128)(2,1)S(1)} %pad_maximum_fusion), channel_id=1, source_target_pairs={{1,0},{0,1},{5,2},{4,3},{3,4},{2,5},{9,6},{8,7},{7,8},{6,9},{13,10... | collective-permute-start | bytes 147464 | tf_op jit(solution)/shard_map/ppermute | solution.py:171
  4.0 4.5 %collective-permute-start.1 = (bf16[192,128]{1,0:T(8,128)(2,1)S(1)}, bf16[192,128]{1,0:T(8,128)(2,1)S(1)}, u32[]{:S(2)}, u32[]{:S(2)}) collective-permute-start(bf16[192,128]{1,0:T(8,128)(2,1)S(1)} %pad_maximum_fusion), channel_id=1, source_target_pairs={{1,0},{0,1},{4,2},{5,3},{2,4},{3,5},{8,6},{9,7},{6,8},{7,9},{12,10... | collective-permute-start | bytes 147464 | tf_op jit(solution)/shard_map/ppermute | solution.py:171
  4.1 6.0 %collective-permute-start = (bf16[256,128]{1,0:T(8,128)(2,1)S(1)}, bf16[256,128]{1,0:T(8,128)(2,1)S(1)}, u32[]{:S(2)}, u32[]{:S(2)}) collective-permute-start(bf16[256,128]{1,0:T(8,128)(2,1)S(1)} %copy-done), channel_id=1, source_target_pairs={{1,0},{0,1},{3,2},{2,3},{5,4},{4,5},{7,6},{6,7},{9,8},{8,9},{11,10... | collective-permute-start | bytes 196616 | tf_op jit(solution)/shard_map/ppermute | solution.py:171
  6.0 4.1 %collective-permute-start.4 = (bf16[192,128]{1,0:T(8,128)(2,1)S(1)}, bf16[192,128]{1,0:T(8,128)(2,1)S(1)}, u32[]{:S(2)}, u32[]{:S(2)}) collective-permute-start(bf16[192,128]{1,0:T(8,128)(2,1)S(1)} %pad_maximum_fusion.1), channel_id=1, source_target_pairs={{3,0},{2,1},{1,2},{0,3},{7,4},{6,5},{5,6},{4,7},{11,8},{10,9},{9,1... | collective-permute-start | bytes 147464 | tf_op jit(solution)/shard_map/ppermute | solution.py:171
  6.4 3.7 %collective-permute-start.3 = (bf16[192,128]{1,0:T(8,128)(2,1)S(1)}, bf16[192,128]{1,0:T(8,128)(2,1)S(1)}, u32[]{:S(2)}, u32[]{:S(2)}) collective-permute-start(bf16[192,128]{1,0:T(8,128)(2,1)S(1)} %pad_maximum_fusion.1), channel_id=1, source_target_pairs={{2,0},{3,1},{0,2},{1,3},{6,4},{7,5},{4,6},{5,7},{10,8},{11,9},{8,1... | collective-permute-start | bytes 147464 | tf_op jit(solution)/shard_map/ppermute | solution.py:171
  6.4 3.7 %copy-start.2 = (s32[256,128]{1,0:T(8,128)S(1)}, s32[256,128]{1,0:T(8,128)}, u32[]{:S(2)}) copy-start(s32[256,128]{1,0:T(8,128)} %refs_7_.1) | copy-start | bytes 393220

commit v4 on v3

--- a/solution.py
+++ b/solution.py
@@ -60,9 +60,33 @@
                 col_ref[s, j * BLOCK : (j + 1) * BLOCK, y * BLOCK : (y + 1) * BLOCK] = piece
 
 
+def pack_kernel(dwell, target, inner_own, outer_own, outer_side, inner_side, sems):
+    tile = dwell.shape[0]
+    odd = lax.rem(lax.axis_index("space"), 2)
+    own = pl.ds(pl.multiple_of(lax.axis_index("scen") * BLOCK, BLOCK), BLOCK)
+    copies = []
+    pairs = ((outer_own, odd), (outer_side, odd), (inner_own, 1 - odd), (inner_side, 1 - odd))
+    for out, low in pairs:
+        dwell_rows = pl.ds(pl.multiple_of(low * (tile - BLOCK), BLOCK), BLOCK)
+        target_rows = pl.ds(pl.multiple_of(low * (tile - HALF), HALF), HALF)
+        copies.append((dwell.at[dwell_rows, :], out.at[pl.ds(0, BLOCK), :]))
+        copies.append((target.at[target_rows, own], out.at[pl.ds(BLOCK, HALF), :]))
+    copies = [pltpu.make_async_copy(a, b, sems.at[i]) for i, (a, b) in enumerate(copies)]
+    for copy in copies:
+        copy.start()
+    for copy in copies:
+        copy.wait()
+
+
 def step_kernel(blocks, rates, fwd, adj, col, *refs):
-    mids, outers = refs[:blocks], refs[blocks : 2 * blocks]
-    inners = refs[2 * blocks : 3 * blocks]
+    groups, at = {}, 1
+    mids = refs[:1]
+    for name, count in (("S", blocks - 1), ("F", blocks - 1), ("P", blocks - 1), ("O", 1), ("E", 1)):
+        groups[name] = refs[at : at + count]
+        at += count
+    mids = mids + groups["S"]
+    outers = groups["O"] + groups["P"]
+    inners = groups["E"] + groups["F"]
     target, bound, out, dwell_all, target_all, fwd_all, back_all = refs[3 * blocks :]
     scen_total = adj.shape[0]
     tile = out.shape[0]
@@ -184,30 +208,26 @@
 
         return partner
 
-    odd = lax.rem(space, 2)
-
-    def edge(x, low, count):
-        return lax.dynamic_slice_in_dim(x, low * (tile - count), count, 0)
 
     window = [0] + sides
-    columns = [lax.rem(scen + n_scen + c, n_scen) * BLOCK for c in window]
+    hbm = pl.BlockSpec(memory_space=pltpu.HBM)
+    inner_own, outer_own, outer_side, inner_side = pl.pallas_call(
+        pack_kernel,
+        out_shape=(
+            pltpu.VMEM((BLOCK + HALF, BLOCK), BF16),
+            pltpu.VMEM((BLOCK + HALF, BLOCK), BF16),
+            pltpu.VMEM((BLOCK + HALF, BLOCK), BF16),
+            pltpu.VMEM((BLOCK + HALF, BLOCK), BF16),
+        ),
+        in_specs=[hbm] * 2,
+        out_specs=(vmem,) * 4,
+        scratch_shapes=[pltpu.SemaphoreType.DMA((8,))],
+        cost_estimate=pl.CostEstimate(flops=1000, bytes_accessed=10**6, transcendentals=0),
+        name="pack",
+    )(dwell_map, target_map)
     mids = [dwell_map] + [moved(dwell_map, side(c)) for c in sides]
-    to_outer = jnp.concatenate(
-        [
-            edge(dwell_map, odd, BLOCK),
-            lax.dynamic_slice(target_map, (odd * (tile - HALF), columns[0]), (HALF, BLOCK)),
-        ],
-        axis=0,
-    )
-    outers = [moved(to_outer, outer(c)) for c in window]
-    to_inner = jnp.concatenate(
-        [
-            edge(dwell_map, 1 - odd, BLOCK),
-            lax.dynamic_slice(target_map, ((1 - odd) * (tile - HALF), columns[0]), (HALF, BLOCK)),
-        ],
-        axis=0,
-    )
-    inners = [moved(to_inner, inner(c)) for c in window]
+    outers = [moved(outer_side if c else outer_own, outer(c)) for c in window]
+    inners = [moved(inner_side if c else inner_own, inner(c)) for c in window]
 
     levels = rate_index.reshape(scen_total)
     fwd, adj, col, rates = pl.pallas_call(
@@ -245,7 +265,7 @@
         compiler_params=pltpu.CompilerParams(vmem_limit_bytes=48 * 1024 * 1024),
         cost_estimate=pl.CostEstimate(flops=10**9, bytes_accessed=10**6, transcendentals=0),
         name="step",
-    )(rates, fwd, adj, col, *mids, *outers, *inners, target, bound_mask)
+    )(rates, fwd, adj, col, mids[0], *mids[1:], *inners[1:], *outers[1:], outers[0], inners[0], target, bound_mask)
 
 
 def solution(mesh):

time: 12.1 us -> 11.6 us (0.959)
  the two profiles are of different devices: /device:TPU:0 before, /device:TPU:8 now
where the time goes in v4:
time: 11.6 us; the launch traced here: 11.4 us
  starting transfers between devices  4.9 us (42%)
  Pallas kernels  4.41 us (38%)
  waiting for transfers between devices  2.03 us (17%)
    ppermute x5, starting transfers between devices, moved(): return lax.ppermute(x, ('space', 'scen'), pairs)  4.9 us
    ppermute x5, waiting for transfers between devices, moved(): return lax.ppermute(x, ('space', 'scen'), pairs)  2.03 us
    pallas_call x1, Pallas kernels, shards(): pl.pallas_call(functools.partial(step_kernel, blocks), out_shape=jax.Shap...  1.87 us
    pallas_call x1, Pallas kernels, shards(): pl.pallas_call(bands_kernel, out_shape=(pltpu.VMEM((scen_total * BLOCK, 2...  1.6 us
    pallas_call x1, Pallas kernels, shards(): pl.pallas_call(pack_kernel, out_shape=(pltpu.VMEM((BLOCK + HALF, BLOCK),...  0.94 us
  transfers between devices with their start and end apart: 5, of which 2 were waited for; matrix products, arithmetic and copies ran while one was open for 0% of the time, Pallas kernels for 22%

profile of v4, /device:TPU:8, one launch (start us, length us, event | category | flops | bytes accessed | tf_op | source)
XLA Modules:
  0.0 11.4 jit_solution(17525324945839295378)
XLA Ops:
  0.0 1.5 %collective-permute-start = (bf16[256,128]{1,0:T(8,128)(2,1)}, bf16[256,128]{1,0:T(8,128)(2,1)S(1)}, u32[]{:S(2)}, u32[]{:S(2)}) collective-permute-start(bf16[256,128]{1,0:T(8,128)(2,1)} %refs_0_.1), channel_id=1, source_target_pairs={{1,0},{0,1},{3,2},{2,3},{5,4},{4,5},{7,6},{6,7},{9,8},{8,9},{11,10... | collective-permute-start | bytes 196616 | tf_op jit(solution)/shard_map/ppermute | solution.py:195
  1.5 0.9 %pack.1 = (bf16[192,128]{1,0:T(8,128)(2,1)S(1)}, bf16[192,128]{1,0:T(8,128)(2,1)S(1)}, bf16[192,128]{1,0:T(8,128)(2,1)S(1)}, bf16[192,128]{1,0:T(8,128)(2,1)S(1)}) custom-call(bf16[256,128]{1,0:T(8,128)(2,1)} %refs_0_.1, bf16[256,256]{1,0:T(8,128)(2,1)} %refs_6_.1), custom_call_target="tpu_custom_call" | custom-call | flops 1000 | bytes 1000000 | tf_op jit(solution)/shard_map/pack/pallas_call | solution.py:214
  2.5 0.1 collective-permute-start.1
  2.5 2.5 %collective-permute-start.2 = (bf16[192,128]{1,0:T(8,128)(2,1)S(1)}, bf16[192,128]{1,0:T(8,128)(2,1)S(1)}, u32[]{:S(2)}, u32[]{:S(2)}) collective-permute-start(bf16[192,128]{1,0:T(8,128)(2,1)S(1)} %get-tuple-element.18), channel_id=1, source_target_pairs={{1,0},{0,1},{5,2},{4,3},{3,4},{2,5},{9,6},{8,7},{7,8},{6,9},{13,10... | collective-permute-start | bytes 147464 | tf_op jit(solution)/shard_map/ppermute | solution.py:195
  5.1 0.7 %collective-permute-start.3 = (bf16[192,128]{1,0:T(8,128)(2,1)S(1)}, bf16[192,128]{1,0:T(8,128)(2,1)S(1)}, u32[]{:S(2)}, u32[]{:S(2)}) collective-permute-start(bf16[192,128]{1,0:T(8,128)(2,1)S(1)} %get-tuple-element.19), channel_id=1, source_target_pairs={{1,0},{0,1},{4,2},{5,3},{2,4},{3,5},{8,6},{9,7},{6,8},{7,9},{12,10... | collective-permute-start | bytes 147464 | tf_op jit(solution)/shard_map/ppermute | solution.py:195
  5.8 0.1 collective-permute-start.4
  5.9 0.0 copy-start
  5.9 0.0 copy-start.1
  5.9 0.0 copy-start.2
  5.9 1.6 %bands.1 = (bf16[512,256]{1,0:T(8,128)(2,1)S(1)}, bf16[4,128,256]{2,1,0:T(8,128)(2,1)S(1)}, bf16[4,256,256]{2,1,0:T(8,128)(2,1)S(1)}, f32[4,8,128]{2,1,0:T(8,128)S(1)}) custom-call(s32[2,4]{1,0:T(2,128)} %bitcast.2, s32[4]{0:T(128)} %bitcast.3, f32[4]{0:T(128)} %rates.1, bf16[4,63]{1,0:T(4,128)(2,1)} %row_taps.1, bf16[4,63]{1,0:T(4,128)(2,1)} %col_taps.1), custom_call_target="tpu_custom_call" | custom-call | flops 100000000 | bytes 1000000 | tf_op jit(solution)/shard_map/bands/pallas_call | solution.py:233
  7.5 0.0 collective-permute-done.1.refs_2_
  7.5 0.5 %collective-permute-done.2.refs_3_ = bf16[192,128]{1,0:T(8,128)(2,1)S(1)} collective-permute-done((bf16[192,128]{1,0:T(8,128)(2,1)S(1)}, bf16[192,128]{1,0:T(8,128)(2,1)S(1)}, u32[]{:S(2)}, u32[]{:S(2)}) %collective-permute-start.2) | collective-permute-done | bytes 49184 | tf_op jit(solution)/shard_map/ppermute | solution.py:195
  8.0 1.5 %collective-permute-done.3.refs_4_ = bf16[192,128]{1,0:T(8,128)(2,1)S(1)} collective-permute-done((bf16[192,128]{1,0:T(8,128)(2,1)S(1)}, bf16[192,128]{1,0:T(8,128)(2,1)S(1)}, u32[]{:S(2)}, u32[]{:S(2)}) %collective-permute-start.3) | collective-permute-done | bytes 49184 | tf_op jit(solution)/shard_map/ppermute | solution.py:195
  9.5 0.0 collective-permute-done.4.refs_5_
  9.5 0.0 collective-permute-done.refs_1_
  9.5 0.0 copy-done
  9.5 0.0 copy-done.1
  9.5 0.0 copy-done.2
  9.5 1.9 %step.1 = bf16[256,128]{1,0:T(8,128)(2,1)} custom-call(f32[4,8,128]{2,1,0:T(8,128)S(1)} %get-tuple-element.13.rates, bf16[512,256]{1,0:T(8,128)(2,1)S(1)} %get-tuple-element.14.fwd, bf16[4,128,256]{2,1,0:T(8,128)(2,1)S(1)} %get-tuple-element.15.adj, bf16[4,256,256]{2,1,0:T(8,128)(2,1)S(1)} %get-tuple-element.16.col, bf16[256,128]{1,0:T(8,128)(2,1)S(1)} %copy-done.1, ...), custom_call_target="tpu_custom_call" | custom-call | flops 1000000000 | bytes 1000000 | tf_op jit(solution)/shard_map/step/pallas_call | solution.py:254
Async XLA Ops:
  0.0 9.5 %collective-permute-start = (bf16[256,128]{1,0:T(8,128)(2,1)}, bf16[256,128]{1,0:T(8,128)(2,1)S(1)}, u32[]{:S(2)}, u32[]{:S(2)}) collective-permute-start(bf16[256,128]{1,0:T(8,128)(2,1)} %refs_0_.1), channel_id=1, source_target_pairs={{1,0},{0,1},{3,2},{2,3},{5,4},{4,5},{7,6},{6,7},{9,8},{8,9},{11,10... | collective-permute-start | bytes 196616 | tf_op jit(solution)/shard_map/ppermute | solution.py:195
  2.5 5.0 %collective-permute-start.1 = (bf16[192,128]{1,0:T(8,128)(2,1)S(1)}, bf16[192,128]{1,0:T(8,128)(2,1)S(1)}, u32[]{:S(2)}, u32[]{:S(2)}) collective-permute-start(bf16[192,128]{1,0:T(8,128)(2,1)S(1)} %get-tuple-element.17), channel_id=1, source_target_pairs={{3,0},{2,1},{1,2},{0,3},{7,4},{6,5},{5,6},{4,7},{11,8},{10,9},{9,1... | collective-permute-start | bytes 147464 | tf_op jit(solution)/shard_map/ppermute | solution.py:195
  2.5 5.5 %collective-permute-start.2 = (bf16[192,128]{1,0:T(8,128)(2,1)S(1)}, bf16[192,128]{1,0:T(8,128)(2,1)S(1)}, u32[]{:S(2)}, u32[]{:S(2)}) collective-permute-start(bf16[192,128]{1,0:T(8,128)(2,1)S(1)} %get-tuple-element.18), channel_id=1, source_target_pairs={{1,0},{0,1},{5,2},{4,3},{3,4},{2,5},{9,6},{8,7},{7,8},{6,9},{13,10... | collective-permute-start | bytes 147464 | tf_op jit(solution)/shard_map/ppermute | solution.py:195
  5.1 4.4 %collective-permute-start.3 = (bf16[192,128]{1,0:T(8,128)(2,1)S(1)}, bf16[192,128]{1,0:T(8,128)(2,1)S(1)}, u32[]{:S(2)}, u32[]{:S(2)}) collective-permute-start(bf16[192,128]{1,0:T(8,128)(2,1)S(1)} %get-tuple-element.19), channel_id=1, source_target_pairs={{1,0},{0,1},{4,2},{5,3},{2,4},{3,5},{8,6},{9,7},{6,8},{7,9},{12,10... | collective-permute-start | bytes 147464 | tf_op jit(solution)/shard_map/ppermute | solution.py:195
  5.8 3.7 %collective-permute-start.4 = (bf16[192,128]{1,0:T(8,128)(2,1)S(1)}, bf16[192,128]{1,0:T(8,128)(2,1)S(1)}, u32[]{:S(2)}, u32[]{:S(2)}) collective-permute-start(bf16[192,128]{1,0:T(8,128)(2,1)S(1)} %get-tuple-element.20), channel_id=1, source_target_pairs={{2,0},{3,1},{0,2},{1,3},{6,4},{7,5},{4,6},{5,7},{10,8},{11,9},{8,1... | collective-permute-start | bytes 147464 | tf_op jit(solution)/shard_map/ppermute | solution.py:195
  5.9 3.7 %copy-start = (bf16[256,256]{1,0:T(8,128)(2,1)S(1)}, bf16[256,256]{1,0:T(8,128)(2,1)}, u32[]{:S(2)}) copy-start(bf16[256,256]{1,0:T(8,128)(2,1)} %refs_6_.1) | copy-start | bytes 393220
  5.9 3.7 %copy-start.1 = (bf16[256,128]{1,0:T(8,128)(2,1)S(1)}, bf16[256,128]{1,0:T(8,128)(2,1)}, u32[]{:S(2)}) copy-start(bf16[256,128]{1,0:T(8,128)(2,1)} %refs_0_.1) | copy-start | bytes 196612
  5.9 3.7 %copy-start.2 = (s32[256,128]{1,0:T(8,128)S(1)}, s32[256,128]{1,0:T(8,128)}, u32[]{:S(2)}) copy-start(s32[256,128]{1,0:T(8,128)} %refs_7_.1) | copy-start | bytes 393220

commit v5 on v1

v5 whole, which is shorter than its diff:
```python
import functools

import jax
import jax.numpy as jnp
from jax import lax
from jax.experimental import pallas as pl
from jax.experimental.pallas import tpu as pltpu
from jax.sharding import PartitionSpec as P

KTAPS = 63
RADIUS = 31
BLOCK = 128
HALF = 64
STEP_SIZE = 1.0
BF16 = jnp.bfloat16
F32 = jnp.float32
SMEM = pl.BlockSpec(memory_space=pltpu.SMEM)
VMEM = pl.BlockSpec(memory_space=pltpu.VMEM)
HBM = pl.BlockSpec(memory_space=pltpu.HBM)


def dot(a, b, contract_b=0):
    return lax.dot_general(
        a, b, (((1,), (contract_b,)), ((), ())), preferred_element_type=F32
    )


def band(taps, start, width):
    line = jnp.concatenate([taps, jnp.zeros((1, width - KTAPS), F32)], axis=1)
    line = pltpu.roll(jnp.broadcast_to(line, (8, width)), start, 1)
    lines = jnp.broadcast_to(line[0:1], (BLOCK, width))
    return pltpu.roll(lines, 0, 1, stride=1, stride_axis=0).astype(BF16)


def bands_kernel(
    offsets, levels, rates, row_taps, col_taps, dwell, target, bound,
    fwd_ref, adj_ref, col_ref, scale_ref, dwell_out, target_out, bound_out, sems,
):
    moves = ((dwell, dwell_out), (target, target_out), (bound, bound_out))
    copies = [pltpu.make_async_copy(a, b, sems.at[i]) for i, (a, b) in enumerate(moves)]
    for copy in copies:
        copy.start()
    scen_total, width = col_ref.shape[0], col_ref.shape[1]
    blocks = width // BLOCK
    scen = lax.axis_index("scen")
    turn = (
        lax.broadcasted_iota(jnp.int32, (KTAPS, KTAPS), 0)
        + lax.broadcasted_iota(jnp.int32, (KTAPS, KTAPS), 1)
        == KTAPS - 1
    )
    turn = turn.astype(F32).astype(BF16)
    rows = row_taps[...].astype(F32)
    rows_turned, cols_turned = dot(row_taps[...], turn), dot(col_taps[...], turn)

    def pick(table, level):
        out = table[0:1]
        for r in range(1, table.shape[0]):
            out = jnp.where(level == r, table[r : r + 1], out)
        return out

    for s in range(scen_total):
        level = levels[s]
        rate = rates[level]
        lanes = slice(s * BLOCK, (s + 1) * BLOCK)
        scale_ref[0:1, lanes] = jnp.full((1, BLOCK), rate * rate * (1.0 / scen_total), F32)
        scale_ref[1:2, lanes] = jnp.full((1, BLOCK), rate * (-1.0 / scen_total), F32)
        shift_row, shift_col = offsets[0, s], offsets[1, s]
        fwd_ref[s] = band(pick(rows, level), HALF - RADIUS - shift_row, 2 * BLOCK)
        adj_ref[s] = band(pick(rows_turned, level), HALF - RADIUS + shift_row, 2 * BLOCK)
        near = band(pick(cols_turned, level), BLOCK - RADIUS + shift_col, 3 * BLOCK)
        for y in range(blocks):
            for j in range(blocks):
                piece = jnp.zeros((BLOCK, BLOCK), BF16)
                if abs(j - y) <= 1:
                    piece = near[:, (j - y + 1) * BLOCK : (j - y + 2) * BLOCK]
                col_ref[s, y * BLOCK : (y + 1) * BLOCK, j * BLOCK : (j + 1) * BLOCK] = piece
    if blocks > 2:
        for outside, j in ((scen == 0, 0), (scen == lax.axis_size("scen") - 1, 2)):

            @pl.when(outside)
            def _():
                for s in range(scen_total):
                    col_ref[s, :, j * BLOCK : (j + 1) * BLOCK] = jnp.zeros((width, BLOCK), BF16)

    for copy in copies:
        copy.wait()


def lanes_of(blocks):
    if blocks == 2:
        own = lax.axis_index("scen") * BLOCK
        return [
            pl.ds(pl.multiple_of(own, BLOCK), BLOCK),
            pl.ds(pl.multiple_of(BLOCK - own, BLOCK), BLOCK),
        ]
    return [pl.ds((blocks - 1) // 2 * BLOCK, BLOCK), pl.ds(0, BLOCK), pl.ds(2 * BLOCK, BLOCK)][:blocks]


def pack_kernel(blocks, *refs):
    mids, (target, tile_ref, to_outer, to_inner) = refs[:blocks], refs[blocks:]
    tile = target.shape[0]
    scen = lax.axis_index("scen")
    odd = lax.rem(lax.axis_index("space"), 2)
    for b, lane in enumerate(lanes_of(blocks)):
        tile_ref[:, lane] = mids[b][...]
    if blocks > 2:
        for outside, b in ((scen == 0, 0), (scen == lax.axis_size("scen") - 1, 2)):

            @pl.when(outside)
            def _():
                tile_ref[:, b * BLOCK : (b + 1) * BLOCK] = jnp.zeros((tile, BLOCK), BF16)

    for out, low in ((to_outer, odd), (to_inner, 1 - odd)):
        out[:BLOCK, :] = tile_ref[pl.ds(pl.multiple_of(low * (tile - BLOCK), BLOCK), BLOCK), :]
        out[BLOCK:, :] = target[pl.ds(pl.multiple_of(low * (tile - HALF), HALF), HALF), :]


def own_kernel(
    blocks, scale, fwd, adj, col, tile_ref, target, dwell,
    partial_ref, fold_ref, own_ref, edge_ref, target_all, rhs,
):
    scen_total, width = col.shape[0], col.shape[1]
    tile = tile_ref.shape[0]
    space = lax.axis_index("space")
    own_rows = lanes_of(blocks)[0]
    target_all[:HALF, :] = jnp.zeros((HALF, width), BF16)
    target_all[HALF : HALF + tile, :] = target[...]
    target_all[HALF + tile :, :] = jnp.zeros((HALF, width), BF16)
    for s in range(scen_total):
        here = slice(s * BLOCK, (s + 1) * BLOCK)
        mine = col[s, own_rows, :]
        own_ref[here, :] = mine
        fold_ref[:, here] = dot(col[s], mine, 1).astype(BF16)
    from_dwell = (dot(tile_ref[...], fold_ref[...]) * scale[0:1, :]).astype(BF16)
    from_target = (dot(target_all[...], own_ref[...], 1) * scale[1:2, :]).astype(BF16)
    lane = lax.broadcasted_iota(jnp.int32, (BLOCK, 2 * BLOCK), 1)
    cuts = (
        (space == 0) & (lane < HALF),
        (space == lax.axis_size("space") - 1) & (lane >= 2 * BLOCK - HALF),
    )
    for b in range(2):
        lhs = []
        for s in range(scen_total):
            here = slice(s * BLOCK, (s + 1) * BLOCK)
            back = jnp.where(cuts[b], jnp.zeros((BLOCK, 2 * BLOCK), BF16), adj[s])
            upper, lower = dot(back[:, :BLOCK], fwd[s]), dot(back[:, BLOCK:], fwd[s])
            both = [
                upper[:, :BLOCK].astype(BF16),
                (upper[:, BLOCK:] + lower[:, :BLOCK]).astype(BF16),
                lower[:, BLOCK:].astype(BF16),
            ]
            at = 2 * s * BLOCK
            edge_ref[b, :, at : at + BLOCK] = both[2 * b]
            edge_ref[b, :, at + BLOCK : at + 2 * BLOCK] = back[:, b * BLOCK : (b + 1) * BLOCK]
            lhs += [both[1 - b], both[2 - b], back]
            at = 4 * s * BLOCK
            rhs[at : at + tile, :] = from_dwell[:, here]
            rhs[at + tile : at + tile + 2 * BLOCK, :] = from_target[b * BLOCK : (b + 2) * BLOCK, here]
        gradient = dot(jnp.concatenate(lhs, axis=1), rhs[...])
        half = slice(b * BLOCK, (b + 1) * BLOCK)
        partial_ref[half, :] = dwell[half, :].astype(F32) - STEP_SIZE * gradient


def halo_kernel(scale, fold, own, edge, partial, bound, outer, inner, out, dwell_halo, target_halo):
    width = outer.shape[1]
    scen_total = own.shape[0] // BLOCK
    space = lax.axis_index("space")
    odd = lax.rem(space, 2)
    outer_rows = pl.ds(pl.multiple_of(odd * BLOCK, BLOCK), BLOCK)
    inner_rows = pl.ds(pl.multiple_of((1 - odd) * BLOCK, BLOCK), BLOCK)
    outer_goal = pl.ds(pl.multiple_of(odd * (BLOCK + HALF), HALF), HALF)
    inner_goal = pl.ds(pl.multiple_of((1 - odd) * (BLOCK + HALF), HALF), HALF)
    dwell_halo[inner_rows, :] = inner[:BLOCK, :]
    dwell_halo[outer_rows, :] = outer[:BLOCK, :]
    target_halo[HALF : HALF + BLOCK, :] = jnp.zeros((BLOCK, width), BF16)
    target_halo[inner_goal, :] = inner[BLOCK:, :]
    target_halo[outer_goal, :] = outer[BLOCK:, :]

    @pl.when((space == 0) | (space == lax.axis_size("space") - 1))
    def _():
        dwell_halo[outer_rows, :] = jnp.zeros((BLOCK, width), BF16)
        target_halo[outer_goal, :] = jnp.zeros((HALF, width), BF16)

    from_dwell = (dot(dwell_halo[...], fold[...]) * scale[0:1, :]).astype(BF16)
    from_target = (dot(target_halo[...], own[...], 1) * scale[1:2, :]).astype(BF16)
    for b in range(2):
        half = slice(b * BLOCK, (b + 1) * BLOCK)
        rhs = []
        for s in range(scen_total):
            here = slice(s * BLOCK, (s + 1) * BLOCK)
            rhs += [from_dwell[half, here], from_target[half, here]]
        gradient = dot(edge[b], jnp.concatenate(rhs, axis=0))
        stepped = partial[half, :] - STEP_SIZE * gradient
        out[half, :] = jnp.where(
            bound[half, :] == 1, jnp.maximum(stepped, 0.0), stepped
        ).astype(BF16)


def shards(
    dwell_map, target_map, bound_mask, offsets, rate_index, rate_table, row_kernels, col_kernels
):
    tile = dwell_map.shape[0]
    n_space, n_scen = lax.axis_size("space"), lax.axis_size("scen")
    scen = lax.axis_index("scen")
    scen_total = offsets.shape[0]
    blocks = min(n_scen, 3)
    width = blocks * BLOCK
    sides = {1: [], 2: [1]}.get(n_scen, [-1, 1])

    def moved(x, partner):
        pairs = []
        for i in range(n_space):
            for j in range(n_scen):
                a, b = partner(i, j)
                pairs.append((a * n_scen + b % n_scen, i * n_scen + j))
        return lax.ppermute(x, ("space", "scen"), pairs)

    def side(cols):
        return lambda i, j: (i, j + cols)

    def inner(i, j):
        return i ^ 1, j

    def outer(i, j):
        if i in (0, n_space - 1):
            return i, (j ^ 1 if n_scen % 2 == 0 else j)
        return ((i - 1) ^ 1) + 1, j

    def call(kernel, name, outs, scratch, flops, specs, *args, limit=32 * 1024 * 1024):
        return pl.pallas_call(
            kernel,
            out_shape=outs,
            in_specs=specs,
            out_specs=jax.tree.map(lambda _: VMEM, outs),
            scratch_shapes=scratch,
            compiler_params=pltpu.CompilerParams(vmem_limit_bytes=limit),
            cost_estimate=pl.CostEstimate(
                flops=flops, bytes_accessed=flops // 100, transcendentals=0
            ),
            name=name,
        )(*args)

    if n_scen <= 2:
        target = target_map
    else:
        target = lax.dynamic_slice_in_dim(
            jnp.pad(target_map, ((0, 0), (BLOCK, BLOCK))), scen * BLOCK, width, 1
        )
    neighbours = [moved(dwell_map, side(c)) for c in sides]

    fwd, adj, col, scale, dwell_here, target_here, bound_here = call(
        bands_kernel,
        "bands",
        (
            pltpu.VMEM((scen_total, BLOCK, 2 * BLOCK), BF16),
            pltpu.VMEM((scen_total, BLOCK, 2 * BLOCK), BF16),
            pltpu.VMEM((scen_total, width, width), BF16),
            pltpu.VMEM((8, scen_total * BLOCK), F32),
            pltpu.VMEM(dwell_map.shape, BF16),
            pltpu.VMEM(target.shape, BF16),
            pltpu.VMEM(bound_mask.shape, jnp.int32),
        ),
        [pltpu.SemaphoreType.DMA((3,))],
        10**8,
        [SMEM] * 3 + [VMEM] * 2 + [HBM] * 3,
        offsets.T,
        rate_index.reshape(scen_total),
        rate_table,
        row_kernels,
        col_kernels,
        dwell_map,
        target,
        bound_mask,
        limit=None,
    )
    tile_here, to_outer, to_inner = call(
        functools.partial(pack_kernel, blocks),
        "pack",
        (
            pltpu.VMEM((tile, width), BF16),
            pltpu.VMEM((BLOCK + HALF, width), BF16),
            pltpu.VMEM((BLOCK + HALF, width), BF16),
        ),
        [],
        10**5,
        [VMEM] * (blocks + 1),
        dwell_here,
        *neighbours,
        target_here,
    )
    outer_rows = moved(to_outer, outer)
    inner_rows = moved(to_inner, inner)
    partial, fold, own, edge = call(
        functools.partial(own_kernel, blocks),
        "own",
        (
            pltpu.VMEM((tile, BLOCK), F32),
            pltpu.VMEM((width, scen_total * BLOCK), BF16),
            pltpu.VMEM((scen_total * BLOCK, width), BF16),
            pltpu.VMEM((2, BLOCK, scen_total * 2 * BLOCK), BF16),
        ),
        [
            pltpu.VMEM((tile + 2 * HALF, width), BF16),
            pltpu.VMEM((scen_total * (tile + 2 * BLOCK), BLOCK), BF16),
        ],
        10**9,
        [VMEM] * 7,
        scale,
        fwd,
        adj,
        col,
        tile_here,
        target_here,
        dwell_here,
    )
    return call(
        halo_kernel,
        "halo",
        jax.ShapeDtypeStruct(dwell_map.shape, BF16),
        [pltpu.VMEM((2 * BLOCK, width), BF16), pltpu.VMEM((2 * BLOCK, width), BF16)],
        10**8,
        [VMEM] * 8,
        scale,
        fold,
        own,
        edge,
        partial,
        bound_here,
        outer_rows,
        inner_rows,
    )


def solution(mesh):
    return jax.shard_map(
        shards,
        mesh=mesh,
        in_specs=(
            P("space", "scen"),
            P("space", None),
            P("space", "scen"),
            P(),
            P(),
            P(),
            P(),
            P(),
        ),
        out_specs=P("space", "scen"),
        check_vma=False,
    )
```

time: 25.7 us -> 11.5 us (0.45)
  the two profiles are of different devices: /device:TPU:24 before, /device:TPU:0 now
where the time goes in v5:
time: 11.5 us; the launch traced here: 11.4 us
  starting transfers between devices  5.14 us (45%)
  Pallas kernels  4.87 us (42%)
  waiting for transfers between devices  1.35 us (12%)
    ppermute x3, starting transfers between devices, moved(): return lax.ppermute(x, ('space', 'scen'), pairs)  5.14 us
    pallas_call x4, Pallas kernels, call(): pl.pallas_call(kernel, out_shape=outs, in_specs=specs, out_specs=jax.tree...  4.87 us
    ppermute x3, waiting for transfers between devices, moved(): return lax.ppermute(x, ('space', 'scen'), pairs)  1.35 us
  transfers between devices with their start and end apart: 3, of which 2 were waited for; matrix products, arithmetic and copies ran while one was open for 0% of the time, Pallas kernels for 32%

profile of v5, /device:TPU:0, one launch (start us, length us, event | category | flops | bytes accessed | tf_op | source)
XLA Modules:
  0.0 11.4 jit_solution(1202360304377570271)
XLA Ops:
  0.0 3.0 %collective-permute-start = (bf16[256,128]{1,0:T(8,128)(2,1)}, bf16[256,128]{1,0:T(8,128)(2,1)S(1)}, u32[]{:S(2)}, u32[]{:S(2)}) collective-permute-start(bf16[256,128]{1,0:T(8,128)(2,1)} %dwell.1), channel_id=1, source_target_pairs={{1,0},{0,1},{3,2},{2,3},{5,4},{4,5},{7,6},{6,7},{9,8},{8,9},{11,10... | collective-permute-start | bytes 196616 | tf_op jit(solution)/shard_map/ppermute | solution.py:216
  3.0 2.4 %bands.1 = (bf16[4,128,256]{2,1,0:T(8,128)(2,1)S(1)}, bf16[4,128,256]{2,1,0:T(8,128)(2,1)S(1)}, bf16[4,256,256]{2,1,0:T(8,128)(2,1)S(1)}, f32[8,512]{1,0:T(8,128...) custom-call(s32[2,4]{1,0:T(2,128)} %bitcast.2, s32[4]{0:T(128)} %bitcast.3, ...), custom_call_target="tpu_custom_call" | custom-call | flops 100000000 | bytes 1000000 | tf_op jit(solution)/shard_map/bands/pallas_call | solution.py:230
  5.3 0.1 collective-permute-done.refs_1_
  5.4 0.1 pack.1
  5.5 2.1 %collective-permute-start.1 = (bf16[192,256]{1,0:T(8,128)(2,1)S(1)}, bf16[192,256]{1,0:T(8,128)(2,1)S(1)}, u32[]{:S(2)}, u32[]{:S(2)}) collective-permute-start(bf16[192,256]{1,0:T(8,128)(2,1)S(1)} %get-tuple-element.31), channel_id=1, source_target_pairs={{1,0},{0,1},{4,2},{5,3},{2,4},{3,5},{8,6},{9,7},{6,8},{7,9},{12,10... | collective-permute-start | bytes 294920 | tf_op jit(solution)/shard_map/ppermute | solution.py:216
  7.6 0.1 collective-permute-start.2
  7.7 1.2 %own.1 = (f32[256,128]{1,0:T(8,128)S(1)}, bf16[256,512]{1,0:T(8,128)(2,1)S(1)}, bf16[512,256]{1,0:T(8,128)(2,1)S(1)}, bf16[2,128,1024]{2,1,0:T(8,128)(2,1)S(1)}) custom-call(f32[8,512]{1,0:T(8,128)S(1)} %get-tuple-element.19.scale, bf16[4,128,256]{2,1,0:T(8,128)(2,1)S(1)} %get-tuple-element.20.fwd, bf16[4,128,256]{2,1,0:T(8,128)(2,1)S(1)} %get-tuple-element.21.adj, ...), custom_call_target="tpu_custom_call" | custom-call | flops 1000000000 | bytes 10000000 | tf_op jit(solution)/shard_map/own/pallas_call | solution.py:230
  8.9 1.3 %collective-permute-done.1.outer = bf16[192,256]{1,0:T(8,128)(2,1)S(1)} collective-permute-done((bf16[192,256]{1,0:T(8,128)(2,1)S(1)}, bf16[192,256]{1,0:T(8,128)(2,1)S(1)}, u32[]{:S(2)}, u32[]{:S(2)}) %collective-permute-start.1) | collective-permute-done | bytes 98336 | tf_op jit(solution)/shard_map/ppermute | solution.py:216
  10.2 0.0 collective-permute-done.2.inner
  10.2 1.2 %halo.1 = bf16[256,128]{1,0:T(8,128)(2,1)} custom-call(f32[8,512]{1,0:T(8,128)S(1)} %get-tuple-element.19.scale, bf16[256,512]{1,0:T(8,128)(2,1)S(1)} %get-tuple-element.26.fold, bf16[512,256]{1,0:T(8,128)(2,1)S(1)} %get-tuple-element.27.own, bf16[2,128,1024]{2,1,0:T(8,128)(2,1)S(1)} %get-tuple-element.28.edge, f32[256,128]{1,0:T(8,128)S(1)} %get-tuple-element.29.partial, ...), custom_call_target="tpu_custom_call" | custom-call | flops 100000000 | bytes 1000000 | tf_op jit(solution)/shard_map/halo/pallas_call | solution.py:230
Async XLA Ops:
  0.0 5.4 %collective-permute-start = (bf16[256,128]{1,0:T(8,128)(2,1)}, bf16[256,128]{1,0:T(8,128)(2,1)S(1)}, u32[]{:S(2)}, u32[]{:S(2)}) collective-permute-start(bf16[256,128]{1,0:T(8,128)(2,1)} %dwell.1), channel_id=1, source_target_pairs={{1,0},{0,1},{3,2},{2,3},{5,4},{4,5},{7,6},{6,7},{9,8},{8,9},{11,10... | collective-permute-start | bytes 196616 | tf_op jit(solution)/shard_map/ppermute | solution.py:216
  5.5 4.7 %collective-permute-start.1 = (bf16[192,256]{1,0:T(8,128)(2,1)S(1)}, bf16[192,256]{1,0:T(8,128)(2,1)S(1)}, u32[]{:S(2)}, u32[]{:S(2)}) collective-permute-start(bf16[192,256]{1,0:T(8,128)(2,1)S(1)} %get-tuple-element.31), channel_id=1, source_target_pairs={{1,0},{0,1},{4,2},{5,3},{2,4},{3,5},{8,6},{9,7},{6,8},{7,9},{12,10... | collective-permute-start | bytes 294920 | tf_op jit(solution)/shard_map/ppermute | solution.py:216
  7.6 2.6 %collective-permute-start.2 = (bf16[192,256]{1,0:T(8,128)(2,1)S(1)}, bf16[192,256]{1,0:T(8,128)(2,1)S(1)}, u32[]{:S(2)}, u32[]{:S(2)}) collective-permute-start(bf16[192,256]{1,0:T(8,128)(2,1)S(1)} %get-tuple-element.32), channel_id=1, source_target_pairs={{2,0},{3,1},{0,2},{1,3},{6,4},{7,5},{4,6},{5,7},{10,8},{11,9},{8,1... | collective-permute-start | bytes 294920 | tf_op jit(solution)/shard_map/ppermute | solution.py:216

commit v6 on v5

v6 whole, which is shorter than its diff:
```python
import functools

import jax
import jax.numpy as jnp
from jax import lax
from jax.experimental import pallas as pl
from jax.experimental.pallas import tpu as pltpu
from jax.sharding import PartitionSpec as P

KTAPS = 63
RADIUS = 31
BLOCK = 128
HALF = 64
STEP_SIZE = 1.0
BF16 = jnp.bfloat16
F32 = jnp.float32
SMEM = pl.BlockSpec(memory_space=pltpu.SMEM)
VMEM = pl.BlockSpec(memory_space=pltpu.VMEM)
HBM = pl.BlockSpec(memory_space=pltpu.HBM)


def dot(a, b, contract_b=0):
    return lax.dot_general(
        a, b, (((1,), (contract_b,)), ((), ())), preferred_element_type=F32
    )


def band(taps, start, width):
    line = jnp.concatenate([taps, jnp.zeros((1, width - KTAPS), F32)], axis=1)
    line = pltpu.roll(jnp.broadcast_to(line, (8, width)), start, 1)
    lines = jnp.broadcast_to(line[0:1], (BLOCK, width))
    return pltpu.roll(lines, 0, 1, stride=1, stride_axis=0).astype(BF16)


def bands_kernel(
    offsets, levels, rates, row_taps, col_taps, dwell, target, bound,
    fwd_ref, adj_ref, fold_ref, own_ref, edge_ref, ends_ref, scale_ref, dwell_out, target_out, bound_out,
    col_ref, target_ends, sems,
):
    moves = ((target, target_out), (dwell, dwell_out), (bound, bound_out))
    copies = [pltpu.make_async_copy(a, b, sems.at[i]) for i, (a, b) in enumerate(moves)]
    for copy in copies:
        copy.start()
    scen_total, width = col_ref.shape[0], col_ref.shape[1]
    blocks = width // BLOCK
    scen = lax.axis_index("scen")
    own_rows = lanes_of(blocks)[0]
    turn = (
        lax.broadcasted_iota(jnp.int32, (KTAPS, KTAPS), 0)
        + lax.broadcasted_iota(jnp.int32, (KTAPS, KTAPS), 1)
        == KTAPS - 1
    )
    turn = turn.astype(F32).astype(BF16)
    rows = row_taps[...].astype(F32)
    rows_turned, cols_turned = dot(row_taps[...], turn), dot(col_taps[...], turn)

    def pick(table, level):
        out = table[0:1]
        for r in range(1, table.shape[0]):
            out = jnp.where(level == r, table[r : r + 1], out)
        return out

    for s in range(scen_total):
        level = levels[s]
        rate = rates[level]
        here = slice(s * BLOCK, (s + 1) * BLOCK)
        scale_ref[0:1, here] = jnp.full((1, BLOCK), rate * rate * (1.0 / scen_total), F32)
        scale_ref[1:2, here] = jnp.full((1, BLOCK), rate * (-1.0 / scen_total), F32)
        shift_row, shift_col = offsets[0, s], offsets[1, s]
        fwd = band(pick(rows, level), HALF - RADIUS - shift_row, 2 * BLOCK)
        adj = band(pick(rows_turned, level), HALF - RADIUS + shift_row, 2 * BLOCK)
        fwd_ref[s] = fwd
        adj_ref[s] = adj
        upper, lower = adj[:, :BLOCK], adj[:, BLOCK:]
        at = 2 * s * BLOCK
        edge_ref[0, :, at : at + BLOCK] = dot(upper, fwd[:, :BLOCK]).astype(BF16)
        edge_ref[0, :, at + BLOCK : at + 2 * BLOCK] = upper
        edge_ref[1, :, at : at + BLOCK] = dot(lower, fwd[:, BLOCK:]).astype(BF16)
        edge_ref[1, :, at + BLOCK : at + 2 * BLOCK] = lower
        near = band(pick(cols_turned, level), BLOCK - RADIUS + shift_col, 3 * BLOCK)
        for y in range(blocks):
            for j in range(blocks):
                piece = jnp.zeros((BLOCK, BLOCK), BF16)
                if abs(j - y) <= 1:
                    piece = near[:, (j - y + 1) * BLOCK : (j - y + 2) * BLOCK]
                col_ref[s, y * BLOCK : (y + 1) * BLOCK, j * BLOCK : (j + 1) * BLOCK] = piece
    if blocks > 2:
        for outside, j in ((scen == 0, 0), (scen == lax.axis_size("scen") - 1, 2)):

            @pl.when(outside)
            def _():
                for s in range(scen_total):
                    col_ref[s, :, j * BLOCK : (j + 1) * BLOCK] = jnp.zeros((width, BLOCK), BF16)

    for s in range(scen_total):
        here = slice(s * BLOCK, (s + 1) * BLOCK)
        mine = col_ref[s, own_rows, :]
        own_ref[here, :] = mine
        fold_ref[:, here] = dot(col_ref[s], mine, 1).astype(BF16)
    copies[0].wait()
    tile = target.shape[0]
    target_ends[:HALF, :] = target_out[tile - HALF :, :]
    target_ends[HALF : HALF + BLOCK, :] = jnp.zeros((BLOCK, width), BF16)
    target_ends[HALF + BLOCK :, :] = target_out[:HALF, :]
    ends_ref[...] = (dot(target_ends[...], own_ref[...], 1) * scale_ref[1:2, :]).astype(BF16)
    for copy in copies[1:]:
        copy.wait()


def lanes_of(blocks):
    if blocks == 2:
        own = lax.axis_index("scen") * BLOCK
        return [
            pl.ds(pl.multiple_of(own, BLOCK), BLOCK),
            pl.ds(pl.multiple_of(BLOCK - own, BLOCK), BLOCK),
        ]
    return [pl.ds((blocks - 1) // 2 * BLOCK, BLOCK), pl.ds(0, BLOCK), pl.ds(2 * BLOCK, BLOCK)][:blocks]


def send_kernel(blocks, scale, fold, edge, ends, *refs):
    mids, (from_ref, to_outer, to_inner, tile_ref) = refs[:blocks], refs[blocks:]
    scen_total = fold.shape[1] // BLOCK
    tile = tile_ref.shape[0]
    scen = lax.axis_index("scen")
    odd = lax.rem(lax.axis_index("space"), 2)
    for b, lane in enumerate(lanes_of(blocks)):
        tile_ref[:, lane] = mids[b][...]
    if blocks > 2:
        for outside, b in ((scen == 0, 0), (scen == lax.axis_size("scen") - 1, 2)):

            @pl.when(outside)
            def _():
                tile_ref[:, b * BLOCK : (b + 1) * BLOCK] = jnp.zeros((tile, BLOCK), BF16)

    from_dwell = (dot(tile_ref[...], fold[...]) * scale[0:1, :]).astype(BF16)
    from_ref[...] = from_dwell
    terms = []
    for b, rows in enumerate((slice(tile - BLOCK, tile), slice(0, BLOCK))):
        rhs = []
        for s in range(scen_total):
            here = slice(s * BLOCK, (s + 1) * BLOCK)
            rhs += [from_dwell[rows, here], ends[b * BLOCK : (b + 1) * BLOCK, here]]
        terms.append(dot(edge[b], jnp.concatenate(rhs, axis=0)).astype(BF16))
    to_outer[...] = jnp.where(odd == 1, terms[0], terms[1])
    to_inner[...] = jnp.where(odd == 1, terms[1], terms[0])


def own_kernel(scale, fwd, adj, own, from_dwell, target, dwell, partial_ref, target_all, rhs):
    scen_total, width = fwd.shape[0], own.shape[1]
    tile = target.shape[0]
    space = lax.axis_index("space")
    target_all[:HALF, :] = jnp.zeros((HALF, width), BF16)
    target_all[HALF : HALF + tile, :] = target[...]
    target_all[HALF + tile :, :] = jnp.zeros((HALF, width), BF16)
    from_target = (dot(target_all[...], own[...], 1) * scale[1:2, :]).astype(BF16)
    lane = lax.broadcasted_iota(jnp.int32, (BLOCK, 2 * BLOCK), 1)
    cuts = (
        (space == 0) & (lane < HALF),
        (space == lax.axis_size("space") - 1) & (lane >= 2 * BLOCK - HALF),
    )
    for b in range(2):
        lhs = []
        for s in range(scen_total):
            here = slice(s * BLOCK, (s + 1) * BLOCK)
            back = jnp.where(cuts[b], jnp.zeros((BLOCK, 2 * BLOCK), BF16), adj[s])
            upper, lower = dot(back[:, :BLOCK], fwd[s]), dot(back[:, BLOCK:], fwd[s])
            middle = (upper[:, BLOCK:] + lower[:, :BLOCK]).astype(BF16)
            if b == 0:
                lhs += [middle, lower[:, BLOCK:].astype(BF16), back]
            else:
                lhs += [upper[:, :BLOCK].astype(BF16), middle, back]
            at = 4 * s * BLOCK
            rhs[at : at + tile, :] = from_dwell[:, here]
            rhs[at + tile : at + tile + 2 * BLOCK, :] = from_target[b * BLOCK : (b + 2) * BLOCK, here]
        gradient = dot(jnp.concatenate(lhs, axis=1), rhs[...])
        half = slice(b * BLOCK, (b + 1) * BLOCK)
        partial_ref[half, :] = dwell[half, :].astype(F32) - STEP_SIZE * gradient


def finish_kernel(partial, bound, outer, inner, out):
    space = lax.axis_index("space")
    odd = lax.rem(space, 2)
    end = (space == 0) | (space == lax.axis_size("space") - 1)
    tile = out.shape[0]
    for at, terms in ((odd, outer), (1 - odd, inner)):
        half = pl.ds(pl.multiple_of(at * (tile - BLOCK), BLOCK), BLOCK)
        gradient = terms[...].astype(F32)
        if terms is outer:
            gradient = jnp.where(end, jnp.zeros_like(gradient), gradient)
        stepped = partial[half, :] - STEP_SIZE * gradient
        out[half, :] = jnp.where(
            bound[half, :] == 1, jnp.maximum(stepped, 0.0), stepped
        ).astype(BF16)


def shards(
    dwell_map, target_map, bound_mask, offsets, rate_index, rate_table, row_kernels, col_kernels
):
    tile = dwell_map.shape[0]
    n_space, n_scen = lax.axis_size("space"), lax.axis_size("scen")
    scen = lax.axis_index("scen")
    scen_total = offsets.shape[0]
    blocks = min(n_scen, 3)
    width = blocks * BLOCK
    sides = {1: [], 2: [1]}.get(n_scen, [-1, 1])

    def moved(x, partner):
        pairs = []
        for i in range(n_space):
            for j in range(n_scen):
                a, b = partner(i, j)
                pairs.append((a * n_scen + b % n_scen, i * n_scen + j))
        return lax.ppermute(x, ("space", "scen"), pairs)

    def side(cols):
        return lambda i, j: (i, j + cols)

    def inner(i, j):
        return i ^ 1, j

    def outer(i, j):
        if i in (0, n_space - 1):
            return i, (j ^ 1 if n_scen % 2 == 0 else j)
        return ((i - 1) ^ 1) + 1, j

    def call(kernel, name, outs, scratch, flops, specs, *args, limit=32 * 1024 * 1024):
        return pl.pallas_call(
            kernel,
            out_shape=outs,
            in_specs=specs,
            out_specs=jax.tree.map(lambda _: VMEM, outs),
            scratch_shapes=scratch,
            compiler_params=pltpu.CompilerParams(vmem_limit_bytes=limit),
            cost_estimate=pl.CostEstimate(
                flops=flops, bytes_accessed=flops // 100, transcendentals=0
            ),
            name=name,
        )(*args)

    if n_scen <= 2:
        target = target_map
    else:
        target = lax.dynamic_slice_in_dim(
            jnp.pad(target_map, ((0, 0), (BLOCK, BLOCK))), scen * BLOCK, width, 1
        )
    neighbours = [moved(dwell_map, side(c)) for c in sides]

    wide = scen_total * BLOCK
    (fwd, adj, fold, own, edge, ends, scale, dwell_here, target_here, bound_here) = call(
        bands_kernel,
        "bands",
        (
            pltpu.VMEM((scen_total, BLOCK, 2 * BLOCK), BF16),
            pltpu.VMEM((scen_total, BLOCK, 2 * BLOCK), BF16),
            pltpu.VMEM((width, wide), BF16),
            pltpu.VMEM((wide, width), BF16),
            pltpu.VMEM((2, BLOCK, 2 * wide), BF16),
            pltpu.VMEM((2 * BLOCK, wide), BF16),
            pltpu.VMEM((8, wide), F32),
            pltpu.VMEM(dwell_map.shape, BF16),
            pltpu.VMEM(target.shape, BF16),
            pltpu.VMEM(bound_mask.shape, jnp.int32),
        ),
        [
            pltpu.VMEM((scen_total, width, width), BF16),
            pltpu.VMEM((2 * BLOCK, width), BF16),
            pltpu.SemaphoreType.DMA((3,)),
        ],
        10**8,
        [SMEM] * 3 + [VMEM] * 2 + [HBM] * 3,
        offsets.T,
        rate_index.reshape(scen_total),
        rate_table,
        row_kernels,
        col_kernels,
        dwell_map,
        target,
        bound_mask,
        limit=None,
    )
    from_dwell, to_outer, to_inner = call(
        functools.partial(send_kernel, blocks),
        "send",
        (
            pltpu.VMEM((tile, wide), BF16),
            pltpu.VMEM((BLOCK, BLOCK), BF16),
            pltpu.VMEM((BLOCK, BLOCK), BF16),
        ),
        [pltpu.VMEM((tile, width), BF16)],
        10**8,
        [VMEM] * (blocks + 4),
        scale,
        fold,
        edge,
        ends,
        dwell_here,
        *neighbours,
    )
    outer_terms = moved(to_outer, outer)
    inner_terms = moved(to_inner, inner)
    partial = call(
        own_kernel,
        "own",
        pltpu.VMEM((tile, BLOCK), F32),
        [
            pltpu.VMEM((tile + 2 * HALF, width), BF16),
            pltpu.VMEM((scen_total * (tile + 2 * BLOCK), BLOCK), BF16),
        ],
        10**9,
        [VMEM] * 7,
        scale,
        fwd,
        adj,
        own,
        from_dwell,
        target_here,
        dwell_here,
    )
    return call(
        finish_kernel,
        "finish",
        jax.ShapeDtypeStruct(dwell_map.shape, BF16),
        [],
        10**6,
        [VMEM] * 4,
        partial,
        bound_here,
        outer_terms,
        inner_terms,
    )


def solution(mesh):
    return jax.shard_map(
        shards,
        mesh=mesh,
        in_specs=(
            P("space", "scen"),
            P("space", None),
            P("space", "scen"),
            P(),
            P(),
            P(),
            P(),
            P(),
        ),
        out_specs=P("space", "scen"),
        check_vma=False,
    )
```

time: 11.5 us -> 11.1 us (0.965)
  starting transfers between devices: 5.14 us -> 4.8 us
    ppermute x3, starting transfers between devices: 5.14 us -> 4.8 us  [moved(): return lax.ppermute(x, ('space', 'scen'), pairs)]
  transfers between devices with their start and end apart: 3 -> 3, of which waited for: 2 -> 1; matrix products, arithmetic and copies ran while one was open for 0% -> 0% of each run, Pallas kernels for 32% -> 34%
where the time goes in v6:
time: 11.1 us; the launch traced here: 10.9 us
  Pallas kernels  4.84 us (44%)
  starting transfers between devices  4.8 us (43%)
  waiting for transfers between devices  1.25 us (11%)
    pallas_call x4, Pallas kernels, call(): pl.pallas_call(kernel, out_shape=outs, in_specs=specs, out_specs=jax.tree...  4.84 us
    ppermute x3, starting transfers between devices, moved(): return lax.ppermute(x, ('space', 'scen'), pairs)  4.8 us
    ppermute x3, waiting for transfers between devices, moved(): return lax.ppermute(x, ('space', 'scen'), pairs)  1.25 us
  transfers between devices with their start and end apart: 3, of which 1 were waited for; matrix products, arithmetic and copies ran while one was open for 0% of the time, Pallas kernels for 34%

profile of v6, /device:TPU:0, one launch (start us, length us, event | category | flops | bytes accessed | tf_op | source)
XLA Modules:
  0.0 10.9 jit_solution(15662325184693752290)
XLA Ops:
  0.0 3.0 %collective-permute-start = (bf16[256,128]{1,0:T(8,128)(2,1)}, bf16[256,128]{1,0:T(8,128)(2,1)S(1)}, u32[]{:S(2)}, u32[]{:S(2)}) collective-permute-start(bf16[256,128]{1,0:T(8,128)(2,1)} %dwell.1), channel_id=1, source_target_pairs={{1,0},{0,1},{3,2},{2,3},{5,4},{4,5},{7,6},{6,7},{9,8},{8,9},{11,10... | collective-permute-start | bytes 196616 | tf_op jit(solution)/shard_map/ppermute | solution.py:213
  3.0 2.8 %bands.1 = (bf16[4,128,256]{2,1,0:T(8,128)(2,1)S(1)}, bf16[4,128,256]{2,1,0:T(8,128)(2,1)S(1)}, bf16[256,512]{1,0:T(8,128)(2,1)S(1)}, bf16[512,256]{1,0:T(8,128)...) custom-call(s32[2,4]{1,0:T(2,128)} %bitcast.2, ...), custom_call_target="tpu_custom_call" | custom-call | flops 100000000 | bytes 1000000 | tf_op jit(solution)/shard_map/bands/pallas_call | solution.py:227
  5.8 0.0 collective-permute-done.refs_1_
  5.8 0.5 %send.1 = (bf16[256,512]{1,0:T(8,128)(2,1)S(1)}, bf16[128,128]{1,0:T(8,128)(2,1)S(1)}, bf16[128,128]{1,0:T(8,128)(2,1)S(1)}) custom-call(f32[8,512]{1,0:T(8,128)S(1)} %get-tuple-element.18.scale, bf16[256,512]{1,0:T(8,128)(2,1)S(1)} %get-tuple-element.22.fold, bf16[2,128,1024]{2,1,0:T(8,128)(2,1)S(1)} %get-tuple-element.23.edge, ...), custom_call_target="tpu_custom_call" | custom-call | flops 100000000 | bytes 1000000 | tf_op jit(solution)/shard_map/send/pallas_call | solution.py:227
  6.3 1.7 %collective-permute-start.1 = (bf16[128,128]{1,0:T(8,128)(2,1)S(1)}, bf16[128,128]{1,0:T(8,128)(2,1)S(1)}, u32[]{:S(2)}, u32[]{:S(2)}) collective-permute-start(bf16[128,128]{1,0:T(8,128)(2,1)S(1)} %get-tuple-element.29), channel_id=1, source_target_pairs={{1,0},{0,1},{4,2},{5,3},{2,4},{3,5},{8,6},{9,7},{6,8},{7,9},{12,10... | collective-permute-start | bytes 98312 | tf_op jit(solution)/shard_map/ppermute | solution.py:213
  8.0 0.1 collective-permute-start.2
  8.1 0.9 %own.1.partial = f32[256,128]{1,0:T(8,128)S(1)} custom-call(f32[8,512]{1,0:T(8,128)S(1)} %get-tuple-element.18.scale, bf16[4,128,256]{2,1,0:T(8,128)(2,1)S(1)} %get-tuple-element.19.fwd, bf16[4,128,256]{2,1,0:T(8,128)(2,1)S(1)} %get-tuple-element.20.adj, bf16[512,256]{1,0:T(8,128)(2,1)S(1)} %get-tuple-element.21.own, ...), custom_call_target="tpu_custom_call" | custom-call | flops 1000000000 | bytes 10000000 | tf_op jit(solution)/shard_map/own/pallas_call | solution.py:227
  9.0 1.2 %collective-permute-done.1.outer = bf16[128,128]{1,0:T(8,128)(2,1)S(1)} collective-permute-done((bf16[128,128]{1,0:T(8,128)(2,1)S(1)}, bf16[128,128]{1,0:T(8,128)(2,1)S(1)}, u32[]{:S(2)}, u32[]{:S(2)}) %collective-permute-start.1) | collective-permute-done | bytes 32800 | tf_op jit(solution)/shard_map/ppermute | solution.py:213
  10.3 0.0 collective-permute-done.2.inner
  10.3 0.7 %finish.1 = bf16[256,128]{1,0:T(8,128)(2,1)} custom-call(f32[256,128]{1,0:T(8,128)S(1)} %own.1.partial, s32[256,128]{1,0:T(8,128)S(1)} %get-tuple-element.28.bound, bf16[128,128]{1,0:T(8,128)(2,1)S(1)} %collective-permute-done.1.outer, bf16[128,128]{1,0:T(8,128)(2,1)S(1)} %collective-permute-done.2.inner), custom_call_target="tpu_custom_call" | custom-call | flops 1000000 | bytes 10000 | tf_op jit(solution)/shard_map/finish/pallas_call | solution.py:227
Async XLA Ops:
  0.0 5.8 %collective-permute-start = (bf16[256,128]{1,0:T(8,128)(2,1)}, bf16[256,128]{1,0:T(8,128)(2,1)S(1)}, u32[]{:S(2)}, u32[]{:S(2)}) collective-permute-start(bf16[256,128]{1,0:T(8,128)(2,1)} %dwell.1), channel_id=1, source_target_pairs={{1,0},{0,1},{3,2},{2,3},{5,4},{4,5},{7,6},{6,7},{9,8},{8,9},{11,10... | collective-permute-start | bytes 196616 | tf_op jit(solution)/shard_map/ppermute | solution.py:213
  6.3 4.0 %collective-permute-start.1 = (bf16[128,128]{1,0:T(8,128)(2,1)S(1)}, bf16[128,128]{1,0:T(8,128)(2,1)S(1)}, u32[]{:S(2)}, u32[]{:S(2)}) collective-permute-start(bf16[128,128]{1,0:T(8,128)(2,1)S(1)} %get-tuple-element.29), channel_id=1, source_target_pairs={{1,0},{0,1},{4,2},{5,3},{2,4},{3,5},{8,6},{9,7},{6,8},{7,9},{12,10... | collective-permute-start | bytes 98312 | tf_op jit(solution)/shard_map/ppermute | solution.py:213
  8.0 2.2 %collective-permute-start.2 = (bf16[128,128]{1,0:T(8,128)(2,1)S(1)}, bf16[128,128]{1,0:T(8,128)(2,1)S(1)}, u32[]{:S(2)}, u32[]{:S(2)}) collective-permute-start(bf16[128,128]{1,0:T(8,128)(2,1)S(1)} %get-tuple-element.30), channel_id=1, source_target_pairs={{2,0},{3,1},{0,2},{1,3},{6,4},{7,5},{4,6},{5,7},{10,8},{11,9},{8,1... | collective-permute-start | bytes 98312 | tf_op jit(solution)/shard_map/ppermute | solution.py:213

commit v7 on v6

v7 whole, which is shorter than its diff:
```python
import functools

import jax
import jax.numpy as jnp
from jax import lax
from jax.experimental import pallas as pl
from jax.experimental.pallas import tpu as pltpu
from jax.sharding import PartitionSpec as P

KTAPS = 63
RADIUS = 31
BLOCK = 128
HALF = 64
STEP_SIZE = 1.0
BF16 = jnp.bfloat16
F32 = jnp.float32
SMEM = pl.BlockSpec(memory_space=pltpu.SMEM)
VMEM = pl.BlockSpec(memory_space=pltpu.VMEM)
HBM = pl.BlockSpec(memory_space=pltpu.HBM)


def dot(a, b, contract_b=0):
    return lax.dot_general(
        a, b, (((1,), (contract_b,)), ((), ())), preferred_element_type=F32
    )


def band(line, width):
    lines = jnp.broadcast_to(line[0:1, :width], (BLOCK, width))
    return pltpu.roll(lines, 0, 1, stride=1, stride_axis=0).astype(BF16)


def lanes_of(blocks):
    if blocks == 2:
        own = lax.axis_index("scen") * BLOCK
        return [
            pl.ds(pl.multiple_of(own, BLOCK), BLOCK),
            pl.ds(pl.multiple_of(BLOCK - own, BLOCK), BLOCK),
        ]
    return [pl.ds((blocks - 1) // 2 * BLOCK, BLOCK), pl.ds(0, BLOCK), pl.ds(2 * BLOCK, BLOCK)][:blocks]


def pack_kernel(
    dwell, target, offsets, levels, rates, row_taps, col_taps,
    outer_side, outer_own, lines, scale_ref,
    offsets_here, levels_here, rates_here, rows_here, cols_here, sems,
):
    tile = dwell.shape[0]
    odd = lax.rem(lax.axis_index("space"), 2)
    mine = pl.ds(pl.multiple_of(lax.axis_index("scen") * BLOCK, BLOCK), BLOCK)
    dwell_rows = pl.ds(pl.multiple_of(odd * (tile - BLOCK), BLOCK), BLOCK)
    target_rows = pl.ds(pl.multiple_of(odd * (tile - HALF), HALF), HALF)
    moves = [
        (offsets, offsets_here),
        (levels, levels_here),
        (rates, rates_here),
        (row_taps, rows_here),
        (col_taps, cols_here),
    ]
    for out in (outer_side, outer_own):
        moves.append((dwell.at[dwell_rows, :], out.at[pl.ds(0, BLOCK), :]))
        moves.append((target.at[target_rows, mine], out.at[pl.ds(BLOCK, HALF), :]))
    copies = [pltpu.make_async_copy(a, b, sems.at[i]) for i, (a, b) in enumerate(moves)]
    for copy in copies:
        copy.start()
    turn = (
        lax.broadcasted_iota(jnp.int32, (KTAPS, KTAPS), 0)
        + lax.broadcasted_iota(jnp.int32, (KTAPS, KTAPS), 1)
        == KTAPS - 1
    )
    turn = turn.astype(F32).astype(BF16)
    for copy in copies:
        copy.wait()
    scen_total = lines.shape[0]
    rest = jnp.zeros((rates.shape[0], 3 * BLOCK - KTAPS), F32)
    rows, cols = rows_here[...], cols_here[...]
    tables = [rows.astype(F32), dot(rows, turn), dot(cols, turn)]
    tables = [jnp.concatenate([table, rest], axis=1) for table in tables]
    for s in range(scen_total):
        level = levels_here[s]
        rate = rates_here[level]
        here = slice(s * BLOCK, (s + 1) * BLOCK)
        scale_ref[0:1, here] = jnp.full((1, BLOCK), rate * rate * (1.0 / scen_total), F32)
        scale_ref[1:2, here] = jnp.full((1, BLOCK), rate * (-1.0 / scen_total), F32)
        shift_row, shift_col = offsets_here[0, s], offsets_here[1, s]
        starts = (
            HALF - RADIUS - shift_row,
            HALF - RADIUS + shift_row,
            BLOCK - RADIUS + shift_col,
        )
        for k, (table, start) in enumerate(zip(tables, starts)):
            line = table[0:1]
            for r in range(1, table.shape[0]):
                line = jnp.where(level == r, table[r : r + 1], line)
            lines[s, k] = pltpu.roll(jnp.broadcast_to(line, (8, 3 * BLOCK)), start, 1)


def bands_kernel(lines, fwd_ref, adj_ref, fold_ref, own_ref, edge_ref, col_ref):
    scen_total, width = col_ref.shape[0], col_ref.shape[1]
    blocks = width // BLOCK
    scen = lax.axis_index("scen")
    own_rows = lanes_of(blocks)[0]
    for s in range(scen_total):
        fwd, adj = band(lines[s, 0], 2 * BLOCK), band(lines[s, 1], 2 * BLOCK)
        fwd_ref[s] = fwd
        adj_ref[s] = adj
        upper, lower = adj[:, :BLOCK], adj[:, BLOCK:]
        at = 2 * s * BLOCK
        edge_ref[0, :, at : at + BLOCK] = dot(upper, fwd[:, :BLOCK]).astype(BF16)
        edge_ref[0, :, at + BLOCK : at + 2 * BLOCK] = upper
        edge_ref[1, :, at : at + BLOCK] = dot(lower, fwd[:, BLOCK:]).astype(BF16)
        edge_ref[1, :, at + BLOCK : at + 2 * BLOCK] = lower
        near = band(lines[s, 2], 3 * BLOCK)
        for y in range(blocks):
            for j in range(blocks):
                piece = jnp.zeros((BLOCK, BLOCK), BF16)
                if abs(j - y) <= 1:
                    piece = near[:, (j - y + 1) * BLOCK : (j - y + 2) * BLOCK]
                col_ref[s, y * BLOCK : (y + 1) * BLOCK, j * BLOCK : (j + 1) * BLOCK] = piece
    if blocks > 2:
        for outside, j in ((scen == 0, 0), (scen == lax.axis_size("scen") - 1, 2)):

            @pl.when(outside)
            def _():
                for s in range(scen_total):
                    col_ref[s, :, j * BLOCK : (j + 1) * BLOCK] = jnp.zeros((width, BLOCK), BF16)

    for s in range(scen_total):
        here = slice(s * BLOCK, (s + 1) * BLOCK)
        mine = col_ref[s, own_rows, :]
        own_ref[here, :] = mine
        fold_ref[:, here] = dot(col_ref[s], mine, 1).astype(BF16)


def clear_outside(blocks, ref):
    if blocks > 2:
        scen = lax.axis_index("scen")
        for outside, b in ((scen == 0, 0), (scen == lax.axis_size("scen") - 1, 2)):

            @pl.when(outside)
            def _():
                ref[:, b * BLOCK : (b + 1) * BLOCK] = jnp.zeros((ref.shape[0], BLOCK), BF16)


def terms_of(edge, dwell_rows, target_rows):
    rhs = []
    for s in range(dwell_rows.shape[1] // BLOCK):
        here = slice(s * BLOCK, (s + 1) * BLOCK)
        rhs += [dwell_rows[:, here], target_rows[:, here]]
    return dot(edge, jnp.concatenate(rhs, axis=0))


def send_kernel(blocks, scale, fold, own, edge, target, *refs):
    mids, (from_ref, to_inner, tile_ref, target_ends) = refs[:blocks], refs[blocks:]
    tile = tile_ref.shape[0]
    odd = lax.rem(lax.axis_index("space"), 2)
    for b, lane in enumerate(lanes_of(blocks)):
        tile_ref[:, lane] = mids[b][...]
    clear_outside(blocks, tile_ref)
    from_ref[...] = (dot(tile_ref[...], fold[...]) * scale[0:1, :]).astype(BF16)
    rows = pl.ds(pl.multiple_of((1 - odd) * (tile - HALF), HALF), HALF)
    target_ends[...] = jnp.zeros(target_ends.shape, BF16)
    target_ends[pl.ds(pl.multiple_of(odd * HALF, HALF), HALF), :] = target[rows, :]
    ends = (dot(target_ends[...], own[...], 1) * scale[1:2, :]).astype(BF16)
    rows = pl.ds(pl.multiple_of((1 - odd) * (tile - BLOCK), BLOCK), BLOCK)
    to_inner[...] = terms_of(edge[odd], from_ref[rows, :], ends).astype(BF16)


def own_kernel(scale, fwd, adj, own, from_dwell, target, dwell, partial_ref, target_all, rhs):
    scen_total, width = fwd.shape[0], own.shape[1]
    tile = target.shape[0]
    space = lax.axis_index("space")
    target_all[:HALF, :] = jnp.zeros((HALF, width), BF16)
    target_all[HALF : HALF + tile, :] = target[...]
    target_all[HALF + tile :, :] = jnp.zeros((HALF, width), BF16)
    from_target = (dot(target_all[...], own[...], 1) * scale[1:2, :]).astype(BF16)
    lane = lax.broadcasted_iota(jnp.int32, (BLOCK, 2 * BLOCK), 1)
    cuts = (
        (space == 0) & (lane < HALF),
        (space == lax.axis_size("space") - 1) & (lane >= 2 * BLOCK - HALF),
    )
    for b in range(2):
        lhs = []
        for s in range(scen_total):
            here = slice(s * BLOCK, (s + 1) * BLOCK)
            back = jnp.where(cuts[b], jnp.zeros((BLOCK, 2 * BLOCK), BF16), adj[s])
            upper, lower = dot(back[:, :BLOCK], fwd[s]), dot(back[:, BLOCK:], fwd[s])
            middle = (upper[:, BLOCK:] + lower[:, :BLOCK]).astype(BF16)
            if b == 0:
                lhs += [middle, lower[:, BLOCK:].astype(BF16), back]
            else:
                lhs += [upper[:, :BLOCK].astype(BF16), middle, back]
            at = 4 * s * BLOCK
            rhs[at : at + tile, :] = from_dwell[:, here]
            rhs[at + tile : at + tile + 2 * BLOCK, :] = from_target[b * BLOCK : (b + 2) * BLOCK, here]
        gradient = dot(jnp.concatenate(lhs, axis=1), rhs[...])
        half = slice(b * BLOCK, (b + 1) * BLOCK)
        partial_ref[half, :] = dwell[half, :].astype(F32) - STEP_SIZE * gradient


def finish_kernel(blocks, scale, fold, own, edge, partial, bound, inner, *refs):
    halos, (out, dwell_halo, target_halo) = refs[blocks - 1 : blocks] + refs[: blocks - 1], refs[blocks:]
    tile, width = out.shape[0], own.shape[1]
    space = lax.axis_index("space")
    odd = lax.rem(space, 2)
    goal_rows = pl.ds(pl.multiple_of(odd * HALF, HALF), HALF)
    target_halo[...] = jnp.zeros((BLOCK, width), BF16)
    for b, lane in enumerate(lanes_of(blocks)):
        dwell_halo[:, lane] = halos[b][:BLOCK, :]
        target_halo[goal_rows, lane] = halos[b][BLOCK:, :]
    clear_outside(blocks, dwell_halo)
    clear_outside(blocks, target_halo)
    from_dwell = (dot(dwell_halo[...], fold[...]) * scale[0:1, :]).astype(BF16)
    from_target = (dot(target_halo[...], own[...], 1) * scale[1:2, :]).astype(BF16)
    terms = terms_of(edge[odd], from_dwell, from_target)
    end = (space == 0) | (space == lax.axis_size("space") - 1)
    terms = jnp.where(end, jnp.zeros_like(terms), terms)
    for at, gradient in ((odd, terms), (1 - odd, inner[...].astype(F32))):
        half = pl.ds(pl.multiple_of(at * (tile - BLOCK), BLOCK), BLOCK)
        stepped = partial[half, :] - STEP_SIZE * gradient
        out[half, :] = jnp.where(
            bound[half, :] == 1, jnp.maximum(stepped, 0.0), stepped
        ).astype(BF16)


def shards(
    dwell_map, target_map, bound_mask, offsets, rate_index, rate_table, row_kernels, col_kernels
):
    tile = dwell_map.shape[0]
    n_space, n_scen = lax.axis_size("space"), lax.axis_size("scen")
    scen = lax.axis_index("scen")
    scen_total = offsets.shape[0]
    blocks = min(n_scen, 3)
    width = blocks * BLOCK
    sides = {1: [], 2: [1]}.get(n_scen, [-1, 1])

    def moved(x, partner):
        pairs = []
        for i in range(n_space):
            for j in range(n_scen):
                a, b = partner(i, j)
                pairs.append((a * n_scen + b % n_scen, i * n_scen + j))
        return lax.ppermute(x, ("space", "scen"), pairs)

    def side(cols):
        return lambda i, j: (i, j + cols)

    def inner(i, j):
        return i ^ 1, j

    def outer(cols):
        def partner(i, j):
            if i in (0, n_space - 1):
                return i, (j ^ 1 if n_scen % 2 == 0 else j)
            return ((i - 1) ^ 1) + 1, j + cols

        return partner

    def call(kernel, name, outs, scratch, flops, specs, *args, limit=32 * 1024 * 1024):
        return pl.pallas_call(
            kernel,
            out_shape=outs,
            in_specs=specs,
            out_specs=jax.tree.map(lambda _: VMEM, outs),
            scratch_shapes=scratch,
            compiler_params=pltpu.CompilerParams(vmem_limit_bytes=limit),
            cost_estimate=pl.CostEstimate(
                flops=flops, bytes_accessed=flops // 100, transcendentals=0
            ),
            name=name,
        )(*args)

    if n_scen <= 2:
        target = target_map
    else:
        target = lax.dynamic_slice_in_dim(
            jnp.pad(target_map, ((0, 0), (BLOCK, BLOCK))), scen * BLOCK, width, 1
        )
    neighbours = [moved(dwell_map, side(c)) for c in sides]
    wide = scen_total * BLOCK
    rates = rate_table.shape[0]
    outer_side, outer_own, lines, scale = call(
        pack_kernel,
        "pack",
        (
            pltpu.VMEM((BLOCK + HALF, BLOCK), BF16),
            pltpu.VMEM((BLOCK + HALF, BLOCK), BF16),
            pltpu.VMEM((scen_total, 3, 8, 3 * BLOCK), F32),
            pltpu.VMEM((8, wide), F32),
        ),
        [
            pltpu.SMEM((2, scen_total), jnp.int32),
            pltpu.SMEM((scen_total,), jnp.int32),
            pltpu.SMEM((rates,), F32),
            pltpu.VMEM((rates, KTAPS), BF16),
            pltpu.VMEM((rates, KTAPS), BF16),
            pltpu.SemaphoreType.DMA((9,)),
        ],
        10**5,
        [HBM] * 7,
        dwell_map,
        target_map,
        offsets.T,
        rate_index.reshape(scen_total),
        rate_table,
        row_kernels,
        col_kernels,
        limit=None,
    )
    fwd, adj, fold, own, edge = call(
        bands_kernel,
        "bands",
        (
            pltpu.VMEM((scen_total, BLOCK, 2 * BLOCK), BF16),
            pltpu.VMEM((scen_total, BLOCK, 2 * BLOCK), BF16),
            pltpu.VMEM((width, wide), BF16),
            pltpu.VMEM((wide, width), BF16),
            pltpu.VMEM((2, BLOCK, 2 * wide), BF16),
        ),
        [pltpu.VMEM((scen_total, width, width), BF16)],
        10**8,
        [VMEM],
        lines,
    )
    halos = [moved(outer_side if c else outer_own, outer(c)) for c in [0] + sides]
    from_dwell, to_inner = call(
        functools.partial(send_kernel, blocks),
        "send",
        (pltpu.VMEM((tile, wide), BF16), pltpu.VMEM((BLOCK, BLOCK), BF16)),
        [pltpu.VMEM((tile, width), BF16), pltpu.VMEM((BLOCK, width), BF16)],
        10**8,
        [VMEM] * (blocks + 5),
        scale,
        fold,
        own,
        edge,
        target,
        dwell_map,
        *neighbours,
    )
    inner_terms = moved(to_inner, inner)
    partial = call(
        own_kernel,
        "own",
        pltpu.VMEM((tile, BLOCK), F32),
        [
            pltpu.VMEM((tile + 2 * HALF, width), BF16),
            pltpu.VMEM((scen_total * (tile + 2 * BLOCK), BLOCK), BF16),
        ],
        10**9,
        [VMEM] * 7,
        scale,
        fwd,
        adj,
        own,
        from_dwell,
        target,
        dwell_map,
    )
    return call(
        functools.partial(finish_kernel, blocks),
        "finish",
        jax.ShapeDtypeStruct(dwell_map.shape, BF16),
        [pltpu.VMEM((BLOCK, width), BF16), pltpu.VMEM((BLOCK, width), BF16)],
        10**6,
        [VMEM] * (7 + blocks),
        scale,
        fold,
        own,
        edge,
        partial,
        bound_mask,
        inner_terms,
        *halos[1:],
        halos[0],
    )


def solution(mesh):
    return jax.shard_map(
        shards,
        mesh=mesh,
        in_specs=(
            P("space", "scen"),
            P("space", None),
            P("space", "scen"),
            P(),
            P(),
            P(),
            P(),
            P(),
        ),
        out_specs=P("space", "scen"),
        check_vma=False,
    )
```

time: 11.1 us -> 10.6 us (0.955)
  Pallas kernels: 4.84 us -> 4.28 us
  waiting for transfers between devices: 1.25 us -> 0.74 us
  starting transfers between devices: 4.8 us -> 5.12 us
  local copies, waits for them, and re-layouts: 0 us -> 0.22 us
    pallas_call x4 -> x5, Pallas kernels: 4.84 us -> 4.28 us  [call(): pl.pallas_call(kernel, out_shape=outs, in_specs=specs, out_specs=jax.tree...]
    ppermute x3 -> x4, waiting for transfers between devices: 1.25 us -> 0.74 us  [moved(): return lax.ppermute(x, ('space', 'scen'), pairs)]
    ppermute x3 -> x4, starting transfers between devices: 4.8 us -> 5.12 us  [moved(): return lax.ppermute(x, ('space', 'scen'), pairs)]
    unnamed x0 -> x6, local copies, waits for them, and re-layouts: none -> 0.22 us
  transfers between devices with their start and end apart: 3 -> 4, of which waited for: 1 -> 2; matrix products, arithmetic and copies ran while one was open for 0% -> 0% of each run, Pallas kernels for 34% -> 26%
where the time goes in v7:
time: 10.6 us; the launch traced here: 10.4 us
  starting transfers between devices  5.12 us (48%)
  Pallas kernels  4.28 us (40%)
  waiting for transfers between devices  0.74 us (7%)
  local copies, waits for them, and re-layouts  0.22 us (2%)
    ppermute x4, starting transfers between devices, moved(): return lax.ppermute(x, ('space', 'scen'), pairs)  5.12 us
    pallas_call x5, Pallas kernels, call(): pl.pallas_call(kernel, out_shape=outs, in_specs=specs, out_specs=jax.tree...  4.28 us
    ppermute x4, waiting for transfers between devices, moved(): return lax.ppermute(x, ('space', 'scen'), pairs)  0.74 us
    unnamed x6, local copies, waits for them, and re-layouts  0.22 us
  transfers between devices with their start and end apart: 4, of which 2 were waited for; matrix products, arithmetic and copies ran while one was open for 0% of the time, Pallas kernels for 26%

profile of v7, /device:TPU:0, one launch (start us, length us, event | category | flops | bytes accessed | tf_op | source)
XLA Modules:
  0.0 10.4 jit_solution(9028703209422933548)
XLA Ops:
  0.0 3.0 %collective-permute-start = (bf16[256,128]{1,0:T(8,128)(2,1)}, bf16[256,128]{1,0:T(8,128)(2,1)S(1)}, u32[]{:S(2)}, u32[]{:S(2)}) collective-permute-start(bf16[256,128]{1,0:T(8,128)(2,1)} %dwell.3), channel_id=1, source_target_pairs={{1,0},{0,1},{3,2},{2,3},{5,4},{4,5},{7,6},{6,7},{9,8},{8,9},{11,10... | collective-permute-start | bytes 196616 | tf_op jit(solution)/shard_map/ppermute | solution.py:243
  3.0 1.1 %pack.1 = (bf16[192,128]{1,0:T(8,128)(2,1)S(1)}, bf16[192,128]{1,0:T(8,128)(2,1)S(1)}, f32[4,3,8,384]{3,2,1,0:T(8,128)S(1)}, f32[8,512]{1,0:T(8,128)S(1)}) custom-call(bf16[256,128]{1,0:T(8,128)(2,1)} %dwell.3, bf16[256,256]{1,0:T(8,128)(2,1)} %target.5, s32[2,4]{1,0:T(2,128)} %bitcast.2, s32[4]{0:T(128)} %bitcast.3, f32[4]{0:T(128)} %rates.1, ...), custom_call_target="tpu_custom_call" | custom-call | flops 100000 | bytes 1000 | tf_op jit(solution)/shard_map/pack/pallas_call | solution.py:260
  4.1 0.1 collective-permute-start.2
  4.2 2.0 %collective-permute-start.3 = (bf16[192,128]{1,0:T(8,128)(2,1)S(1)}, bf16[192,128]{1,0:T(8,128)(2,1)S(1)}, u32[]{:S(2)}, u32[]{:S(2)}) collective-permute-start(bf16[192,128]{1,0:T(8,128)(2,1)S(1)} %get-tuple-element.26), channel_id=1, source_target_pairs={{1,0},{0,1},{4,2},{5,3},{2,4},{3,5},{8,6},{9,7},{6,8},{7,9},{12,10... | collective-permute-start | bytes 147464 | tf_op jit(solution)/shard_map/ppermute | solution.py:243
  6.2 0.0 copy-start
  6.2 0.0 copy-start.1
  6.2 0.7 %bands.1 = (bf16[4,128,256]{2,1,0:T(8,128)(2,1)S(1)}, bf16[4,128,256]{2,1,0:T(8,128)(2,1)S(1)}, bf16[256,512]{1,0:T(8,128)(2,1)S(1)}, bf16[512,256]{1,0:T(8,128)(2,1)S(1)}, bf16[2,128,1024]{2,1,0:T(8,128)(2,1)S(1)}) custom-call(f32[4,3,8,384]{3,2,1,0:T(8,128)S(1)} %get-tuple-element.17.lines), custom_call_target="tpu_custom_call" | custom-call | flops 100000000 | bytes 1000000 | tf_op jit(solution)/shard_map/bands/pallas_call | solution.py:260
  6.9 0.0 collective-permute-done.refs_1_
  6.9 0.2 %copy-done = bf16[256,256]{1,0:T(8,128)(2,1)S(1)} copy-done((bf16[256,256]{1,0:T(8,128)(2,1)S(1)}, bf16[256,256]{1,0:T(8,128)(2,1)}, u32[]{:S(2)}) %copy-start) | copy-done | bytes 131096
  7.1 0.0 copy-done.1
  7.1 0.5 %send.1 = (bf16[256,512]{1,0:T(8,128)(2,1)S(1)}, bf16[128,128]{1,0:T(8,128)(2,1)S(1)}) custom-call(f32[8,512]{1,0:T(8,128)S(1)} %get-tuple-element.16.scale, bf16[256,512]{1,0:T(8,128)(2,1)S(1)} %get-tuple-element.18.fold, bf16[512,256]{1,0:T(8,128)(2,1)S(1)} %get-tuple-element.19.own, bf16[2,128,1024]{2,1,0:T(8,128)(2,1)S(1)} %get-tuple-element.20.edge, ...), custom_call_target="tpu_custom_call" | custom-call | flops 100000000 | bytes 1000000 | tf_op jit(solution)/shard_map/send/pallas_call | solution.py:260
  7.6 0.1 collective-permute-start.1
  7.7 0.0 copy-start.2
  7.7 0.9 %own.1.partial = f32[256,128]{1,0:T(8,128)S(1)} custom-call(f32[8,512]{1,0:T(8,128)S(1)} %get-tuple-element.16.scale, bf16[4,128,256]{2,1,0:T(8,128)(2,1)S(1)} %get-tuple-element.21.fwd, bf16[4,128,256]{2,1,0:T(8,128)(2,1)S(1)} %get-tuple-element.22.adj, bf16[512,256]{1,0:T(8,128)(2,1)S(1)} %get-tuple-element.19.own, ...), custom_call_target="tpu_custom_call" | custom-call | flops 1000000000 | bytes 10000000 | tf_op jit(solution)/shard_map/own/pallas_call | solution.py:260
  8.6 0.2 %collective-permute-done.2.refs_0_ = bf16[192,128]{1,0:T(8,128)(2,1)S(1)} collective-permute-done((bf16[192,128]{1,0:T(8,128)(2,1)S(1)}, bf16[192,128]{1,0:T(8,128)(2,1)S(1)}, u32[]{:S(2)}, u32[]{:S(2)}) %collective-permute-start.2) | collective-permute-done | bytes 49184 | tf_op jit(solution)/shard_map/ppermute | solution.py:243
  8.8 0.5 %collective-permute-done.3.refs_1_ = bf16[192,128]{1,0:T(8,128)(2,1)S(1)} collective-permute-done((bf16[192,128]{1,0:T(8,128)(2,1)S(1)}, bf16[192,128]{1,0:T(8,128)(2,1)S(1)}, u32[]{:S(2)}, u32[]{:S(2)}) %collective-permute-start.3) | collective-permute-done | bytes 49184 | tf_op jit(solution)/shard_map/ppermute | solution.py:243
  9.3 0.0 collective-permute-done.1.inner
  9.3 0.0 copy-done.2
  9.3 1.1 %finish.1 = bf16[256,128]{1,0:T(8,128)(2,1)} custom-call(f32[8,512]{1,0:T(8,128)S(1)} %get-tuple-element.16.scale, bf16[256,512]{1,0:T(8,128)(2,1)S(1)} %get-tuple-element.18.fold, bf16[512,256]{1,0:T(8,128)(2,1)S(1)} %get-tuple-element.19.own, bf16[2,128,1024]{2,1,0:T(8,128)(2,1)S(1)} %get-tuple-element.20.edge, f32[256,128]{1,0:T(8,128)S(1)} %own.1.partial, ...), custom_call_target="tpu_custom_call" | custom-call | flops 1000000 | bytes 10000 | tf_op jit(solution)/shard_map/finish/pallas_call | solution.py:260
Async XLA Ops:
  0.0 6.9 %collective-permute-start = (bf16[256,128]{1,0:T(8,128)(2,1)}, bf16[256,128]{1,0:T(8,128)(2,1)S(1)}, u32[]{:S(2)}, u32[]{:S(2)}) collective-permute-start(bf16[256,128]{1,0:T(8,128)(2,1)} %dwell.3), channel_id=1, source_target_pairs={{1,0},{0,1},{3,2},{2,3},{5,4},{4,5},{7,6},{6,7},{9,8},{8,9},{11,10... | collective-permute-start | bytes 196616 | tf_op jit(solution)/shard_map/ppermute | solution.py:243
  4.1 4.7 %collective-permute-start.2 = (bf16[192,128]{1,0:T(8,128)(2,1)S(1)}, bf16[192,128]{1,0:T(8,128)(2,1)S(1)}, u32[]{:S(2)}, u32[]{:S(2)}) collective-permute-start(bf16[192,128]{1,0:T(8,128)(2,1)S(1)} %get-tuple-element.25), channel_id=1, source_target_pairs={{1,0},{0,1},{5,2},{4,3},{3,4},{2,5},{9,6},{8,7},{7,8},{6,9},{13,10... | collective-permute-start | bytes 147464 | tf_op jit(solution)/shard_map/ppermute | solution.py:243
  4.2 5.1 %collective-permute-start.3 = (bf16[192,128]{1,0:T(8,128)(2,1)S(1)}, bf16[192,128]{1,0:T(8,128)(2,1)S(1)}, u32[]{:S(2)}, u32[]{:S(2)}) collective-permute-start(bf16[192,128]{1,0:T(8,128)(2,1)S(1)} %get-tuple-element.26), channel_id=1, source_target_pairs={{1,0},{0,1},{4,2},{5,3},{2,4},{3,5},{8,6},{9,7},{6,8},{7,9},{12,10... | collective-permute-start | bytes 147464 | tf_op jit(solution)/shard_map/ppermute | solution.py:243
  6.2 0.9 %copy-start = (bf16[256,256]{1,0:T(8,128)(2,1)S(1)}, bf16[256,256]{1,0:T(8,128)(2,1)}, u32[]{:S(2)}) copy-start(bf16[256,256]{1,0:T(8,128)(2,1)} %target.5) | copy-start | bytes 393220
  6.2 0.9 %copy-start.1 = (bf16[256,128]{1,0:T(8,128)(2,1)S(1)}, bf16[256,128]{1,0:T(8,128)(2,1)}, u32[]{:S(2)}) copy-start(bf16[256,128]{1,0:T(8,128)(2,1)} %dwell.3) | copy-start | bytes 196612
  7.6 1.7 %collective-permute-start.1 = (bf16[128,128]{1,0:T(8,128)(2,1)S(1)}, bf16[128,128]{1,0:T(8,128)(2,1)S(1)}, u32[]{:S(2)}, u32[]{:S(2)}) collective-permute-start(bf16[128,128]{1,0:T(8,128)(2,1)S(1)} %get-tuple-element.24), channel_id=1, source_target_pairs={{2,0},{3,1},{0,2},{1,3},{6,4},{7,5},{4,6},{5,7},{10,8},{11,9},{8,1... | collective-permute-start | bytes 98312 | tf_op jit(solution)/shard_map/ppermute | solution.py:243
  7.7 1.7 %copy-start.2 = (s32[256,128]{1,0:T(8,128)S(1)}, s32[256,128]{1,0:T(8,128)}, u32[]{:S(2)}) copy-start(s32[256,128]{1,0:T(8,128)} %bound.1) | copy-start | bytes 393220

commit v8 on v7

--- a/solution.py
+++ b/solution.py
@@ -14,7 +14,6 @@
 STEP_SIZE = 1.0
 BF16 = jnp.bfloat16
 F32 = jnp.float32
-SMEM = pl.BlockSpec(memory_space=pltpu.SMEM)
 VMEM = pl.BlockSpec(memory_space=pltpu.VMEM)
 HBM = pl.BlockSpec(memory_space=pltpu.HBM)
 
@@ -25,9 +24,18 @@
     )
 
 
-def band(line, width):
-    lines = jnp.broadcast_to(line[0:1, :width], (BLOCK, width))
+def band(table, level, start, width):
+    taps = table[0:1]
+    for r in range(1, table.shape[0]):
+        taps = jnp.where(level == r, table[r : r + 1], taps)
+    line = jnp.concatenate([taps, jnp.zeros((1, width - KTAPS), F32)], axis=1)
+    line = pltpu.roll(jnp.broadcast_to(line, (8, width)), start, 1)
+    lines = jnp.broadcast_to(line[0:1], (BLOCK, width))
     return pltpu.roll(lines, 0, 1, stride=1, stride_axis=0).astype(BF16)
+
+
+def number(one):
+    return jnp.max(one.astype(F32)).astype(jnp.int32)
 
 
 def lanes_of(blocks):
@@ -40,68 +48,35 @@
     return [pl.ds((blocks - 1) // 2 * BLOCK, BLOCK), pl.ds(0, BLOCK), pl.ds(2 * BLOCK, BLOCK)][:blocks]
 
 
-def pack_kernel(
-    dwell, target, offsets, levels, rates, row_taps, col_taps,
-    outer_side, outer_own, lines, scale_ref,
-    offsets_here, levels_here, rates_here, rows_here, cols_here, sems,
+def bands_kernel(
+    offsets, levels, rates, row_taps, col_taps,
+    fwd_ref, adj_ref, fold_ref, own_ref, edge_ref, scale_ref, col_ref,
 ):
-    tile = dwell.shape[0]
-    odd = lax.rem(lax.axis_index("space"), 2)
-    mine = pl.ds(pl.multiple_of(lax.axis_index("scen") * BLOCK, BLOCK), BLOCK)
-    dwell_rows = pl.ds(pl.multiple_of(odd * (tile - BLOCK), BLOCK), BLOCK)
-    target_rows = pl.ds(pl.multiple_of(odd * (tile - HALF), HALF), HALF)
-    moves = [
-        (offsets, offsets_here),
-        (levels, levels_here),
-        (rates, rates_here),
-        (row_taps, rows_here),
-        (col_taps, cols_here),
-    ]
-    for out in (outer_side, outer_own):
-        moves.append((dwell.at[dwell_rows, :], out.at[pl.ds(0, BLOCK), :]))
-        moves.append((target.at[target_rows, mine], out.at[pl.ds(BLOCK, HALF), :]))
-    copies = [pltpu.make_async_copy(a, b, sems.at[i]) for i, (a, b) in enumerate(moves)]
-    for copy in copies:
-        copy.start()
+    scen_total, width = col_ref.shape[0], col_ref.shape[1]
+    blocks = width // BLOCK
+    scen = lax.axis_index("scen")
+    own_rows = lanes_of(blocks)[0]
     turn = (
         lax.broadcasted_iota(jnp.int32, (KTAPS, KTAPS), 0)
         + lax.broadcasted_iota(jnp.int32, (KTAPS, KTAPS), 1)
         == KTAPS - 1
     )
     turn = turn.astype(F32).astype(BF16)
-    for copy in copies:
-        copy.wait()
-    scen_total = lines.shape[0]
-    rest = jnp.zeros((rates.shape[0], 3 * BLOCK - KTAPS), F32)
-    rows, cols = rows_here[...], cols_here[...]
-    tables = [rows.astype(F32), dot(rows, turn), dot(cols, turn)]
-    tables = [jnp.concatenate([table, rest], axis=1) for table in tables]
+    rows, cols = row_taps[...], col_taps[...]
+    rows_turned, cols_turned = dot(rows, turn), dot(cols, turn)
+    rows = rows.astype(F32)
+
     for s in range(scen_total):
-        level = levels_here[s]
-        rate = rates_here[level]
+        level = levels[0:1, s : s + 1]
+        rate = rates[0:1, 0:1]
+        for r in range(1, rates.shape[1]):
+            rate = jnp.where(level == r, rates[0:1, r : r + 1], rate)
         here = slice(s * BLOCK, (s + 1) * BLOCK)
-        scale_ref[0:1, here] = jnp.full((1, BLOCK), rate * rate * (1.0 / scen_total), F32)
-        scale_ref[1:2, here] = jnp.full((1, BLOCK), rate * (-1.0 / scen_total), F32)
-        shift_row, shift_col = offsets_here[0, s], offsets_here[1, s]
-        starts = (
-            HALF - RADIUS - shift_row,
-            HALF - RADIUS + shift_row,
-            BLOCK - RADIUS + shift_col,
-        )
-        for k, (table, start) in enumerate(zip(tables, starts)):
-            line = table[0:1]
-            for r in range(1, table.shape[0]):
-                line = jnp.where(level == r, table[r : r + 1], line)
-            lines[s, k] = pltpu.roll(jnp.broadcast_to(line, (8, 3 * BLOCK)), start, 1)
-
-
-def bands_kernel(lines, fwd_ref, adj_ref, fold_ref, own_ref, edge_ref, col_ref):
-    scen_total, width = col_ref.shape[0], col_ref.shape[1]
-    blocks = width // BLOCK
-    scen = lax.axis_index("scen")
-    own_rows = lanes_of(blocks)[0]
-    for s in range(scen_total):
-        fwd, adj = band(lines[s, 0], 2 * BLOCK), band(lines[s, 1], 2 * BLOCK)
+        scale_ref[0:1, here] = jnp.broadcast_to(rate * rate * (1.0 / scen_total), (1, BLOCK))
+        scale_ref[1:2, here] = jnp.broadcast_to(rate * (-1.0 / scen_total), (1, BLOCK))
+        shift_row, shift_col = [number(offsets[k : k + 1, s : s + 1]) for k in range(2)]
+        fwd = band(rows, level, HALF - RADIUS - shift_row, 2 * BLOCK)
+        adj = band(rows_turned, level, HALF - RADIUS + shift_row, 2 * BLOCK)
         fwd_ref[s] = fwd
         adj_ref[s] = adj
         upper, lower = adj[:, :BLOCK], adj[:, BLOCK:]
@@ -110,7 +85,7 @@
         edge_ref[0, :, at + BLOCK : at + 2 * BLOCK] = upper
         edge_ref[1, :, at : at + BLOCK] = dot(lower, fwd[:, BLOCK:]).astype(BF16)
         edge_ref[1, :, at + BLOCK : at + 2 * BLOCK] = lower
-        near = band(lines[s, 2], 3 * BLOCK)
+        near = band(cols_turned, level, BLOCK - RADIUS + shift_col, 3 * BLOCK)
         for y in range(blocks):
             for j in range(blocks):
                 piece = jnp.zeros((BLOCK, BLOCK), BF16)
@@ -130,6 +105,25 @@
         mine = col_ref[s, own_rows, :]
         own_ref[here, :] = mine
         fold_ref[:, here] = dot(col_ref[s], mine, 1).astype(BF16)
+
+
+def pack_kernel(dwell, target, *refs):
+    small, (out, *small_out), sems = refs[:5], refs[5:11], refs[11]
+    tile = dwell.shape[0]
+    odd = lax.rem(lax.axis_index("space"), 2)
+    mine = pl.ds(pl.multiple_of(lax.axis_index("scen") * BLOCK, BLOCK), BLOCK)
+    dwell_rows = pl.ds(pl.multiple_of(odd * (tile - BLOCK), BLOCK), BLOCK)
+    target_rows = pl.ds(pl.multiple_of(odd * (tile - HALF), HALF), HALF)
+    moves = [
+        (dwell.at[dwell_rows, :], out.at[pl.ds(0, BLOCK), :]),
+        (target.at[target_rows, mine], out.at[pl.ds(BLOCK, HALF), :]),
+        *zip(small, small_out),
+    ]
+    copies = [pltpu.make_async_copy(a, b, sems.at[i]) for i, (a, b) in enumerate(moves)]
+    for copy in copies:
+        copy.start()
+    for copy in copies:
+        copy.wait()
 
 
 def clear_outside(blocks, ref):
@@ -199,28 +193,39 @@
 
 
 def finish_kernel(blocks, scale, fold, own, edge, partial, bound, inner, *refs):
-    halos, (out, dwell_halo, target_halo) = refs[blocks - 1 : blocks] + refs[: blocks - 1], refs[blocks:]
+    halos, refs = refs[blocks - 1 : blocks] + refs[: blocks - 1], refs[blocks:]
+    out, dwell_halo, target_halo, terms = refs
     tile, width = out.shape[0], own.shape[1]
     space = lax.axis_index("space")
     odd = lax.rem(space, 2)
-    goal_rows = pl.ds(pl.multiple_of(odd * HALF, HALF), HALF)
-    target_halo[...] = jnp.zeros((BLOCK, width), BF16)
-    for b, lane in enumerate(lanes_of(blocks)):
-        dwell_halo[:, lane] = halos[b][:BLOCK, :]
-        target_halo[goal_rows, lane] = halos[b][BLOCK:, :]
-    clear_outside(blocks, dwell_halo)
-    clear_outside(blocks, target_halo)
-    from_dwell = (dot(dwell_halo[...], fold[...]) * scale[0:1, :]).astype(BF16)
-    from_target = (dot(target_halo[...], own[...], 1) * scale[1:2, :]).astype(BF16)
-    terms = terms_of(edge[odd], from_dwell, from_target)
     end = (space == 0) | (space == lax.axis_size("space") - 1)
-    terms = jnp.where(end, jnp.zeros_like(terms), terms)
-    for at, gradient in ((odd, terms), (1 - odd, inner[...].astype(F32))):
+
+    def step(at, gradient):
         half = pl.ds(pl.multiple_of(at * (tile - BLOCK), BLOCK), BLOCK)
         stepped = partial[half, :] - STEP_SIZE * gradient
         out[half, :] = jnp.where(
             bound[half, :] == 1, jnp.maximum(stepped, 0.0), stepped
         ).astype(BF16)
+
+    @pl.when(end)
+    def _():
+        terms[...] = jnp.zeros(terms.shape, F32)
+
+    @pl.when(jnp.logical_not(end))
+    def _():
+        goal_rows = pl.ds(pl.multiple_of(odd * HALF, HALF), HALF)
+        target_halo[...] = jnp.zeros((BLOCK, width), BF16)
+        for b, lane in enumerate(lanes_of(blocks)):
+            dwell_halo[:, lane] = halos[b][:BLOCK, :]
+            target_halo[goal_rows, lane] = halos[b][BLOCK:, :]
+        clear_outside(blocks, dwell_halo)
+        clear_outside(blocks, target_halo)
+        from_dwell = (dot(dwell_halo[...], fold[...]) * scale[0:1, :]).astype(BF16)
+        from_target = (dot(target_halo[...], own[...], 1) * scale[1:2, :]).astype(BF16)
+        terms[...] = terms_of(edge[odd], from_dwell, from_target)
+
+    step(1 - odd, inner[...].astype(F32))
+    step(odd, terms[...])
 
 
 def shards(
@@ -278,36 +283,30 @@
         )
     neighbours = [moved(dwell_map, side(c)) for c in sides]
     wide = scen_total * BLOCK
-    rates = rate_table.shape[0]
-    outer_side, outer_own, lines, scale = call(
+    small = (
+        offsets.T,
+        rate_index.reshape(1, scen_total),
+        rate_table.reshape(1, rate_table.shape[0]),
+        row_kernels,
+        col_kernels,
+    )
+    to_outer, *small = call(
         pack_kernel,
         "pack",
         (
             pltpu.VMEM((BLOCK + HALF, BLOCK), BF16),
-            pltpu.VMEM((BLOCK + HALF, BLOCK), BF16),
-            pltpu.VMEM((scen_total, 3, 8, 3 * BLOCK), F32),
-            pltpu.VMEM((8, wide), F32),
+            *(pltpu.VMEM(x.shape, x.dtype) for x in small),
         ),
-        [
-            pltpu.SMEM((2, scen_total), jnp.int32),
-            pltpu.SMEM((scen_total,), jnp.int32),
-            pltpu.SMEM((rates,), F32),
-            pltpu.VMEM((rates, KTAPS), BF16),
-            pltpu.VMEM((rates, KTAPS), BF16),
-            pltpu.SemaphoreType.DMA((9,)),
-        ],
+        [pltpu.SemaphoreType.DMA((7,))],
         10**5,
         [HBM] * 7,
         dwell_map,
         target_map,
-        offsets.T,
-        rate_index.reshape(scen_total),
-        rate_table,
-        row_kernels,
-        col_kernels,
+        *small,
         limit=None,
     )
-    fwd, adj, fold, own, edge = call(
+    halos = [moved(to_outer, outer(c)) for c in [0] + sides]
+    fwd, adj, fold, own, edge, scale = call(
         bands_kernel,
         "bands",
         (
@@ -316,13 +315,15 @@
             pltpu.VMEM((width, wide), BF16),
             pltpu.VMEM((wide, width), BF16),
             pltpu.VMEM((2, BLOCK, 2 * wide), BF16),
+            pltpu.VMEM((8, wide), F32),
         ),
-        [pltpu.VMEM((scen_total, width, width), BF16)],
+        [
+            pltpu.VMEM((scen_total, width, width), BF16),
+        ],
         10**8,
-        [VMEM],
-        lines,
-    )
-    halos = [moved(outer_side if c else outer_own, outer(c)) for c in [0] + sides]
+        [VMEM] * 5,
+        *small,
+    )
     from_dwell, to_inner = call(
         functools.partial(send_kernel, blocks),
         "send",
@@ -361,7 +362,11 @@
         functools.partial(finish_kernel, blocks),
         "finish",
         jax.ShapeDtypeStruct(dwell_map.shape, BF16),
-        [pltpu.VMEM((BLOCK, width), BF16), pltpu.VMEM((BLOCK, width), BF16)],
+        [
+            pltpu.VMEM((BLOCK, width), BF16),
+            pltpu.VMEM((BLOCK, width), BF16),
+            pltpu.VMEM((BLOCK, BLOCK), F32),
+        ],
         10**6,
         [VMEM] * (7 + blocks),
         scale,

time: 10.6 us -> 10 us (0.943)
  the two profiles are of different devices: /device:TPU:0 before, /device:TPU:1 now
where the time goes in v8:
time: 10 us; the launch traced here: 9.85 us
  starting transfers between devices  5.18 us (52%)
  Pallas kernels  4.34 us (43%)
  waiting for transfers between devices  0.26 us (3%)
    ppermute x4, starting transfers between devices, moved(): return lax.ppermute(x, ('space', 'scen'), pairs)  5.18 us
    pallas_call x5, Pallas kernels, call(): pl.pallas_call(kernel, out_shape=outs, in_specs=specs, out_specs=jax.tree...  4.34 us
    ppermute x4, waiting for transfers between devices, moved(): return lax.ppermute(x, ('space', 'scen'), pairs)  0.26 us
  transfers between devices with their start and end apart: 4, of which 1 were waited for; matrix products, arithmetic and copies ran while one was open for 0% of the time, Pallas kernels for 28%

profile of v8, /device:TPU:1, one launch (start us, length us, event | category | flops | bytes accessed | tf_op | source)
XLA Modules:
  0.0 9.8 jit_solution(13976213970966644937)
XLA Ops:
  0.0 2.1 %collective-permute-start = (bf16[256,128]{1,0:T(8,128)(2,1)}, bf16[256,128]{1,0:T(8,128)(2,1)S(1)}, u32[]{:S(2)}, u32[]{:S(2)}) collective-permute-start(bf16[256,128]{1,0:T(8,128)(2,1)} %dwell.3), channel_id=1, source_target_pairs={{1,0},{0,1},{3,2},{2,3},{5,4},{4,5},{7,6},{6,7},{9,8},{8,9},{11,10... | collective-permute-start | bytes 196616 | tf_op jit(solution)/shard_map/ppermute | solution.py:248
  2.1 0.9 %pack.1 = (bf16[192,128]{1,0:T(8,128)(2,1)S(1)}, s32[2,4]{1,0:T(2,128)S(1)}, s32[1,4]{1,0:T(1,128)S(1)}, f32[1,4]{1,0:T(1,128)S(1)}, bf16[4,63]{1,0:T(4,128)(2,1)S(1)}, /*index=5*/bf16[4,63]{1,0:T(4,128)(2,1)S(1)}) custom-call(bf16[256,128]{1,0:T(8,128)(2,1)} %dwell.3, bf16[256,256]{1,0:T(8,128)(2,1)} %target.5, s32[2,4]{1,0:T(2,128)} %bitcast.3, ...), custom_call_target="tpu_custom_call" | custom-call | flops 100000 | bytes 1000 | tf_op jit(solution)/shard_map/pack/pallas_call | solution.py:265
  2.9 2.1 %collective-permute-start.2 = (bf16[192,128]{1,0:T(8,128)(2,1)S(1)}, bf16[192,128]{1,0:T(8,128)(2,1)S(1)}, u32[]{:S(2)}, u32[]{:S(2)}) collective-permute-start(bf16[192,128]{1,0:T(8,128)(2,1)S(1)} %get-tuple-element.32), channel_id=1, source_target_pairs={{1,0},{0,1},{5,2},{4,3},{3,4},{2,5},{9,6},{8,7},{7,8},{6,9},{13,10... | collective-permute-start | bytes 147464 | tf_op jit(solution)/shard_map/ppermute | solution.py:248
  5.0 0.1 %collective-permute-start.3 = (bf16[192,128]{1,0:T(8,128)(2,1)S(1)}, bf16[192,128]{1,0:T(8,128)(2,1)S(1)}, u32[]{:S(2)}, u32[]{:S(2)}) collective-permute-start(bf16[192,128]{1,0:T(8,128)(2,1)S(1)} %get-tuple-element.32), channel_id=1, source_target_pairs={{1,0},{0,1},{4,2},{5,3},{2,4},{3,5},{8,6},{9,7},{6,8},{7,9},{12,10... | collective-permute-start | bytes 147464 | tf_op jit(solution)/shard_map/ppermute | solution.py:248
  5.1 0.0 copy-start
  5.1 0.0 copy-start.1
  5.1 1.0 %bands.1 = (bf16[4,128,256]{2,1,0:T(8,128)(2,1)S(1)}, bf16[4,128,256]{2,1,0:T(8,128)(2,1)S(1)}, bf16[256,512]{1,0:T(8,128)(2,1)S(1)}, bf16[512,256]{1,0:T(8,128)...) custom-call(s32[2,4]{1,0:T(2,128)S(1)} %get-tuple-element.19.offsets, ...), custom_call_target="tpu_custom_call" | custom-call | flops 100000000 | bytes 1000000 | tf_op jit(solution)/shard_map/bands/pallas_call | solution.py:265
  6.1 0.0 collective-permute-done.refs_1_
  6.1 0.0 copy-done
  6.1 0.0 copy-done.1
  6.1 0.5 %send.1 = (bf16[256,512]{1,0:T(8,128)(2,1)S(1)}, bf16[128,128]{1,0:T(8,128)(2,1)S(1)}) custom-call(f32[8,512]{1,0:T(8,128)S(1)} %get-tuple-element.24.scale, bf16[256,512]{1,0:T(8,128)(2,1)S(1)} %get-tuple-element.25.fold, bf16[512,256]{1,0:T(8,128)(2,1)S(1)} %get-tuple-element.26.own, bf16[2,128,1024]{2,1,0:T(8,128)(2,1)S(1)} %get-tuple-element.27.edge, ...), custom_call_target="tpu_custom_call" | custom-call | flops 100000000 | bytes 1000000 | tf_op jit(solution)/shard_map/send/pallas_call | solution.py:265
  6.6 0.9 %collective-permute-start.1 = (bf16[128,128]{1,0:T(8,128)(2,1)S(1)}, bf16[128,128]{1,0:T(8,128)(2,1)S(1)}, u32[]{:S(2)}, u32[]{:S(2)}) collective-permute-start(bf16[128,128]{1,0:T(8,128)(2,1)S(1)} %get-tuple-element.31), channel_id=1, source_target_pairs={{2,0},{3,1},{0,2},{1,3},{6,4},{7,5},{4,6},{5,7},{10,8},{11,9},{8,1... | collective-permute-start | bytes 98312 | tf_op jit(solution)/shard_map/ppermute | solution.py:248
  7.5 0.0 copy-start.2
  7.5 0.9 %own.1.partial = f32[256,128]{1,0:T(8,128)S(1)} custom-call(f32[8,512]{1,0:T(8,128)S(1)} %get-tuple-element.24.scale, bf16[4,128,256]{2,1,0:T(8,128)(2,1)S(1)} %get-tuple-element.28.fwd, bf16[4,128,256]{2,1,0:T(8,128)(2,1)S(1)} %get-tuple-element.29.adj, bf16[512,256]{1,0:T(8,128)(2,1)S(1)} %get-tuple-element.26.own, ...), custom_call_target="tpu_custom_call" | custom-call | flops 1000000000 | bytes 10000000 | tf_op jit(solution)/shard_map/own/pallas_call | solution.py:265
  8.4 0.0 collective-permute-done.2.refs_0_
  8.5 0.3 %collective-permute-done.3.refs_1_ = bf16[192,128]{1,0:T(8,128)(2,1)S(1)} collective-permute-done((bf16[192,128]{1,0:T(8,128)(2,1)S(1)}, bf16[192,128]{1,0:T(8,128)(2,1)S(1)}, u32[]{:S(2)}, u32[]{:S(2)}) %collective-permute-start.3) | collective-permute-done | bytes 49184 | tf_op jit(solution)/shard_map/ppermute | solution.py:248
  8.7 0.0 collective-permute-done.1.inner
  8.7 0.0 copy-done.2
  8.7 1.1 %finish.1 = bf16[256,128]{1,0:T(8,128)(2,1)} custom-call(f32[8,512]{1,0:T(8,128)S(1)} %get-tuple-element.24.scale, bf16[256,512]{1,0:T(8,128)(2,1)S(1)} %get-tuple-element.25.fold, bf16[512,256]{1,0:T(8,128)(2,1)S(1)} %get-tuple-element.26.own, bf16[2,128,1024]{2,1,0:T(8,128)(2,1)S(1)} %get-tuple-element.27.edge, f32[256,128]{1,0:T(8,128)S(1)} %own.1.partial, ...), custom_call_target="tpu_custom_call" | custom-call | flops 1000000 | bytes 10000 | tf_op jit(solution)/shard_map/finish/pallas_call | solution.py:265
Async XLA Ops:
  0.0 6.1 %collective-permute-start = (bf16[256,128]{1,0:T(8,128)(2,1)}, bf16[256,128]{1,0:T(8,128)(2,1)S(1)}, u32[]{:S(2)}, u32[]{:S(2)}) collective-permute-start(bf16[256,128]{1,0:T(8,128)(2,1)} %dwell.3), channel_id=1, source_target_pairs={{1,0},{0,1},{3,2},{2,3},{5,4},{4,5},{7,6},{6,7},{9,8},{8,9},{11,10... | collective-permute-start | bytes 196616 | tf_op jit(solution)/shard_map/ppermute | solution.py:248
  2.9 5.5 %collective-permute-start.2 = (bf16[192,128]{1,0:T(8,128)(2,1)S(1)}, bf16[192,128]{1,0:T(8,128)(2,1)S(1)}, u32[]{:S(2)}, u32[]{:S(2)}) collective-permute-start(bf16[192,128]{1,0:T(8,128)(2,1)S(1)} %get-tuple-element.32), channel_id=1, source_target_pairs={{1,0},{0,1},{5,2},{4,3},{3,4},{2,5},{9,6},{8,7},{7,8},{6,9},{13,10... | collective-permute-start | bytes 147464 | tf_op jit(solution)/shard_map/ppermute | solution.py:248
  5.0 3.7 %collective-permute-start.3 = (bf16[192,128]{1,0:T(8,128)(2,1)S(1)}, bf16[192,128]{1,0:T(8,128)(2,1)S(1)}, u32[]{:S(2)}, u32[]{:S(2)}) collective-permute-start(bf16[192,128]{1,0:T(8,128)(2,1)S(1)} %get-tuple-element.32), channel_id=1, source_target_pairs={{1,0},{0,1},{4,2},{5,3},{2,4},{3,5},{8,6},{9,7},{6,8},{7,9},{12,10... | collective-permute-start | bytes 147464 | tf_op jit(solution)/shard_map/ppermute | solution.py:248
  5.1 1.0 %copy-start = (bf16[256,256]{1,0:T(8,128)(2,1)S(1)}, bf16[256,256]{1,0:T(8,128)(2,1)}, u32[]{:S(2)}) copy-start(bf16[256,256]{1,0:T(8,128)(2,1)} %target.5) | copy-start | bytes 393220
  5.1 1.0 %copy-start.1 = (bf16[256,128]{1,0:T(8,128)(2,1)S(1)}, bf16[256,128]{1,0:T(8,128)(2,1)}, u32[]{:S(2)}) copy-start(bf16[256,128]{1,0:T(8,128)(2,1)} %dwell.3) | copy-start | bytes 196612
  6.6 2.1 %collective-permute-start.1 = (bf16[128,128]{1,0:T(8,128)(2,1)S(1)}, bf16[128,128]{1,0:T(8,128)(2,1)S(1)}, u32[]{:S(2)}, u32[]{:S(2)}) collective-permute-start(bf16[128,128]{1,0:T(8,128)(2,1)S(1)} %get-tuple-element.31), channel_id=1, source_target_pairs={{2,0},{3,1},{0,2},{1,3},{6,4},{7,5},{4,6},{5,7},{10,8},{11,9},{8,1... | collective-permute-start | bytes 98312 | tf_op jit(solution)/shard_map/ppermute | solution.py:248
  7.5 1.2 %copy-start.2 = (s32[256,128]{1,0:T(8,128)S(1)}, s32[256,128]{1,0:T(8,128)}, u32[]{:S(2)}) copy-start(s32[256,128]{1,0:T(8,128)} %bound.1) | copy-start | bytes 393220

commit v9 on v8

--- a/solution.py
+++ b/solution.py
@@ -18,10 +18,8 @@
 HBM = pl.BlockSpec(memory_space=pltpu.HBM)
 
 
-def dot(a, b, contract_b=0):
-    return lax.dot_general(
-        a, b, (((1,), (contract_b,)), ((), ())), preferred_element_type=F32
-    )
+def dot(a, b):
+    return jnp.dot(a, b, preferred_element_type=F32)
 
 
 def band(table, level, start, width):
@@ -102,9 +100,9 @@
 
     for s in range(scen_total):
         here = slice(s * BLOCK, (s + 1) * BLOCK)
-        mine = col_ref[s, own_rows, :]
-        own_ref[here, :] = mine
-        fold_ref[:, here] = dot(col_ref[s], mine, 1).astype(BF16)
+        mine = col_ref[s, own_rows, :].T
+        own_ref[:, here] = mine
+        fold_ref[:, here] = dot(col_ref[s], mine).astype(BF16)
 
 
 def pack_kernel(dwell, target, *refs):
@@ -155,19 +153,19 @@
     rows = pl.ds(pl.multiple_of((1 - odd) * (tile - HALF), HALF), HALF)
     target_ends[...] = jnp.zeros(target_ends.shape, BF16)
     target_ends[pl.ds(pl.multiple_of(odd * HALF, HALF), HALF), :] = target[rows, :]
-    ends = (dot(target_ends[...], own[...], 1) * scale[1:2, :]).astype(BF16)
+    ends = (dot(target_ends[...], own[...]) * scale[1:2, :]).astype(BF16)
     rows = pl.ds(pl.multiple_of((1 - odd) * (tile - BLOCK), BLOCK), BLOCK)
     to_inner[...] = terms_of(edge[odd], from_ref[rows, :], ends).astype(BF16)
 
 
 def own_kernel(scale, fwd, adj, own, from_dwell, target, dwell, partial_ref, target_all, rhs):
-    scen_total, width = fwd.shape[0], own.shape[1]
+    scen_total, width = fwd.shape[0], own.shape[0]
     tile = target.shape[0]
     space = lax.axis_index("space")
     target_all[:HALF, :] = jnp.zeros((HALF, width), BF16)
     target_all[HALF : HALF + tile, :] = target[...]
     target_all[HALF + tile :, :] = jnp.zeros((HALF, width), BF16)
-    from_target = (dot(target_all[...], own[...], 1) * scale[1:2, :]).astype(BF16)
+    from_target = (dot(target_all[...], own[...]) * scale[1:2, :]).astype(BF16)
     lane = lax.broadcasted_iota(jnp.int32, (BLOCK, 2 * BLOCK), 1)
     cuts = (
         (space == 0) & (lane < HALF),
@@ -194,8 +192,8 @@
 
 def finish_kernel(blocks, scale, fold, own, edge, partial, bound, inner, *refs):
     halos, refs = refs[blocks - 1 : blocks] + refs[: blocks - 1], refs[blocks:]
-    out, dwell_halo, target_halo, terms = refs
-    tile, width = out.shape[0], own.shape[1]
+    out, dwell_halo, target_halo = refs
+    tile, width = out.shape[0], own.shape[0]
     space = lax.axis_index("space")
     odd = lax.rem(space, 2)
     end = (space == 0) | (space == lax.axis_size("space") - 1)
@@ -209,7 +207,8 @@
 
     @pl.when(end)
     def _():
-        terms[...] = jnp.zeros(terms.shape, F32)
+        step(1 - odd, inner[...].astype(F32))
+        step(odd, 0.0)
 
     @pl.when(jnp.logical_not(end))
     def _():
@@ -221,11 +220,10 @@
         clear_outside(blocks, dwell_halo)
         clear_outside(blocks, target_halo)
         from_dwell = (dot(dwell_halo[...], fold[...]) * scale[0:1, :]).astype(BF16)
-        from_target = (dot(target_halo[...], own[...], 1) * scale[1:2, :]).astype(BF16)
-        terms[...] = terms_of(edge[odd], from_dwell, from_target)
-
-    step(1 - odd, inner[...].astype(F32))
-    step(odd, terms[...])
+        from_target = (dot(target_halo[...], own[...]) * scale[1:2, :]).astype(BF16)
+        terms = terms_of(edge[odd], from_dwell, from_target)
+        step(1 - odd, inner[...].astype(F32))
+        step(odd, terms)
 
 
 def shards(
@@ -313,7 +311,7 @@
             pltpu.VMEM((scen_total, BLOCK, 2 * BLOCK), BF16),
             pltpu.VMEM((scen_total, BLOCK, 2 * BLOCK), BF16),
             pltpu.VMEM((width, wide), BF16),
-            pltpu.VMEM((wide, width), BF16),
+            pltpu.VMEM((width, wide), BF16),
             pltpu.VMEM((2, BLOCK, 2 * wide), BF16),
             pltpu.VMEM((8, wide), F32),
         ),
@@ -362,11 +360,7 @@
         functools.partial(finish_kernel, blocks),
         "finish",
         jax.ShapeDtypeStruct(dwell_map.shape, BF16),
-        [
-            pltpu.VMEM((BLOCK, width), BF16),
-            pltpu.VMEM((BLOCK, width), BF16),
-            pltpu.VMEM((BLOCK, BLOCK), F32),
-        ],
+        [pltpu.VMEM((BLOCK, width), BF16), pltpu.VMEM((BLOCK, width), BF16)],
         10**6,
         [VMEM] * (7 + blocks),
         scale,

time: 10 us -> 9.97 us (level)
  no operation moved by 1% of the time
where the time goes in v9:
time: 9.97 us; the launch traced here: 9.79 us
  starting transfers between devices  5.18 us (52%)
  Pallas kernels  4.29 us (43%)
  waiting for transfers between devices  0.25 us (3%)
    ppermute x4, starting transfers between devices, moved(): return lax.ppermute(x, ('space', 'scen'), pairs)  5.18 us
    pallas_call x5, Pallas kernels, call(): pl.pallas_call(kernel, out_shape=outs, in_specs=specs, out_specs=jax.tree...  4.29 us
    ppermute x4, waiting for transfers between devices, moved(): return lax.ppermute(x, ('space', 'scen'), pairs)  0.25 us
  transfers between devices with their start and end apart: 4, of which 1 were waited for; matrix products, arithmetic and copies ran while one was open for 0% of the time, Pallas kernels for 28%

profile of v9, /device:TPU:1, one launch (start us, length us, event | category | flops | bytes accessed | tf_op | source)
XLA Modules:
  0.0 9.8 jit_solution(15601658111839335307)
XLA Ops:
  0.0 2.1 %collective-permute-start = (bf16[256,128]{1,0:T(8,128)(2,1)}, bf16[256,128]{1,0:T(8,128)(2,1)S(1)}, u32[]{:S(2)}, u32[]{:S(2)}) collective-permute-start(bf16[256,128]{1,0:T(8,128)(2,1)} %dwell.3), channel_id=1, source_target_pairs={{1,0},{0,1},{3,2},{2,3},{5,4},{4,5},{7,6},{6,7},{9,8},{8,9},{11,10... | collective-permute-start | bytes 196616 | tf_op jit(solution)/shard_map/ppermute | solution.py:246
  2.1 0.9 %pack.1 = (bf16[192,128]{1,0:T(8,128)(2,1)S(1)}, s32[2,4]{1,0:T(2,128)S(1)}, s32[1,4]{1,0:T(1,128)S(1)}, f32[1,4]{1,0:T(1,128)S(1)}, bf16[4,63]{1,0:T(4,128)(2,1)S(1)}, /*index=5*/bf16[4,63]{1,0:T(4,128)(2,1)S(1)}) custom-call(bf16[256,128]{1,0:T(8,128)(2,1)} %dwell.3, bf16[256,256]{1,0:T(8,128)(2,1)} %target.5, s32[2,4]{1,0:T(2,128)} %bitcast.3, ...), custom_call_target="tpu_custom_call" | custom-call | flops 100000 | bytes 1000 | tf_op jit(solution)/shard_map/pack/pallas_call | solution.py:263
  2.9 2.1 %collective-permute-start.2 = (bf16[192,128]{1,0:T(8,128)(2,1)S(1)}, bf16[192,128]{1,0:T(8,128)(2,1)S(1)}, u32[]{:S(2)}, u32[]{:S(2)}) collective-permute-start(bf16[192,128]{1,0:T(8,128)(2,1)S(1)} %get-tuple-element.32), channel_id=1, source_target_pairs={{1,0},{0,1},{5,2},{4,3},{3,4},{2,5},{9,6},{8,7},{7,8},{6,9},{13,10... | collective-permute-start | bytes 147464 | tf_op jit(solution)/shard_map/ppermute | solution.py:246
  5.0 0.1 %collective-permute-start.3 = (bf16[192,128]{1,0:T(8,128)(2,1)S(1)}, bf16[192,128]{1,0:T(8,128)(2,1)S(1)}, u32[]{:S(2)}, u32[]{:S(2)}) collective-permute-start(bf16[192,128]{1,0:T(8,128)(2,1)S(1)} %get-tuple-element.32), channel_id=1, source_target_pairs={{1,0},{0,1},{4,2},{5,3},{2,4},{3,5},{8,6},{9,7},{6,8},{7,9},{12,10... | collective-permute-start | bytes 147464 | tf_op jit(solution)/shard_map/ppermute | solution.py:246
  5.1 0.0 copy-start
  5.1 0.0 copy-start.1
  5.1 1.0 %bands.1 = (bf16[4,128,256]{2,1,0:T(8,128)(2,1)S(1)}, bf16[4,128,256]{2,1,0:T(8,128)(2,1)S(1)}, bf16[256,512]{1,0:T(8,128)(2,1)S(1)}, bf16[256,512]{1,0:T(8,128)...) custom-call(s32[2,4]{1,0:T(2,128)S(1)} %get-tuple-element.19.offsets, ...), custom_call_target="tpu_custom_call" | custom-call | flops 100000000 | bytes 1000000 | tf_op jit(solution)/shard_map/bands/pallas_call | solution.py:263
  6.1 0.0 collective-permute-done.refs_1_
  6.2 0.0 copy-done
  6.2 0.0 copy-done.1
  6.2 0.5 %send.1 = (bf16[256,512]{1,0:T(8,128)(2,1)S(1)}, bf16[128,128]{1,0:T(8,128)(2,1)S(1)}) custom-call(f32[8,512]{1,0:T(8,128)S(1)} %get-tuple-element.24.scale, bf16[256,512]{1,0:T(8,128)(2,1)S(1)} %get-tuple-element.25.fold, bf16[256,512]{1,0:T(8,128)(2,1)S(1)} %get-tuple-element.26.own, bf16[2,128,1024]{2,1,0:T(8,128)(2,1)S(1)} %get-tuple-element.27.edge, ...), custom_call_target="tpu_custom_call" | custom-call | flops 100000000 | bytes 1000000 | tf_op jit(solution)/shard_map/send/pallas_call | solution.py:263
  6.7 0.9 %collective-permute-start.1 = (bf16[128,128]{1,0:T(8,128)(2,1)S(1)}, bf16[128,128]{1,0:T(8,128)(2,1)S(1)}, u32[]{:S(2)}, u32[]{:S(2)}) collective-permute-start(bf16[128,128]{1,0:T(8,128)(2,1)S(1)} %get-tuple-element.31), channel_id=1, source_target_pairs={{2,0},{3,1},{0,2},{1,3},{6,4},{7,5},{4,6},{5,7},{10,8},{11,9},{8,1... | collective-permute-start | bytes 98312 | tf_op jit(solution)/shard_map/ppermute | solution.py:246
  7.6 0.0 copy-start.2
  7.6 0.9 %own.1.partial = f32[256,128]{1,0:T(8,128)S(1)} custom-call(f32[8,512]{1,0:T(8,128)S(1)} %get-tuple-element.24.scale, bf16[4,128,256]{2,1,0:T(8,128)(2,1)S(1)} %get-tuple-element.28.fwd, bf16[4,128,256]{2,1,0:T(8,128)(2,1)S(1)} %get-tuple-element.29.adj, bf16[256,512]{1,0:T(8,128)(2,1)S(1)} %get-tuple-element.26.own, ...), custom_call_target="tpu_custom_call" | custom-call | flops 1000000000 | bytes 10000000 | tf_op jit(solution)/shard_map/own/pallas_call | solution.py:263
  8.5 0.0 collective-permute-done.2.refs_0_
  8.5 0.2 %collective-permute-done.3.refs_1_ = bf16[192,128]{1,0:T(8,128)(2,1)S(1)} collective-permute-done((bf16[192,128]{1,0:T(8,128)(2,1)S(1)}, bf16[192,128]{1,0:T(8,128)(2,1)S(1)}, u32[]{:S(2)}, u32[]{:S(2)}) %collective-permute-start.3) | collective-permute-done | bytes 49184 | tf_op jit(solution)/shard_map/ppermute | solution.py:246
  8.7 0.0 collective-permute-done.1.inner
  8.7 0.0 copy-done.2
  8.7 1.1 %finish.1 = bf16[256,128]{1,0:T(8,128)(2,1)} custom-call(f32[8,512]{1,0:T(8,128)S(1)} %get-tuple-element.24.scale, bf16[256,512]{1,0:T(8,128)(2,1)S(1)} %get-tuple-element.25.fold, bf16[256,512]{1,0:T(8,128)(2,1)S(1)} %get-tuple-element.26.own, bf16[2,128,1024]{2,1,0:T(8,128)(2,1)S(1)} %get-tuple-element.27.edge, f32[256,128]{1,0:T(8,128)S(1)} %own.1.partial, ...), custom_call_target="tpu_custom_call" | custom-call | flops 1000000 | bytes 10000 | tf_op jit(solution)/shard_map/finish/pallas_call | solution.py:263
Async XLA Ops:
  0.0 6.1 %collective-permute-start = (bf16[256,128]{1,0:T(8,128)(2,1)}, bf16[256,128]{1,0:T(8,128)(2,1)S(1)}, u32[]{:S(2)}, u32[]{:S(2)}) collective-permute-start(bf16[256,128]{1,0:T(8,128)(2,1)} %dwell.3), channel_id=1, source_target_pairs={{1,0},{0,1},{3,2},{2,3},{5,4},{4,5},{7,6},{6,7},{9,8},{8,9},{11,10... | collective-permute-start | bytes 196616 | tf_op jit(solution)/shard_map/ppermute | solution.py:246
  2.9 5.5 %collective-permute-start.2 = (bf16[192,128]{1,0:T(8,128)(2,1)S(1)}, bf16[192,128]{1,0:T(8,128)(2,1)S(1)}, u32[]{:S(2)}, u32[]{:S(2)}) collective-permute-start(bf16[192,128]{1,0:T(8,128)(2,1)S(1)} %get-tuple-element.32), channel_id=1, source_target_pairs={{1,0},{0,1},{5,2},{4,3},{3,4},{2,5},{9,6},{8,7},{7,8},{6,9},{13,10... | collective-permute-start | bytes 147464 | tf_op jit(solution)/shard_map/ppermute | solution.py:246
  5.0 3.7 %collective-permute-start.3 = (bf16[192,128]{1,0:T(8,128)(2,1)S(1)}, bf16[192,128]{1,0:T(8,128)(2,1)S(1)}, u32[]{:S(2)}, u32[]{:S(2)}) collective-permute-start(bf16[192,128]{1,0:T(8,128)(2,1)S(1)} %get-tuple-element.32), channel_id=1, source_target_pairs={{1,0},{0,1},{4,2},{5,3},{2,4},{3,5},{8,6},{9,7},{6,8},{7,9},{12,10... | collective-permute-start | bytes 147464 | tf_op jit(solution)/shard_map/ppermute | solution.py:246
  5.1 1.0 %copy-start = (bf16[256,256]{1,0:T(8,128)(2,1)S(1)}, bf16[256,256]{1,0:T(8,128)(2,1)}, u32[]{:S(2)}) copy-start(bf16[256,256]{1,0:T(8,128)(2,1)} %target.5) | copy-start | bytes 393220
  5.1 1.0 %copy-start.1 = (bf16[256,128]{1,0:T(8,128)(2,1)S(1)}, bf16[256,128]{1,0:T(8,128)(2,1)}, u32[]{:S(2)}) copy-start(bf16[256,128]{1,0:T(8,128)(2,1)} %dwell.3) | copy-start | bytes 196612
  6.7 2.0 %collective-permute-start.1 = (bf16[128,128]{1,0:T(8,128)(2,1)S(1)}, bf16[128,128]{1,0:T(8,128)(2,1)S(1)}, u32[]{:S(2)}, u32[]{:S(2)}) collective-permute-start(bf16[128,128]{1,0:T(8,128)(2,1)S(1)} %get-tuple-element.31), channel_id=1, source_target_pairs={{2,0},{3,1},{0,2},{1,3},{6,4},{7,5},{4,6},{5,7},{10,8},{11,9},{8,1... | collective-permute-start | bytes 98312 | tf_op jit(solution)/shard_map/ppermute | solution.py:246
  7.6 1.1 %copy-start.2 = (s32[256,128]{1,0:T(8,128)S(1)}, s32[256,128]{1,0:T(8,128)}, u32[]{:S(2)}) copy-start(s32[256,128]{1,0:T(8,128)} %bound.1) | copy-start | bytes 393220

commit v10 on v9

--- a/solution.py
+++ b/solution.py
@@ -105,23 +105,16 @@
         fold_ref[:, here] = dot(col_ref[s], mine).astype(BF16)
 
 
-def pack_kernel(dwell, target, *refs):
-    small, (out, *small_out), sems = refs[:5], refs[5:11], refs[11]
+def lead_kernel(out):
+    out[...] = jnp.zeros(out.shape, F32)
+
+
+def pack_kernel(dwell, target, lead, out):
     tile = dwell.shape[0]
     odd = lax.rem(lax.axis_index("space"), 2)
     mine = pl.ds(pl.multiple_of(lax.axis_index("scen") * BLOCK, BLOCK), BLOCK)
-    dwell_rows = pl.ds(pl.multiple_of(odd * (tile - BLOCK), BLOCK), BLOCK)
-    target_rows = pl.ds(pl.multiple_of(odd * (tile - HALF), HALF), HALF)
-    moves = [
-        (dwell.at[dwell_rows, :], out.at[pl.ds(0, BLOCK), :]),
-        (target.at[target_rows, mine], out.at[pl.ds(BLOCK, HALF), :]),
-        *zip(small, small_out),
-    ]
-    copies = [pltpu.make_async_copy(a, b, sems.at[i]) for i, (a, b) in enumerate(moves)]
-    for copy in copies:
-        copy.start()
-    for copy in copies:
-        copy.wait()
+    out[:BLOCK, :] = dwell[pl.ds(pl.multiple_of(odd * (tile - BLOCK), BLOCK), BLOCK), :]
+    out[BLOCK:, :] = target[pl.ds(pl.multiple_of(odd * (tile - HALF), HALF), HALF), mine]
 
 
 def clear_outside(blocks, ref):
@@ -288,20 +281,17 @@
         row_kernels,
         col_kernels,
     )
-    to_outer, *small = call(
+    lead = call(lead_kernel, "lead", pltpu.VMEM((8, BLOCK), F32), [], 10**9, [])
+    to_outer = call(
         pack_kernel,
         "pack",
-        (
-            pltpu.VMEM((BLOCK + HALF, BLOCK), BF16),
-            *(pltpu.VMEM(x.shape, x.dtype) for x in small),
-        ),
-        [pltpu.SemaphoreType.DMA((7,))],
+        pltpu.VMEM((BLOCK + HALF, BLOCK), BF16),
+        [],
         10**5,
-        [HBM] * 7,
+        [VMEM] * 3,
         dwell_map,
         target_map,
-        *small,
-        limit=None,
+        lead,
     )
     halos = [moved(to_outer, outer(c)) for c in [0] + sides]
     fwd, adj, fold, own, edge, scale = call(

time: 9.97 us -> 9.72 us (0.975)
  the two profiles are of different devices: /device:TPU:1 before, /device:TPU:25 now
where the time goes in v10:
time: 9.72 us; the launch traced here: 9.57 us
  starting transfers between devices  5.29 us (54%)
  Pallas kernels  3.47 us (36%)
  local copies, waits for them, and re-layouts  0.68 us (7%)
  between operations  0.11 us (1%)
    ppermute x4, starting transfers between devices, moved(): return lax.ppermute(x, ('space', 'scen'), pairs)  5.29 us
    pallas_call x6, Pallas kernels, call(): pl.pallas_call(kernel, out_shape=outs, in_specs=specs, out_specs=jax.tree...  3.47 us
    unnamed x16, local copies, waits for them, and re-layouts  0.68 us
  transfers between devices with their start and end apart: 4, of which 0 were waited for; matrix products, arithmetic and copies ran while one was open for 0% of the time, Pallas kernels for 20%

profile of v10, /device:TPU:25, one launch (start us, length us, event | category | flops | bytes accessed | tf_op | source)
XLA Modules:
  0.0 9.6 jit_solution(17016666724459523811)
XLA Ops:
  0.0 0.0 copy-start.1
  0.0 0.0 copy-start
  0.0 1.2 %collective-permute-start = (bf16[256,128]{1,0:T(8,128)(2,1)}, bf16[256,128]{1,0:T(8,128)(2,1)S(1)}, u32[]{:S(2)}, u32[]{:S(2)}) collective-permute-start(bf16[256,128]{1,0:T(8,128)(2,1)} %dwell.3), channel_id=1, source_target_pairs={{1,0},{0,1},{3,2},{2,3},{5,4},{4,5},{7,6},{6,7},{9,8},{8,9},{11,10... | collective-permute-start | bytes 196616 | tf_op jit(solution)/shard_map/ppermute | solution.py:239
  1.2 0.0 copy-done.1
  1.2 0.0 copy-done
  1.3 0.0 copy-start.5
  1.3 0.0 copy-start.7
  1.3 2.4 %collective-permute-start.2 = (bf16[192,128]{1,0:T(8,128)(2,1)S(1)}, bf16[192,128]{1,0:T(8,128)(2,1)S(1)}, u32[]{:S(2)}, u32[]{:S(2)}) collective-permute-start(bf16[192,128]{1,0:T(8,128)(2,1)S(1)} %pack.1), channel_id=1, source_target_pairs={{1,0},{0,1},{5,2},{4,3},{3,4},{2,5},{9,6},{8,7},{7,8},{6,9},{13,10... | collective-permute-start | bytes 147464 | tf_op jit(solution)/shard_map/ppermute | solution.py:239
  3.8 0.0 collective-permute-start.3
  3.8 0.0 copy-done.4
  3.8 0.0 copy-done.5
  3.8 0.0 copy-done.7
  3.8 0.7 %copy-done.3 = s32[4,2]{0,1:T(2,128)S(1)} copy-done((s32[4,2]{0,1:T(2,128)S(1)}, s32[4,2]{0,1:T(2,128)}, u32[]{:S(2)}) %copy-start.3) | copy-done | bytes 56
  4.4 0.0 copy-done.6
  4.4 1.0 %bands.1 = (bf16[4,128,256]{2,1,0:T(8,128)(2,1)S(1)}, bf16[4,128,256]{2,1,0:T(8,128)(2,1)S(1)}, bf16[256,512]{1,0:T(8,128)(2,1)S(1)}, bf16[256,512]{1,0:T(8,128)...) custom-call(s32[2,4]{1,0:T(2,128)S(1)} %bitcast.3, s32[1,4]{1,0:T(1,128)S(1)} %bitcast.4, ...), custom_call_target="tpu_custom_call" | custom-call | flops 100000000 | bytes 1000000 | tf_op jit(solution)/shard_map/bands/pallas_call | solution.py:256
  5.4 0.0 collective-permute-done.refs_1_
  5.5 0.5 %send.1 = (bf16[256,512]{1,0:T(8,128)(2,1)S(1)}, bf16[128,128]{1,0:T(8,128)(2,1)S(1)}) custom-call(f32[8,512]{1,0:T(8,128)S(1)} %get-tuple-element.13.scale, bf16[256,512]{1,0:T(8,128)(2,1)S(1)} %get-tuple-element.14.fold, bf16[256,512]{1,0:T(8,128)(2,1)S(1)} %get-tuple-element.15.own, bf16[2,128,1024]{2,1,0:T(8,128)(2,1)S(1)} %get-tuple-element.16.edge, ...), custom_call_target="tpu_custom_call" | custom-call | flops 100000000 | bytes 1000000 | tf_op jit(solution)/shard_map/send/pallas_call | solution.py:256
  5.9 1.6 %collective-permute-start.1 = (bf16[128,128]{1,0:T(8,128)(2,1)S(1)}, bf16[128,128]{1,0:T(8,128)(2,1)S(1)}, u32[]{:S(2)}, u32[]{:S(2)}) collective-permute-start(bf16[128,128]{1,0:T(8,128)(2,1)S(1)} %get-tuple-element.20), channel_id=1, source_target_pairs={{2,0},{3,1},{0,2},{1,3},{6,4},{7,5},{4,6},{5,7},{10,8},{11,9},{8,1... | collective-permute-start | bytes 98312 | tf_op jit(solution)/shard_map/ppermute | solution.py:239
  7.6 0.9 %own.1.partial = f32[256,128]{1,0:T(8,128)S(1)} custom-call(f32[8,512]{1,0:T(8,128)S(1)} %get-tuple-element.13.scale, bf16[4,128,256]{2,1,0:T(8,128)(2,1)S(1)} %get-tuple-element.17.fwd, bf16[4,128,256]{2,1,0:T(8,128)(2,1)S(1)} %get-tuple-element.18.adj, bf16[256,512]{1,0:T(8,128)(2,1)S(1)} %get-tuple-element.15.own, ...), custom_call_target="tpu_custom_call" | custom-call | flops 1000000000 | bytes 10000000 | tf_op jit(solution)/shard_map/own/pallas_call | solution.py:256
  8.4 0.0 collective-permute-done.2.refs_0_
  8.4 0.0 collective-permute-done.3.refs_1_
  8.5 0.0 collective-permute-done.1.inner
  8.5 0.0 copy-done.2
  8.5 1.1 %finish.1 = bf16[256,128]{1,0:T(8,128)(2,1)} custom-call(f32[8,512]{1,0:T(8,128)S(1)} %get-tuple-element.13.scale, bf16[256,512]{1,0:T(8,128)(2,1)S(1)} %get-tuple-element.14.fold, bf16[256,512]{1,0:T(8,128)(2,1)S(1)} %get-tuple-element.15.own, bf16[2,128,1024]{2,1,0:T(8,128)(2,1)S(1)} %get-tuple-element.16.edge, f32[256,128]{1,0:T(8,128)S(1)} %own.1.partial, ...), custom_call_target="tpu_custom_call" | custom-call | flops 1000000 | bytes 10000 | tf_op jit(solution)/shard_map/finish/pallas_call | solution.py:256
  (6 shorter events, 0.0 us)
Async XLA Ops:
  0.0 1.2 %copy-start.1 = (bf16[256,128]{1,0:T(8,128)(2,1)S(1)}, bf16[256,128]{1,0:T(8,128)(2,1)}, u32[]{:S(2)}) copy-start(bf16[256,128]{1,0:T(8,128)(2,1)} %dwell.3) | copy-start | bytes 196612
  0.0 1.2 %copy-start = (bf16[256,256]{1,0:T(8,128)(2,1)S(1)}, bf16[256,256]{1,0:T(8,128)(2,1)}, u32[]{:S(2)}) copy-start(bf16[256,256]{1,0:T(8,128)(2,1)} %target.5) | copy-start | bytes 393220
  0.0 5.4 %collective-permute-start = (bf16[256,128]{1,0:T(8,128)(2,1)}, bf16[256,128]{1,0:T(8,128)(2,1)S(1)}, u32[]{:S(2)}, u32[]{:S(2)}) collective-permute-start(bf16[256,128]{1,0:T(8,128)(2,1)} %dwell.3), channel_id=1, source_target_pairs={{1,0},{0,1},{3,2},{2,3},{5,4},{4,5},{7,6},{6,7},{9,8},{8,9},{11,10... | collective-permute-start | bytes 196616 | tf_op jit(solution)/shard_map/ppermute | solution.py:239
  1.3 2.5 %copy-start.4 = (bf16[4,63]{1,0:T(4,128)(2,1)S(1)}, bf16[4,63]{1,0:T(4,128)(2,1)}, u32[]{:S(2)}) copy-start(bf16[4,63]{1,0:T(4,128)(2,1)} %row_taps.1) | copy-start | bytes 1516
  1.3 2.5 %copy-start.5 = (bf16[4,63]{1,0:T(4,128)(2,1)S(1)}, bf16[4,63]{1,0:T(4,128)(2,1)}, u32[]{:S(2)}) copy-start(bf16[4,63]{1,0:T(4,128)(2,1)} %col_taps.1) | copy-start | bytes 1516
  1.3 2.5 %copy-start.7 = (f32[4]{0:T(128)S(1)}, f32[4]{0:T(128)}, u32[]{:S(2)}) copy-start(f32[4]{0:T(128)} %param.13) | copy-start | bytes 52
  1.3 7.1 %collective-permute-start.2 = (bf16[192,128]{1,0:T(8,128)(2,1)S(1)}, bf16[192,128]{1,0:T(8,128)(2,1)S(1)}, u32[]{:S(2)}, u32[]{:S(2)}) collective-permute-start(bf16[192,128]{1,0:T(8,128)(2,1)S(1)} %pack.1), channel_id=1, source_target_pairs={{1,0},{0,1},{5,2},{4,3},{3,4},{2,5},{9,6},{8,7},{7,8},{6,9},{13,10... | collective-permute-start | bytes 147464 | tf_op jit(solution)/shard_map/ppermute | solution.py:239
  3.8 4.7 %collective-permute-start.3 = (bf16[192,128]{1,0:T(8,128)(2,1)S(1)}, bf16[192,128]{1,0:T(8,128)(2,1)S(1)}, u32[]{:S(2)}, u32[]{:S(2)}) collective-permute-start(bf16[192,128]{1,0:T(8,128)(2,1)S(1)} %pack.1), channel_id=1, source_target_pairs={{1,0},{0,1},{4,2},{5,3},{2,4},{3,5},{8,6},{9,7},{6,8},{7,9},{12,10... | collective-permute-start | bytes 147464 | tf_op jit(solution)/shard_map/ppermute | solution.py:239
  3.8 0.7 %copy-start.3 = (s32[4,2]{0,1:T(2,128)S(1)}, s32[4,2]{0,1:T(2,128)}, u32[]{:S(2)}) copy-start(s32[4,2]{0,1:T(2,128)} %param.11) | copy-start | bytes 100
  3.8 0.7 %copy-start.6 = (s32[4,1]{0,1:T(1,128)S(1)}, s32[4,1]{0,1:T(1,128)}, u32[]{:S(2)}) copy-start(s32[4,1]{0,1:T(1,128)} %param.12) | copy-start | bytes 52
  5.9 2.5 %collective-permute-start.1 = (bf16[128,128]{1,0:T(8,128)(2,1)S(1)}, bf16[128,128]{1,0:T(8,128)(2,1)S(1)}, u32[]{:S(2)}, u32[]{:S(2)}) collective-permute-start(bf16[128,128]{1,0:T(8,128)(2,1)S(1)} %get-tuple-element.20), channel_id=1, source_target_pairs={{2,0},{3,1},{0,2},{1,3},{6,4},{7,5},{4,6},{5,7},{10,8},{11,9},{8,1... | collective-permute-start | bytes 98312 | tf_op jit(solution)/shard_map/ppermute | solution.py:239
  7.6 0.9 %copy-start.2 = (s32[256,128]{1,0:T(8,128)S(1)}, s32[256,128]{1,0:T(8,128)}, u32[]{:S(2)}) copy-start(s32[256,128]{1,0:T(8,128)} %bound.1) | copy-start | bytes 393220

commit v11 on v10

--- a/solution.py
+++ b/solution.py
@@ -282,6 +282,7 @@
         col_kernels,
     )
     lead = call(lead_kernel, "lead", pltpu.VMEM((8, BLOCK), F32), [], 10**9, [])
+    *small, lead = lax.optimization_barrier((*small, lead))
     to_outer = call(
         pack_kernel,
         "pack",

time: 9.72 us -> 9.49 us (0.976)
  the two profiles are of different devices: /device:TPU:25 before, /device:TPU:3 now
where the time goes in v11:
time: 9.49 us; the launch traced here: 9.35 us
  starting transfers between devices  4.63 us (49%)
  Pallas kernels  3.46 us (36%)
  waiting for transfers between devices  1.09 us (11%)
  between operations  0.12 us (1%)
    ppermute x4, starting transfers between devices, moved(): return lax.ppermute(x, ('space', 'scen'), pairs)  4.63 us
    pallas_call x6, Pallas kernels, call(): pl.pallas_call(kernel, out_shape=outs, in_specs=specs, out_specs=jax.tree...  3.46 us
    ppermute x4, waiting for transfers between devices, moved(): return lax.ppermute(x, ('space', 'scen'), pairs)  1.09 us
  transfers between devices with their start and end apart: 4, of which 1 were waited for; matrix products, arithmetic and copies ran while one was open for 0% of the time, Pallas kernels for 20%

profile of v11, /device:TPU:3, one launch (start us, length us, event | category | flops | bytes accessed | tf_op | source)
XLA Modules:
  0.0 9.3 jit_solution(759000367505545075)
XLA Ops:
  0.0 1.2 %collective-permute-start = (bf16[256,128]{1,0:T(8,128)(2,1)}, bf16[256,128]{1,0:T(8,128)(2,1)S(1)}, u32[]{:S(2)}, u32[]{:S(2)}) collective-permute-start(bf16[256,128]{1,0:T(8,128)(2,1)} %dwell.3), channel_id=1, source_target_pairs={{1,0},{0,1},{3,2},{2,3},{5,4},{4,5},{7,6},{6,7},{9,8},{8,9},{11,10... | collective-permute-start | bytes 196616 | tf_op jit(solution)/shard_map/ppermute | solution.py:239
  1.2 0.0 copy-done.1
  1.2 0.0 copy-done
  1.3 0.0 copy-start.4
  1.3 0.0 copy-start.5
  1.3 0.0 copy-start.6
  1.3 0.0 copy-start.7
  1.3 2.5 %collective-permute-start.2 = (bf16[192,128]{1,0:T(8,128)(2,1)S(1)}, bf16[192,128]{1,0:T(8,128)(2,1)S(1)}, u32[]{:S(2)}, u32[]{:S(2)}) collective-permute-start(bf16[192,128]{1,0:T(8,128)(2,1)S(1)} %pack.1), channel_id=1, source_target_pairs={{1,0},{0,1},{5,2},{4,3},{3,4},{2,5},{9,6},{8,7},{7,8},{6,9},{13,10... | collective-permute-start | bytes 147464 | tf_op jit(solution)/shard_map/ppermute | solution.py:239
  3.8 0.8 %collective-permute-start.3 = (bf16[192,128]{1,0:T(8,128)(2,1)S(1)}, bf16[192,128]{1,0:T(8,128)(2,1)S(1)}, u32[]{:S(2)}, u32[]{:S(2)}) collective-permute-start(bf16[192,128]{1,0:T(8,128)(2,1)S(1)} %pack.1), channel_id=1, source_target_pairs={{1,0},{0,1},{4,2},{5,3},{2,4},{3,5},{8,6},{9,7},{6,8},{7,9},{12,10... | collective-permute-start | bytes 147464 | tf_op jit(solution)/shard_map/ppermute | solution.py:239
  4.7 0.0 copy-done.3
  4.7 0.0 copy-done.4
  4.7 0.0 copy-done.5
  4.7 0.0 copy-done.6
  4.7 1.0 %bands.1 = (bf16[4,128,256]{2,1,0:T(8,128)(2,1)S(1)}, bf16[4,128,256]{2,1,0:T(8,128)(2,1)S(1)}, bf16[256,512]{1,0:T(8,128)(2,1)S(1)}, bf16[256,512]{1,0:T(8,128)...) custom-call(s32[2,4]{1,0:T(2,128)S(1)} %bitcast.3, s32[1,4]{1,0:T(1,128)S(1)} %bitcast.4, ...), custom_call_target="tpu_custom_call" | custom-call | flops 100000000 | bytes 1000000 | tf_op jit(solution)/shard_map/bands/pallas_call | solution.py:256
  5.7 0.0 collective-permute-done.refs_1_
  5.7 0.5 %send.1 = (bf16[256,512]{1,0:T(8,128)(2,1)S(1)}, bf16[128,128]{1,0:T(8,128)(2,1)S(1)}) custom-call(f32[8,512]{1,0:T(8,128)S(1)} %get-tuple-element.24.scale, bf16[256,512]{1,0:T(8,128)(2,1)S(1)} %get-tuple-element.25.fold, bf16[256,512]{1,0:T(8,128)(2,1)S(1)} %get-tuple-element.26.own, bf16[2,128,1024]{2,1,0:T(8,128)(2,1)S(1)} %get-tuple-element.27.edge, ...), custom_call_target="tpu_custom_call" | custom-call | flops 100000000 | bytes 1000000 | tf_op jit(solution)/shard_map/send/pallas_call | solution.py:256
  6.2 0.1 collective-permute-start.1
  6.3 0.0 copy-start.2
  6.3 0.9 %own.1.partial = f32[256,128]{1,0:T(8,128)S(1)} custom-call(f32[8,512]{1,0:T(8,128)S(1)} %get-tuple-element.24.scale, bf16[4,128,256]{2,1,0:T(8,128)(2,1)S(1)} %get-tuple-element.28.fwd, bf16[4,128,256]{2,1,0:T(8,128)(2,1)S(1)} %get-tuple-element.29.adj, bf16[256,512]{1,0:T(8,128)(2,1)S(1)} %get-tuple-element.26.own, ...), custom_call_target="tpu_custom_call" | custom-call | flops 1000000000 | bytes 10000000 | tf_op jit(solution)/shard_map/own/pallas_call | solution.py:256
  7.2 0.0 collective-permute-done.2.refs_0_
  7.2 1.1 %collective-permute-done.3.refs_1_ = bf16[192,128]{1,0:T(8,128)(2,1)S(1)} collective-permute-done((bf16[192,128]{1,0:T(8,128)(2,1)S(1)}, bf16[192,128]{1,0:T(8,128)(2,1)S(1)}, u32[]{:S(2)}, u32[]{:S(2)}) %collective-permute-start.3) | collective-permute-done | bytes 49184 | tf_op jit(solution)/shard_map/ppermute | solution.py:239
  8.3 0.0 collective-permute-done.1.inner
  8.3 0.0 copy-done.2
  8.3 1.1 %finish.1 = bf16[256,128]{1,0:T(8,128)(2,1)} custom-call(f32[8,512]{1,0:T(8,128)S(1)} %get-tuple-element.24.scale, bf16[256,512]{1,0:T(8,128)(2,1)S(1)} %get-tuple-element.25.fold, bf16[256,512]{1,0:T(8,128)(2,1)S(1)} %get-tuple-element.26.own, bf16[2,128,1024]{2,1,0:T(8,128)(2,1)S(1)} %get-tuple-element.27.edge, f32[256,128]{1,0:T(8,128)S(1)} %own.1.partial, ...), custom_call_target="tpu_custom_call" | custom-call | flops 1000000 | bytes 10000 | tf_op jit(solution)/shard_map/finish/pallas_call | solution.py:256
  (6 shorter events, 0.0 us)
Async XLA Ops:
  0.0 1.2 %copy-start.1 = (bf16[256,128]{1,0:T(8,128)(2,1)S(1)}, bf16[256,128]{1,0:T(8,128)(2,1)}, u32[]{:S(2)}) copy-start(bf16[256,128]{1,0:T(8,128)(2,1)} %dwell.3) | copy-start | bytes 196612
  0.0 1.2 %copy-start = (bf16[256,256]{1,0:T(8,128)(2,1)S(1)}, bf16[256,256]{1,0:T(8,128)(2,1)}, u32[]{:S(2)}) copy-start(bf16[256,256]{1,0:T(8,128)(2,1)} %target.5) | copy-start | bytes 393220
  0.0 5.7 %collective-permute-start = (bf16[256,128]{1,0:T(8,128)(2,1)}, bf16[256,128]{1,0:T(8,128)(2,1)S(1)}, u32[]{:S(2)}, u32[]{:S(2)}) collective-permute-start(bf16[256,128]{1,0:T(8,128)(2,1)} %dwell.3), channel_id=1, source_target_pairs={{1,0},{0,1},{3,2},{2,3},{5,4},{4,5},{7,6},{6,7},{9,8},{8,9},{11,10... | collective-permute-start | bytes 196616 | tf_op jit(solution)/shard_map/ppermute | solution.py:239
  1.3 3.4 %copy-start.3 = (s32[4,2]{0,1:T(2,128)S(1)}, s32[4,2]{0,1:T(2,128)}, u32[]{:S(2)}) copy-start(s32[4,2]{0,1:T(2,128)} %param.11) | copy-start | bytes 100
  1.3 3.4 %copy-start.4 = (bf16[4,63]{1,0:T(4,128)(2,1)S(1)}, bf16[4,63]{1,0:T(4,128)(2,1)}, u32[]{:S(2)}) copy-start(bf16[4,63]{1,0:T(4,128)(2,1)} %row_taps) | copy-start | bytes 1516
  1.3 3.4 %copy-start.5 = (bf16[4,63]{1,0:T(4,128)(2,1)S(1)}, bf16[4,63]{1,0:T(4,128)(2,1)}, u32[]{:S(2)}) copy-start(bf16[4,63]{1,0:T(4,128)(2,1)} %col_taps) | copy-start | bytes 1516
  1.3 3.4 %copy-start.6 = (s32[4,1]{0,1:T(1,128)S(1)}, s32[4,1]{0,1:T(1,128)}, u32[]{:S(2)}) copy-start(s32[4,1]{0,1:T(1,128)} %param.12) | copy-start | bytes 52
  1.3 3.4 %copy-start.7 = (f32[4]{0:T(128)S(1)}, f32[4]{0:T(128)}, u32[]{:S(2)}) copy-start(f32[4]{0:T(128)} %param.13) | copy-start | bytes 52
  1.3 5.8 %collective-permute-start.2 = (bf16[192,128]{1,0:T(8,128)(2,1)S(1)}, bf16[192,128]{1,0:T(8,128)(2,1)S(1)}, u32[]{:S(2)}, u32[]{:S(2)}) collective-permute-start(bf16[192,128]{1,0:T(8,128)(2,1)S(1)} %pack.1), channel_id=1, source_target_pairs={{1,0},{0,1},{5,2},{4,3},{3,4},{2,5},{9,6},{8,7},{7,8},{6,9},{13,10... | collective-permute-start | bytes 147464 | tf_op jit(solution)/shard_map/ppermute | solution.py:239
  3.8 4.4 %collective-permute-start.3 = (bf16[192,128]{1,0:T(8,128)(2,1)S(1)}, bf16[192,128]{1,0:T(8,128)(2,1)S(1)}, u32[]{:S(2)}, u32[]{:S(2)}) collective-permute-start(bf16[192,128]{1,0:T(8,128)(2,1)S(1)} %pack.1), channel_id=1, source_target_pairs={{1,0},{0,1},{4,2},{5,3},{2,4},{3,5},{8,6},{9,7},{6,8},{7,9},{12,10... | collective-permute-start | bytes 147464 | tf_op jit(solution)/shard_map/ppermute | solution.py:239
  6.2 2.1 %collective-permute-start.1 = (bf16[128,128]{1,0:T(8,128)(2,1)S(1)}, bf16[128,128]{1,0:T(8,128)(2,1)S(1)}, u32[]{:S(2)}, u32[]{:S(2)}) collective-permute-start(bf16[128,128]{1,0:T(8,128)(2,1)S(1)} %get-tuple-element.31), channel_id=1, source_target_pairs={{2,0},{3,1},{0,2},{1,3},{6,4},{7,5},{4,6},{5,7},{10,8},{11,9},{8,1... | collective-permute-start | bytes 98312 | tf_op jit(solution)/shard_map/ppermute | solution.py:239
  6.3 2.0 %copy-start.2 = (s32[256,128]{1,0:T(8,128)S(1)}, s32[256,128]{1,0:T(8,128)}, u32[]{:S(2)}) copy-start(s32[256,128]{1,0:T(8,128)} %bound.1) | copy-start | bytes 393220

commit v12 on v11

--- a/solution.py
+++ b/solution.py
@@ -205,15 +205,33 @@
 
     @pl.when(jnp.logical_not(end))
     def _():
-        goal_rows = pl.ds(pl.multiple_of(odd * HALF, HALF), HALF)
-        target_halo[...] = jnp.zeros((BLOCK, width), BF16)
-        for b, lane in enumerate(lanes_of(blocks)):
-            dwell_halo[:, lane] = halos[b][:BLOCK, :]
-            target_halo[goal_rows, lane] = halos[b][BLOCK:, :]
-        clear_outside(blocks, dwell_halo)
-        clear_outside(blocks, target_halo)
-        from_dwell = (dot(dwell_halo[...], fold[...]) * scale[0:1, :]).astype(BF16)
-        from_target = (dot(target_halo[...], own[...]) * scale[1:2, :]).astype(BF16)
+        if blocks == 2:
+            flip = lax.axis_index("scen") == 1
+
+            def window(rows):
+                mine, other = halos[0][rows, :], halos[1][rows, :]
+                return jnp.where(
+                    flip,
+                    jnp.concatenate([other, mine], axis=1),
+                    jnp.concatenate([mine, other], axis=1),
+                )
+
+            dwell_rows, target_rows = window(slice(0, BLOCK)), window(slice(BLOCK, BLOCK + HALF))
+        else:
+            for b, lane in enumerate(lanes_of(blocks)):
+                dwell_halo[:, lane] = halos[b][:BLOCK, :]
+                target_halo[:, lane] = halos[b][BLOCK:, :]
+            clear_outside(blocks, dwell_halo)
+            clear_outside(blocks, target_halo)
+            dwell_rows, target_rows = dwell_halo[...], target_halo[...]
+        from_dwell = (dot(dwell_rows, fold[...]) * scale[0:1, :]).astype(BF16)
+        from_target = (dot(target_rows, own[...]) * scale[1:2, :]).astype(BF16)
+        none = jnp.zeros_like(from_target)
+        from_target = jnp.where(
+            odd == 1,
+            jnp.concatenate([none, from_target], axis=0),
+            jnp.concatenate([from_target, none], axis=0),
+        )
         terms = terms_of(edge[odd], from_dwell, from_target)
         step(1 - odd, inner[...].astype(F32))
         step(odd, terms)
@@ -351,7 +369,7 @@
         functools.partial(finish_kernel, blocks),
         "finish",
         jax.ShapeDtypeStruct(dwell_map.shape, BF16),
-        [pltpu.VMEM((BLOCK, width), BF16), pltpu.VMEM((BLOCK, width), BF16)],
+        [pltpu.VMEM((BLOCK, width), BF16), pltpu.VMEM((HALF, width), BF16)],
         10**6,
         [VMEM] * (7 + blocks),
         scale,

time: 9.49 us -> 9.47 us (level)
  no operation moved by 1% of the time
where the time goes in v12:
time: 9.47 us; the launch traced here: 9.33 us
  starting transfers between devices  4.63 us (49%)
  Pallas kernels  3.44 us (36%)
  waiting for transfers between devices  1.09 us (12%)
  between operations  0.12 us (1%)
    ppermute x4, starting transfers between devices, moved(): return lax.ppermute(x, ('space', 'scen'), pairs)  4.63 us
    pallas_call x6, Pallas kernels, call(): pl.pallas_call(kernel, out_shape=outs, in_specs=specs, out_specs=jax.tree...  3.44 us
    ppermute x4, waiting for transfers between devices, moved(): return lax.ppermute(x, ('space', 'scen'), pairs)  1.09 us
  transfers between devices with their start and end apart: 4, of which 1 were waited for; matrix products, arithmetic and copies ran while one was open for 0% of the time, Pallas kernels for 20%

profile of v12, /device:TPU:3, one launch (start us, length us, event | category | flops | bytes accessed | tf_op | source)
XLA Modules:
  0.0 9.3 jit_solution(18168556781759412249)
XLA Ops:
  0.0 1.2 %collective-permute-start = (bf16[256,128]{1,0:T(8,128)(2,1)}, bf16[256,128]{1,0:T(8,128)(2,1)S(1)}, u32[]{:S(2)}, u32[]{:S(2)}) collective-permute-start(bf16[256,128]{1,0:T(8,128)(2,1)} %dwell.3), channel_id=1, source_target_pairs={{1,0},{0,1},{3,2},{2,3},{5,4},{4,5},{7,6},{6,7},{9,8},{8,9},{11,10... | collective-permute-start | bytes 196616 | tf_op jit(solution)/shard_map/ppermute | solution.py:257
  1.2 0.0 copy-done.1
  1.2 0.0 copy-done
  1.3 0.0 copy-start.4
  1.3 0.0 copy-start.5
  1.3 0.0 copy-start.6
  1.3 0.0 copy-start.7
  1.3 2.5 %collective-permute-start.2 = (bf16[192,128]{1,0:T(8,128)(2,1)S(1)}, bf16[192,128]{1,0:T(8,128)(2,1)S(1)}, u32[]{:S(2)}, u32[]{:S(2)}) collective-permute-start(bf16[192,128]{1,0:T(8,128)(2,1)S(1)} %pack.1), channel_id=1, source_target_pairs={{1,0},{0,1},{5,2},{4,3},{3,4},{2,5},{9,6},{8,7},{7,8},{6,9},{13,10... | collective-permute-start | bytes 147464 | tf_op jit(solution)/shard_map/ppermute | solution.py:257
  3.8 0.8 %collective-permute-start.3 = (bf16[192,128]{1,0:T(8,128)(2,1)S(1)}, bf16[192,128]{1,0:T(8,128)(2,1)S(1)}, u32[]{:S(2)}, u32[]{:S(2)}) collective-permute-start(bf16[192,128]{1,0:T(8,128)(2,1)S(1)} %pack.1), channel_id=1, source_target_pairs={{1,0},{0,1},{4,2},{5,3},{2,4},{3,5},{8,6},{9,7},{6,8},{7,9},{12,10... | collective-permute-start | bytes 147464 | tf_op jit(solution)/shard_map/ppermute | solution.py:257
  4.7 0.0 copy-done.3
  4.7 0.0 copy-done.4
  4.7 0.0 copy-done.5
  4.7 0.0 copy-done.6
  4.7 1.0 %bands.1 = (bf16[4,128,256]{2,1,0:T(8,128)(2,1)S(1)}, bf16[4,128,256]{2,1,0:T(8,128)(2,1)S(1)}, bf16[256,512]{1,0:T(8,128)(2,1)S(1)}, bf16[256,512]{1,0:T(8,128)...) custom-call(s32[2,4]{1,0:T(2,128)S(1)} %bitcast.3, s32[1,4]{1,0:T(1,128)S(1)} %bitcast.4, ...), custom_call_target="tpu_custom_call" | custom-call | flops 100000000 | bytes 1000000 | tf_op jit(solution)/shard_map/bands/pallas_call | solution.py:274
  5.7 0.0 collective-permute-done.refs_1_
  5.7 0.5 %send.1 = (bf16[256,512]{1,0:T(8,128)(2,1)S(1)}, bf16[128,128]{1,0:T(8,128)(2,1)S(1)}) custom-call(f32[8,512]{1,0:T(8,128)S(1)} %get-tuple-element.24.scale, bf16[256,512]{1,0:T(8,128)(2,1)S(1)} %get-tuple-element.25.fold, bf16[256,512]{1,0:T(8,128)(2,1)S(1)} %get-tuple-element.26.own, bf16[2,128,1024]{2,1,0:T(8,128)(2,1)S(1)} %get-tuple-element.27.edge, ...), custom_call_target="tpu_custom_call" | custom-call | flops 100000000 | bytes 1000000 | tf_op jit(solution)/shard_map/send/pallas_call | solution.py:274
  6.2 0.1 collective-permute-start.1
  6.3 0.0 copy-start.2
  6.3 0.9 %own.1.partial = f32[256,128]{1,0:T(8,128)S(1)} custom-call(f32[8,512]{1,0:T(8,128)S(1)} %get-tuple-element.24.scale, bf16[4,128,256]{2,1,0:T(8,128)(2,1)S(1)} %get-tuple-element.28.fwd, bf16[4,128,256]{2,1,0:T(8,128)(2,1)S(1)} %get-tuple-element.29.adj, bf16[256,512]{1,0:T(8,128)(2,1)S(1)} %get-tuple-element.26.own, ...), custom_call_target="tpu_custom_call" | custom-call | flops 1000000000 | bytes 10000000 | tf_op jit(solution)/shard_map/own/pallas_call | solution.py:274
  7.2 0.0 collective-permute-done.2.refs_0_
  7.2 1.1 %collective-permute-done.3.refs_1_ = bf16[192,128]{1,0:T(8,128)(2,1)S(1)} collective-permute-done((bf16[192,128]{1,0:T(8,128)(2,1)S(1)}, bf16[192,128]{1,0:T(8,128)(2,1)S(1)}, u32[]{:S(2)}, u32[]{:S(2)}) %collective-permute-start.3) | collective-permute-done | bytes 49184 | tf_op jit(solution)/shard_map/ppermute | solution.py:257
  8.3 0.0 collective-permute-done.1.inner
  8.3 0.0 copy-done.2
  8.3 1.1 %finish.1 = bf16[256,128]{1,0:T(8,128)(2,1)} custom-call(f32[8,512]{1,0:T(8,128)S(1)} %get-tuple-element.24.scale, bf16[256,512]{1,0:T(8,128)(2,1)S(1)} %get-tuple-element.25.fold, bf16[256,512]{1,0:T(8,128)(2,1)S(1)} %get-tuple-element.26.own, bf16[2,128,1024]{2,1,0:T(8,128)(2,1)S(1)} %get-tuple-element.27.edge, f32[256,128]{1,0:T(8,128)S(1)} %own.1.partial, ...), custom_call_target="tpu_custom_call" | custom-call | flops 1000000 | bytes 10000 | tf_op jit(solution)/shard_map/finish/pallas_call | solution.py:274
  (6 shorter events, 0.0 us)
Async XLA Ops:
  0.0 1.2 %copy-start.1 = (bf16[256,128]{1,0:T(8,128)(2,1)S(1)}, bf16[256,128]{1,0:T(8,128)(2,1)}, u32[]{:S(2)}) copy-start(bf16[256,128]{1,0:T(8,128)(2,1)} %dwell.3) | copy-start | bytes 196612
  0.0 1.2 %copy-start = (bf16[256,256]{1,0:T(8,128)(2,1)S(1)}, bf16[256,256]{1,0:T(8,128)(2,1)}, u32[]{:S(2)}) copy-start(bf16[256,256]{1,0:T(8,128)(2,1)} %target.5) | copy-start | bytes 393220
  0.0 5.7 %collective-permute-start = (bf16[256,128]{1,0:T(8,128)(2,1)}, bf16[256,128]{1,0:T(8,128)(2,1)S(1)}, u32[]{:S(2)}, u32[]{:S(2)}) collective-permute-start(bf16[256,128]{1,0:T(8,128)(2,1)} %dwell.3), channel_id=1, source_target_pairs={{1,0},{0,1},{3,2},{2,3},{5,4},{4,5},{7,6},{6,7},{9,8},{8,9},{11,10... | collective-permute-start | bytes 196616 | tf_op jit(solution)/shard_map/ppermute | solution.py:257
  1.3 3.4 %copy-start.3 = (s32[4,2]{0,1:T(2,128)S(1)}, s32[4,2]{0,1:T(2,128)}, u32[]{:S(2)}) copy-start(s32[4,2]{0,1:T(2,128)} %param.11) | copy-start | bytes 100
  1.3 3.4 %copy-start.4 = (bf16[4,63]{1,0:T(4,128)(2,1)S(1)}, bf16[4,63]{1,0:T(4,128)(2,1)}, u32[]{:S(2)}) copy-start(bf16[4,63]{1,0:T(4,128)(2,1)} %row_taps) | copy-start | bytes 1516
  1.3 3.4 %copy-start.5 = (bf16[4,63]{1,0:T(4,128)(2,1)S(1)}, bf16[4,63]{1,0:T(4,128)(2,1)}, u32[]{:S(2)}) copy-start(bf16[4,63]{1,0:T(4,128)(2,1)} %col_taps) | copy-start | bytes 1516
  1.3 3.4 %copy-start.6 = (s32[4,1]{0,1:T(1,128)S(1)}, s32[4,1]{0,1:T(1,128)}, u32[]{:S(2)}) copy-start(s32[4,1]{0,1:T(1,128)} %param.12) | copy-start | bytes 52
  1.3 3.4 %copy-start.7 = (f32[4]{0:T(128)S(1)}, f32[4]{0:T(128)}, u32[]{:S(2)}) copy-start(f32[4]{0:T(128)} %param.13) | copy-start | bytes 52
  1.3 5.8 %collective-permute-start.2 = (bf16[192,128]{1,0:T(8,128)(2,1)S(1)}, bf16[192,128]{1,0:T(8,128)(2,1)S(1)}, u32[]{:S(2)}, u32[]{:S(2)}) collective-permute-start(bf16[192,128]{1,0:T(8,128)(2,1)S(1)} %pack.1), channel_id=1, source_target_pairs={{1,0},{0,1},{5,2},{4,3},{3,4},{2,5},{9,6},{8,7},{7,8},{6,9},{13,10... | collective-permute-start | bytes 147464 | tf_op jit(solution)/shard_map/ppermute | solution.py:257
  3.8 4.4 %collective-permute-start.3 = (bf16[192,128]{1,0:T(8,128)(2,1)S(1)}, bf16[192,128]{1,0:T(8,128)(2,1)S(1)}, u32[]{:S(2)}, u32[]{:S(2)}) collective-permute-start(bf16[192,128]{1,0:T(8,128)(2,1)S(1)} %pack.1), channel_id=1, source_target_pairs={{1,0},{0,1},{4,2},{5,3},{2,4},{3,5},{8,6},{9,7},{6,8},{7,9},{12,10... | collective-permute-start | bytes 147464 | tf_op jit(solution)/shard_map/ppermute | solution.py:257
  6.2 2.1 %collective-permute-start.1 = (bf16[128,128]{1,0:T(8,128)(2,1)S(1)}, bf16[128,128]{1,0:T(8,128)(2,1)S(1)}, u32[]{:S(2)}, u32[]{:S(2)}) collective-permute-start(bf16[128,128]{1,0:T(8,128)(2,1)S(1)} %get-tuple-element.31), channel_id=1, source_target_pairs={{2,0},{3,1},{0,2},{1,3},{6,4},{7,5},{4,6},{5,7},{10,8},{11,9},{8,1... | collective-permute-start | bytes 98312 | tf_op jit(solution)/shard_map/ppermute | solution.py:257
  6.3 2.0 %copy-start.2 = (s32[256,128]{1,0:T(8,128)S(1)}, s32[256,128]{1,0:T(8,128)}, u32[]{:S(2)}) copy-start(s32[256,128]{1,0:T(8,128)} %bound.1) | copy-start | bytes 393220
